TPU v7x, 1024 devices: a whole 8x8x8 slice. The times are simulated.
1024 devices in a mesh: blk: 16 (over z, y_hi), group: 64 (over y_lo, x, core).
Axes of the slice: x: 8, y: 8 (y_hi: 2, y_lo: 4; y = y_hi * 4 + y_lo), z: 8, core: 2. Of those that a mesh axis runs over, the one named last changes fastest.
Arguments:
- images: bfloat16 [131072, 1152], P(('blk', 'group')), may hold values from -6 to 6
- texts: bfloat16 [131072, 1152], P(('blk', 'group')), may hold values from -6 to 6
- labels: int32 [16, 8192], P(None, 'group'), may hold values from 0 to 511
- weights: float32 [131072], P(('blk', 'group')), may hold values from 0.3 to 20
- log_temp: float32 [1], replicated, may hold values from 1.6 to 3
- bias: float32 [1], replicated, may hold values from -4 to -1
Outputs:
- image_grad: bfloat16 [131072, 1152], P(('blk', 'group'))
- text_grad: bfloat16 [131072, 1152], P(('blk', 'group'))
- stats: float32 [3], replicated
All inputs are finite; a program needn't handle non-finite values.
Results may differ from a plain program's by a relative error of at most 0.0061.
Values may be sent and summed in bfloat16 or wider, within the bound.
No kernel may reach another device: no remote copies, remote signals or barrier semaphores. Data moves between devices by JAX's collectives and lax.ppermute only.
A program may use at most 32 MiB of HBM per device.

v0:
```python
import jax
import jax.numpy as jnp
from jax import lax
from jax.sharding import PartitionSpec as P


def passed_along(value, axis, steps):
    count = lax.axis_size(axis)
    pairs = [(source, (source + steps) % count) for source in range(count)]
    return lax.ppermute(value, axis, pairs)


def normalize(raw):
    values = raw.astype(jnp.float32)
    scale = lax.rsqrt(jnp.sum(values * values, axis=-1, keepdims=True) + 1e-06)
    return (values * scale, scale)


def norm_back(unit, scale, upstream):
    return (upstream - unit * jnp.sum(unit * upstream, axis=-1, keepdims=True)) * scale


def score_side(image_unit, text_block, image_label, text_label, image_weight, temper, offset_bias):
    scores = lax.dot_general(
        image_unit, text_block, (((1,), (1,)), ((), ())), preferred_element_type=jnp.float32
    )
    scaled = temper * scores
    logits = scaled + offset_bias
    target = (image_label[:, None] == text_label[None, :]).astype(jnp.float32)
    signed = 2.0 * target - 1.0
    grads = image_weight[:, None] * (jax.nn.sigmoid(logits) - target)
    losses = image_weight[:, None] * jax.nn.softplus(-signed * logits)
    rounded = grads.astype(jnp.bfloat16)
    image_part = temper * jnp.dot(rounded, text_block, preferred_element_type=jnp.float32)
    part_sums = jnp.stack([jnp.sum(losses), jnp.sum(grads * scaled), jnp.sum(grads)])
    return (image_part, rounded, part_sums)


def text_side(rounded, image_block, temper):
    return temper * lax.dot_general(
        rounded, image_block, (((0,), (0,)), ((), ())), preferred_element_type=jnp.float32
    )


def per_device(images, texts, labels, weights, log_temp, bias):
    cycle = lax.axis_size("blk")
    groups = lax.axis_size("group")
    place = lax.axis_index("blk")
    span = min(8, cycle)
    half = span // 2
    pair_rows = images.shape[0]
    image_norm, image_scale = normalize(images)
    text_norm, text_scale = normalize(texts)
    image_unit = image_norm.astype(jnp.bfloat16)
    text_unit = text_norm.astype(jnp.bfloat16)
    temper = jnp.exp(log_temp[0])
    offset_bias = bias[0]

    def label_of(offset):
        return lax.dynamic_index_in_dim(labels, (place + offset) % cycle, 0, keepdims=False)

    image_label = label_of(0)
    current = passed_along(text_unit, "blk", half - 1)
    carried = None
    image_total = None
    sums = None
    for step in range(span):
        offset = step - (half - 1)
        if step > 0:
            current = passed_along(current, "blk", -1)
            carried = passed_along(carried, "blk", -1)
        image_part, rounded, part_sums = score_side(
            image_unit, current, image_label, label_of(offset), weights, temper, offset_bias
        )
        visit_image_part = image_part
        visit_part_sums = part_sums
        image_part = visit_image_part
        text_part = text_side(rounded, image_unit, temper)
        part_sums = visit_part_sums
        if step == 0:
            carried, image_total, sums = (text_part, image_part, part_sums)
        else:
            carried = carried + text_part
            image_total = image_total + image_part
            sums = sums + part_sums
    text_total = passed_along(carried, "blk", half)
    summed = lax.psum(sums, ("blk", "group"))
    count = float(cycle * groups * pair_rows) * float(pair_rows) * float(span)
    image_grad = norm_back(image_norm, image_scale, image_total).astype(jnp.bfloat16)
    text_grad = norm_back(text_norm, text_scale, text_total).astype(jnp.bfloat16)
    return (image_grad, text_grad, summed / count)


def solution(mesh):
    in_specs = (
        P(("blk", "group"), None),
        P(("blk", "group"), None),
        P(None, "group"),
        P(("blk", "group")),
        P(),
        P(),
    )
    out_specs = (P(("blk", "group"), None), P(("blk", "group"), None), P())
    return jax.shard_map(
        per_device, mesh=mesh, in_specs=in_specs, out_specs=out_specs, check_vma=False
    )
```

profile of v0, /device:TPU:1, one launch (start us, length us, event | category | flops | bytes accessed | tf_op | source)
XLA Modules:
  0.0 523.4 jit_solution(6687307934061010383)
XLA Ops:
  2.4 11.4 %collective-permute-start = (bf16[128,1152]{1,0:T(8,128)(2,1)S(1)}, bf16[128,1152]{1,0:T(8,128)(2,1)S(1)}, u32[]{:S(2)}, u32[]{:S(2)}) collective-permute-start(bf16[128,1152]{1,0:T(8,128)(2,1)S(1)} %fusion.4), channel_id=1, source_target_pairs={{0,192},{64,256},{128,320},{192,384},{256,448},{320,512},{384,576}... | collective-permute-start | bytes 884744 | tf_op jit(solution)/shard_map/ppermute | solution.py:10
  13.9 19.9 %collective-permute-done = bf16[128,1152]{1,0:T(8,128)(2,1)S(1)} collective-permute-done((bf16[128,1152]{1,0:T(8,128)(2,1)S(1)}, bf16[128,1152]{1,0:T(8,128)(2,1)S(1)}, u32[]{:S(2)}, u32[]{:S(2)}) %collective-permute-start) | collective-permute-done | bytes 294944 | tf_op jit(solution)/shard_map/ppermute | solution.py:10
  33.8 6.8 %collective-permute-start.1 = (bf16[128,1152]{1,0:T(8,128)(2,1)S(1)}, bf16[128,1152]{1,0:T(8,128)(2,1)S(1)}, u32[]{:S(2)}, u32[]{:S(2)}) collective-permute-start(bf16[128,1152]{1,0:T(8,128)(2,1)S(1)} %collective-permute-done), channel_id=1, source_target_pairs={{0,960},{64,0},{128,64},{192,128},{256,192},{320,256},{384,320},{4... | collective-permute-start | bytes 884744 | tf_op jit(solution)/shard_map/ppermute | solution.py:10
  45.2 9.6 %collective-permute-start.2 = (bf16[128,1152]{1,0:T(8,128)(2,1)S(1)}, bf16[128,1152]{1,0:T(8,128)(2,1)S(1)}, u32[]{:S(2)}, u32[]{:S(2)}) collective-permute-start(bf16[128,1152]{1,0:T(8,128)(2,1)S(1)} %collective-permute-done.1), channel_id=1, source_target_pairs={{0,960},{64,0},{128,64},{192,128},{256,192},{320,256},{384,320},{4... | collective-permute-start | bytes 884744 | tf_op jit(solution)/shard_map/ppermute | solution.py:10
  54.7 10.3 %collective-permute-done.2 = bf16[128,1152]{1,0:T(8,128)(2,1)S(1)} collective-permute-done((bf16[128,1152]{1,0:T(8,128)(2,1)S(1)}, bf16[128,1152]{1,0:T(8,128)(2,1)S(1)}, u32[]{:S(2)}, u32[]{:S(2)}) %collective-permute-start.2) | collective-permute-done | bytes 294944 | tf_op jit(solution)/shard_map/ppermute | solution.py:10
  71.5 7.4 %collective-permute-done.3 = bf16[128,1152]{1,0:T(8,128)(2,1)S(1)} collective-permute-done((bf16[128,1152]{1,0:T(8,128)(2,1)S(1)}, bf16[128,1152]{1,0:T(8,128)(2,1)S(1)}, u32[]{:S(2)}, u32[]{:S(2)}) %collective-permute-start.3) | collective-permute-done | bytes 294944 | tf_op jit(solution)/shard_map/ppermute | solution.py:10
  91.5 15.4 %collective-permute-start.5 = (bf16[128,1152]{1,0:T(8,128)(2,1)S(1)}, bf16[128,1152]{1,0:T(8,128)(2,1)S(1)}, u32[]{:S(2)}, u32[]{:S(2)}) collective-permute-start(bf16[128,1152]{1,0:T(8,128)(2,1)S(1)} %collective-permute-done.4), channel_id=1, source_target_pairs={{0,960},{64,0},{128,64},{192,128},{256,192},{320,256},{384,320},{4... | collective-permute-start | bytes 884744 | tf_op jit(solution)/shard_map/ppermute | solution.py:10
  111.5 14.9 %collective-permute-start.6 = (bf16[128,1152]{1,0:T(8,128)(2,1)S(1)}, bf16[128,1152]{1,0:T(8,128)(2,1)S(1)}, u32[]{:S(2)}, u32[]{:S(2)}) collective-permute-start(bf16[128,1152]{1,0:T(8,128)(2,1)S(1)} %collective-permute-done.5), channel_id=1, source_target_pairs={{0,960},{64,0},{128,64},{192,128},{256,192},{320,256},{384,320},{4... | collective-permute-start | bytes 884744 | tf_op jit(solution)/shard_map/ppermute | solution.py:10
  127.0 11.0 %collective-permute-done.6 = bf16[128,1152]{1,0:T(8,128)(2,1)S(1)} collective-permute-done((bf16[128,1152]{1,0:T(8,128)(2,1)S(1)}, bf16[128,1152]{1,0:T(8,128)(2,1)S(1)}, u32[]{:S(2)}, u32[]{:S(2)}) %collective-permute-start.6) | collective-permute-done | bytes 294944 | tf_op jit(solution)/shard_map/ppermute | solution.py:10
  138.0 10.1 %collective-permute-start.7 = (bf16[128,1152]{1,0:T(8,128)(2,1)S(1)}, bf16[128,1152]{1,0:T(8,128)(2,1)S(1)}, u32[]{:S(2)}, u32[]{:S(2)}) collective-permute-start(bf16[128,1152]{1,0:T(8,128)(2,1)S(1)} %collective-permute-done.6), channel_id=1, source_target_pairs={{0,960},{64,0},{128,64},{192,128},{256,192},{320,256},{384,320},{4... | collective-permute-start | bytes 884744 | tf_op jit(solution)/shard_map/ppermute | solution.py:10
  148.7 10.6 %collective-permute-done.7 = bf16[128,1152]{1,0:T(8,128)(2,1)S(1)} collective-permute-done((bf16[128,1152]{1,0:T(8,128)(2,1)S(1)}, bf16[128,1152]{1,0:T(8,128)(2,1)S(1)}, u32[]{:S(2)}, u32[]{:S(2)}) %collective-permute-start.7) | collective-permute-done | bytes 294944 | tf_op jit(solution)/shard_map/ppermute | solution.py:10
  162.2 10.1 %collective-permute-start.8 = (f32[128,1152]{1,0:T(8,128)S(1)}, f32[128,1152]{1,0:T(8,128)S(1)}, u32[]{:S(2)}, u32[]{:S(2)}) collective-permute-start(f32[128,1152]{1,0:T(8,128)S(1)} %convolution_multiply_fusion.7), channel_id=1, source_target_pairs={{0,960},{64,0},{128,64},{192,128},{256,192},{320,256},{384,320},{4... | collective-permute-start | bytes 1769480 | tf_op jit(solution)/shard_map/ppermute | solution.py:10
  172.3 15.6 %collective-permute-done.8 = f32[128,1152]{1,0:T(8,128)S(1)} collective-permute-done((f32[128,1152]{1,0:T(8,128)S(1)}, f32[128,1152]{1,0:T(8,128)S(1)}, u32[]{:S(2)}, u32[]{:S(2)}) %collective-permute-start.8) | collective-permute-done | bytes 589856 | tf_op jit(solution)/shard_map/ppermute | solution.py:10
  188.3 6.7 %collective-permute-start.9 = (f32[128,1152]{1,0:T(8,128)S(1)}, f32[128,1152]{1,0:T(8,128)S(1)}, u32[]{:S(2)}, u32[]{:S(2)}) collective-permute-start(f32[128,1152]{1,0:T(8,128)S(1)} %fusion), channel_id=1, source_target_pairs={{0,960},{64,0},{128,64},{192,128},{256,192},{320,256},{384,320},{4... | collective-permute-start | bytes 1769480 | tf_op jit(solution)/shard_map/ppermute | solution.py:10
  195.3 21.3 %collective-permute-done.9 = f32[128,1152]{1,0:T(8,128)S(1)} collective-permute-done((f32[128,1152]{1,0:T(8,128)S(1)}, f32[128,1152]{1,0:T(8,128)S(1)}, u32[]{:S(2)}, u32[]{:S(2)}) %collective-permute-start.9) | collective-permute-done | bytes 589856 | tf_op jit(solution)/shard_map/ppermute | solution.py:10
  216.7 7.4 %collective-permute-start.10 = (f32[128,1152]{1,0:T(8,128)S(1)}, f32[128,1152]{1,0:T(8,128)S(1)}, u32[]{:S(2)}, u32[]{:S(2)}) collective-permute-start(f32[128,1152]{1,0:T(8,128)S(1)} %add.295), channel_id=1, source_target_pairs={{0,960},{64,0},{128,64},{192,128},{256,192},{320,256},{384,320},{4... | collective-permute-start | bytes 1769480 | tf_op jit(solution)/shard_map/ppermute | solution.py:10
  224.9 20.2 %collective-permute-done.10 = f32[128,1152]{1,0:T(8,128)S(1)} collective-permute-done((f32[128,1152]{1,0:T(8,128)S(1)}, f32[128,1152]{1,0:T(8,128)S(1)}, u32[]{:S(2)}, u32[]{:S(2)}) %collective-permute-start.10) | collective-permute-done | bytes 589856 | tf_op jit(solution)/shard_map/ppermute | solution.py:10
  252.2 19.9 %collective-permute-done.11 = f32[128,1152]{1,0:T(8,128)S(1)} collective-permute-done((f32[128,1152]{1,0:T(8,128)S(1)}, f32[128,1152]{1,0:T(8,128)S(1)}, u32[]{:S(2)}, u32[]{:S(2)}) %collective-permute-start.11) | collective-permute-done | bytes 589856 | tf_op jit(solution)/shard_map/ppermute | solution.py:10
  272.2 7.3 %collective-permute-start.12 = (f32[128,1152]{1,0:T(8,128)S(1)}, f32[128,1152]{1,0:T(8,128)S(1)}, u32[]{:S(2)}, u32[]{:S(2)}) collective-permute-start(f32[128,1152]{1,0:T(8,128)S(1)} %add.297), channel_id=1, source_target_pairs={{0,960},{64,0},{128,64},{192,128},{256,192},{320,256},{384,320},{4... | collective-permute-start | bytes 1769480 | tf_op jit(solution)/shard_map/ppermute | solution.py:10
  280.4 20.0 %collective-permute-done.12 = f32[128,1152]{1,0:T(8,128)S(1)} collective-permute-done((f32[128,1152]{1,0:T(8,128)S(1)}, f32[128,1152]{1,0:T(8,128)S(1)}, u32[]{:S(2)}, u32[]{:S(2)}) %collective-permute-start.12) | collective-permute-done | bytes 589856 | tf_op jit(solution)/shard_map/ppermute | solution.py:10
  306.6 15.6 %maximum_add_fusion.2 = f32[3]{0:T(128)} fusion(f32[1]{0:T(128)} %bitcast.33, f32[1]{0:T(128)} %bitcast.32, f32[1]{0:T(128)} %bitcast.31, f32[1]{0:T(128)} %bitcast.30, f32[1]{0:T(128)} %bitcast.29, f32[1]{0:T(128)} %bitcast.28, f32[1]{0:T(128)} %bitcast.27, f32[1]{0:T(128)} %bitcast.26, f32[1]{0:T(128)} %bitcast.25, f32[1]{0:T(128)} %bitcast.24, ...), kind=kLoop, calls=%fused_computation.172 | loop fusion | flops 69 | bytes 108 | tf_op jit(solution)/shard_map/add | solution.py:85
  327.6 7.3 %collective-permute-start.14 = (f32[128,1152]{1,0:T(8,128)S(1)}, f32[128,1152]{1,0:T(8,128)S(1)}, u32[]{:S(2)}, u32[]{:S(2)}) collective-permute-start(f32[128,1152]{1,0:T(8,128)S(1)} %add.299), channel_id=1, source_target_pairs={{0,960},{64,0},{128,64},{192,128},{256,192},{320,256},{384,320},{4... | collective-permute-start | bytes 1769480 | tf_op jit(solution)/shard_map/ppermute | solution.py:10
  335.3 155.5 %psum.7 = f32[3]{0:T(128)} all-reduce(f32[3]{0:T(128)} %maximum_add_fusion.2), channel_id=1, replica_groups=mesh['blk'=16,'group'=64] {'blk','group'}, use_global_device_ids=true, to_apply=%region_28.29 | all-reduce | flops 3 | bytes 24 | tf_op jit(solution)/shard_map/psum | solution.py:87
  498.8 23.5 %collective-permute-done.15 = f32[128,1152]{1,0:T(8,128)S(1)} collective-permute-done((f32[128,1152]{1,0:T(8,128)S(1)}, f32[128,1152]{1,0:T(8,128)S(1)}, u32[]{:S(2)}, u32[]{:S(2)}) %collective-permute-start.15) | collective-permute-done | bytes 589856 | tf_op jit(solution)/shard_map/ppermute | solution.py:10
  (74 shorter events, 63.0 us)
Async XLA Ops:
  0.6 1.2 copy-start.1
  1.8 69.5 %copy-start = (bf16[128,1152]{1,0:T(8,128)(2,1)S(1)}, bf16[128,1152]{1,0:T(8,128)(2,1)}, u32[]{:S(2)}) copy-start(bf16[128,1152]{1,0:T(8,128)(2,1)} %param.6) | copy-start | bytes 884740
  2.4 31.4 %collective-permute-start = (bf16[128,1152]{1,0:T(8,128)(2,1)S(1)}, bf16[128,1152]{1,0:T(8,128)(2,1)S(1)}, u32[]{:S(2)}, u32[]{:S(2)}) collective-permute-start(bf16[128,1152]{1,0:T(8,128)(2,1)S(1)} %fusion.4), channel_id=1, source_target_pairs={{0,192},{64,256},{128,320},{192,384},{256,448},{320,512},{384,576}... | collective-permute-start | bytes 884744 | tf_op jit(solution)/shard_map/ppermute | solution.py:10
  33.8 11.4 %collective-permute-start.1 = (bf16[128,1152]{1,0:T(8,128)(2,1)S(1)}, bf16[128,1152]{1,0:T(8,128)(2,1)S(1)}, u32[]{:S(2)}, u32[]{:S(2)}) collective-permute-start(bf16[128,1152]{1,0:T(8,128)(2,1)S(1)} %collective-permute-done), channel_id=1, source_target_pairs={{0,960},{64,0},{128,64},{192,128},{256,192},{320,256},{384,320},{4... | collective-permute-start | bytes 884744 | tf_op jit(solution)/shard_map/ppermute | solution.py:10
  45.2 19.9 %collective-permute-start.2 = (bf16[128,1152]{1,0:T(8,128)(2,1)S(1)}, bf16[128,1152]{1,0:T(8,128)(2,1)S(1)}, u32[]{:S(2)}, u32[]{:S(2)}) collective-permute-start(bf16[128,1152]{1,0:T(8,128)(2,1)S(1)} %collective-permute-done.1), channel_id=1, source_target_pairs={{0,960},{64,0},{128,64},{192,128},{256,192},{320,256},{384,320},{4... | collective-permute-start | bytes 884744 | tf_op jit(solution)/shard_map/ppermute | solution.py:10
  65.0 13.9 %collective-permute-start.3 = (bf16[128,1152]{1,0:T(8,128)(2,1)S(1)}, bf16[128,1152]{1,0:T(8,128)(2,1)S(1)}, u32[]{:S(2)}, u32[]{:S(2)}) collective-permute-start(bf16[128,1152]{1,0:T(8,128)(2,1)S(1)} %collective-permute-done.2), channel_id=1, source_target_pairs={{0,960},{64,0},{128,64},{192,128},{256,192},{320,256},{384,320},{4... | collective-permute-start | bytes 884744 | tf_op jit(solution)/shard_map/ppermute | solution.py:10
  71.3 13.9 %copy-start.10 = (s32[16,128]{1,0:T(8,128)S(1)}, s32[16,128]{1,0:T(8,128)}, u32[]{:S(2)}) copy-start(s32[16,128]{1,0:T(8,128)} %param.8) | copy-start | bytes 24580
  78.9 12.6 %collective-permute-start.4 = (bf16[128,1152]{1,0:T(8,128)(2,1)S(1)}, bf16[128,1152]{1,0:T(8,128)(2,1)S(1)}, u32[]{:S(2)}, u32[]{:S(2)}) collective-permute-start(bf16[128,1152]{1,0:T(8,128)(2,1)S(1)} %collective-permute-done.3), channel_id=1, source_target_pairs={{0,960},{64,0},{128,64},{192,128},{256,192},{320,256},{384,320},{4... | collective-permute-start | bytes 884744 | tf_op jit(solution)/shard_map/ppermute | solution.py:10
  85.3 166.2 %copy-start.6 = (s32[128]{0:T(128)}, s32[128]{0:T(128)S(1)}, u32[]{:S(2)}) copy-start(s32[128]{0:T(128)S(1)} %get-tuple-element.55) | copy-start | bytes 1540
  91.5 20.1 %collective-permute-start.5 = (bf16[128,1152]{1,0:T(8,128)(2,1)S(1)}, bf16[128,1152]{1,0:T(8,128)(2,1)S(1)}, u32[]{:S(2)}, u32[]{:S(2)}) collective-permute-start(bf16[128,1152]{1,0:T(8,128)(2,1)S(1)} %collective-permute-done.4), channel_id=1, source_target_pairs={{0,960},{64,0},{128,64},{192,128},{256,192},{320,256},{384,320},{4... | collective-permute-start | bytes 884744 | tf_op jit(solution)/shard_map/ppermute | solution.py:10
  111.5 26.4 %collective-permute-start.6 = (bf16[128,1152]{1,0:T(8,128)(2,1)S(1)}, bf16[128,1152]{1,0:T(8,128)(2,1)S(1)}, u32[]{:S(2)}, u32[]{:S(2)}) collective-permute-start(bf16[128,1152]{1,0:T(8,128)(2,1)S(1)} %collective-permute-done.5), channel_id=1, source_target_pairs={{0,960},{64,0},{128,64},{192,128},{256,192},{320,256},{384,320},{4... | collective-permute-start | bytes 884744 | tf_op jit(solution)/shard_map/ppermute | solution.py:10
  138.0 21.3 %collective-permute-start.7 = (bf16[128,1152]{1,0:T(8,128)(2,1)S(1)}, bf16[128,1152]{1,0:T(8,128)(2,1)S(1)}, u32[]{:S(2)}, u32[]{:S(2)}) collective-permute-start(bf16[128,1152]{1,0:T(8,128)(2,1)S(1)} %collective-permute-done.6), channel_id=1, source_target_pairs={{0,960},{64,0},{128,64},{192,128},{256,192},{320,256},{384,320},{4... | collective-permute-start | bytes 884744 | tf_op jit(solution)/shard_map/ppermute | solution.py:10
  148.7 102.9 %copy-start.4 = (f32[128,128]{1,0:T(8,128)}, f32[128,128]{1,0:T(8,128)S(1)}, u32[]{:S(2)}) copy-start(f32[128,128]{1,0:T(8,128)S(1)} %convolution_multiply_fusion.9) | copy-start | bytes 196612
  159.6 175.3 %copy-start.2 = (f32[128,128]{1,0:T(8,128)}, f32[128,128]{1,0:T(8,128)S(1)}, u32[]{:S(2)}) copy-start(f32[128,128]{1,0:T(8,128)S(1)} %convolution_multiply_fusion.8) | copy-start | bytes 196612
  162.2 25.7 %collective-permute-start.8 = (f32[128,1152]{1,0:T(8,128)S(1)}, f32[128,1152]{1,0:T(8,128)S(1)}, u32[]{:S(2)}, u32[]{:S(2)}) collective-permute-start(f32[128,1152]{1,0:T(8,128)S(1)} %convolution_multiply_fusion.7), channel_id=1, source_target_pairs={{0,960},{64,0},{128,64},{192,128},{256,192},{320,256},{384,320},{4... | collective-permute-start | bytes 1769480 | tf_op jit(solution)/shard_map/ppermute | solution.py:10
  188.3 28.4 %collective-permute-start.9 = (f32[128,1152]{1,0:T(8,128)S(1)}, f32[128,1152]{1,0:T(8,128)S(1)}, u32[]{:S(2)}, u32[]{:S(2)}) collective-permute-start(f32[128,1152]{1,0:T(8,128)S(1)} %fusion), channel_id=1, source_target_pairs={{0,960},{64,0},{128,64},{192,128},{256,192},{320,256},{384,320},{4... | collective-permute-start | bytes 1769480 | tf_op jit(solution)/shard_map/ppermute | solution.py:10
  216.7 28.3 %collective-permute-start.10 = (f32[128,1152]{1,0:T(8,128)S(1)}, f32[128,1152]{1,0:T(8,128)S(1)}, u32[]{:S(2)}, u32[]{:S(2)}) collective-permute-start(f32[128,1152]{1,0:T(8,128)S(1)} %add.295), channel_id=1, source_target_pairs={{0,960},{64,0},{128,64},{192,128},{256,192},{320,256},{384,320},{4... | collective-permute-start | bytes 1769480 | tf_op jit(solution)/shard_map/ppermute | solution.py:10
  245.1 27.0 %collective-permute-start.11 = (f32[128,1152]{1,0:T(8,128)S(1)}, f32[128,1152]{1,0:T(8,128)S(1)}, u32[]{:S(2)}, u32[]{:S(2)}) collective-permute-start(f32[128,1152]{1,0:T(8,128)S(1)} %add.296), channel_id=1, source_target_pairs={{0,960},{64,0},{128,64},{192,128},{256,192},{320,256},{384,320},{4... | collective-permute-start | bytes 1769480 | tf_op jit(solution)/shard_map/ppermute | solution.py:10
  272.2 28.3 %collective-permute-start.12 = (f32[128,1152]{1,0:T(8,128)S(1)}, f32[128,1152]{1,0:T(8,128)S(1)}, u32[]{:S(2)}, u32[]{:S(2)}) collective-permute-start(f32[128,1152]{1,0:T(8,128)S(1)} %add.297), channel_id=1, source_target_pairs={{0,960},{64,0},{128,64},{192,128},{256,192},{320,256},{384,320},{4... | collective-permute-start | bytes 1769480 | tf_op jit(solution)/shard_map/ppermute | solution.py:10
  300.5 27.0 %collective-permute-start.13 = (f32[128,1152]{1,0:T(8,128)S(1)}, f32[128,1152]{1,0:T(8,128)S(1)}, u32[]{:S(2)}, u32[]{:S(2)}) collective-permute-start(f32[128,1152]{1,0:T(8,128)S(1)} %add.298), channel_id=1, source_target_pairs={{0,960},{64,0},{128,64},{192,128},{256,192},{320,256},{384,320},{4... | collective-permute-start | bytes 1769480 | tf_op jit(solution)/shard_map/ppermute | solution.py:10
  327.6 165.4 %collective-permute-start.14 = (f32[128,1152]{1,0:T(8,128)S(1)}, f32[128,1152]{1,0:T(8,128)S(1)}, u32[]{:S(2)}, u32[]{:S(2)}) collective-permute-start(f32[128,1152]{1,0:T(8,128)S(1)} %add.299), channel_id=1, source_target_pairs={{0,960},{64,0},{128,64},{192,128},{256,192},{320,256},{384,320},{4... | collective-permute-start | bytes 1769480 | tf_op jit(solution)/shard_map/ppermute | solution.py:10
  492.9 4.3 copy-start.11
  493.0 29.2 %collective-permute-start.15 = (f32[128,1152]{1,0:T(8,128)S(1)}, f32[128,1152]{1,0:T(8,128)S(1)}, u32[]{:S(2)}, u32[]{:S(2)}) collective-permute-start(f32[128,1152]{1,0:T(8,128)S(1)} %add.300), channel_id=1, source_target_pairs={{0,256},{64,320},{128,384},{192,448},{256,512},{320,576},{384,640}... | collective-permute-start | bytes 1769480 | tf_op jit(solution)/shard_map/ppermute | solution.py:10
  497.8 24.4 %copy-start.9 = (f32[128]{0:T(128)S(1)}, f32[128]{0:T(128)}, u32[]{:S(2)}) copy-start(f32[128]{0:T(128)} %copy-done.8) | copy-start | bytes 1540
  (4 other events, 3.1 us)
where the time goes:
time: 525 us; the launch traced here: 523 us
  waiting for transfers between devices  199 us (38%)
  blocking collectives  155 us (30%)
  starting transfers between devices  134 us (26%)
  other arithmetic  20 us (4%)
  matrix products  9.62 us (2%)
    ppermute x16, waiting for transfers between devices, passed_along(): return lax.ppermute(value, axis, pairs)  199 us
    psum x1, blocking collectives, per_device(): summed = lax.psum(sums, ('blk', 'group'))  155 us
    ppermute x16, starting transfers between devices, passed_along(): return lax.ppermute(value, axis, pairs)  134 us
    add x1, other arithmetic, per_device(): sums = sums + part_sums  15.6 us
  transfers between devices with their start and end apart: 16, of which 15 were waited for; matrix products, arithmetic and copies ran while one was open for 5% of the time, Pallas kernels for 0%

commit v1 on v0

v1 whole, which is shorter than its diff:
```python
import functools

import jax
import jax.numpy as jnp
from jax import lax
from jax.experimental import pallas as pl
from jax.experimental.pallas import tpu as pltpu
from jax.sharding import PartitionSpec as P

VMEM = pl.BlockSpec(memory_space=pltpu.VMEM)
SMEM = pl.BlockSpec(memory_space=pltpu.SMEM)
F32 = jnp.float32
BF16 = jnp.bfloat16
PARAMS = pltpu.CompilerParams(vmem_limit_bytes=40 * 1024 * 1024)


def shape(rows, cols, dtype):
    return jax.ShapeDtypeStruct((rows, cols), dtype)


def as_column(row):
    n = row.shape[1]
    return jnp.broadcast_to(row, (n, n)).T


def normalize(raw):
    values = raw.astype(F32)
    scale = lax.rsqrt(jnp.sum(values * values, axis=-1, keepdims=True) + 1e-06)
    return values * scale, scale


def norm_back(unit, scale, upstream):
    return (upstream - unit * jnp.sum(unit * upstream, axis=-1, keepdims=True)) * scale


def matmul_t(a, b):
    return lax.dot_general(a, b, (((1,), (1,)), ((), ())), preferred_element_type=F32)


def matmul(a, b):
    return jnp.dot(a, b, preferred_element_type=F32)


def t_matmul(a, b):
    return lax.dot_general(a, b, (((0,), (0,)), ((), ())), preferred_element_type=F32)


class Scorer:
    def __init__(self, scal_ref, label_ref, place_ref):
        self.temper = jnp.exp(jnp.full((1, 128), scal_ref[0], F32))
        self.bias = scal_ref[1]
        self.labels = label_ref
        self.place = place_ref[0]
        self.columns = {}
        self.sums = None

    def side(self):
        return 1 - 2 * lax.rem(self.place, 2)

    def label_row(self, offset):
        count = self.labels.shape[0]
        at = lax.rem(self.place + offset + count, count)
        return self.labels[pl.ds(at, 1), :]

    def label_column(self, name, offset):
        if name not in self.columns:
            self.columns[name] = as_column(self.label_row(offset).astype(F32))
        return self.columns[name]

    def grads(self, image, text, weight, image_label, text_label, count_it):
        scaled = self.temper * matmul_t(image, text)
        logit = scaled + self.bias
        pos = image_label == text_label.astype(F32)
        small = jnp.exp(-jnp.abs(logit))
        share = 1.0 / (1.0 + small)
        sigmoid = jnp.where(logit >= 0, share, small * share)
        grad = weight * (sigmoid - pos.astype(F32))
        if count_it:
            signed = jnp.where(pos, -logit, logit)
            loss = weight * (jnp.maximum(signed, 0.0) + jnp.log1p(small))
            terms = (loss, grad * scaled, grad)
            self.sums = terms if self.sums is None else tuple(a + b for a, b in zip(self.sums, terms))
        return grad.astype(BF16)


def weight_of(packed, width):
    parts = [packed[:, width + at : width + at + 1].astype(F32) for at in (0, 32, 64)]
    return parts[0] + parts[1] + parts[2]


def prepare(image_ref, text_ref, weight_ref, text_unit_ref, image_pack_ref, both_ref):
    width = image_ref.shape[1]
    v = normalize(text_ref[...])[0].astype(BF16)
    u = normalize(image_ref[...])[0].astype(BF16)
    weight = as_column(weight_ref[...])
    high = weight.astype(BF16)
    rest = weight - high.astype(F32)
    middle = rest.astype(BF16)
    low = (rest - middle.astype(F32)).astype(BF16)
    lane = lax.broadcasted_iota(jnp.int32, weight.shape, 1)
    coded = jnp.where(lane < 32, high.astype(F32), jnp.where(lane < 64, middle.astype(F32), low.astype(F32))).astype(BF16)
    text_unit_ref[...] = v
    image_pack_ref[:, :width] = u
    image_pack_ref[:, width:] = coded
    both_ref[:, :width] = u
    both_ref[:, width : width + 128] = coded
    both_ref[:, width + 128 :] = v


def early_kernel(
    scal_ref, place_ref, label_ref, own_ref, after_ref, before_ref, cross_ref,
    image_total_ref, text_total_ref, far_ref, down_ref, up_ref, sums_ref,
):
    width = cross_ref.shape[1]
    scorer = Scorer(scal_ref, label_ref, place_ref)
    side = scorer.side()
    even = side == 1
    u, v = own_ref[:, :width], own_ref[:, width + 128 :]
    ua, va = after_ref[:, :width], after_ref[:, width + 128 :]
    ub, vb = before_ref[:, :width], before_ref[:, width + 128 :]
    vc = cross_ref[...]
    w, wa, wb = weight_of(own_ref, width), weight_of(after_ref, width), weight_of(before_ref, width)
    row, row_a, row_b = scorer.label_row(0), scorer.label_row(2), scorer.label_row(-2)
    row_c = scorer.label_row(side)
    col, col_a, col_b = as_column(row.astype(F32)), as_column(row_a.astype(F32)), as_column(row_b.astype(F32))
    g0 = scorer.grads(u, v, w, col, row, True)
    ga = scorer.grads(u, va, w, col, row_a, True)
    gb = scorer.grads(u, vb, w, col, row_b, True)
    gc = scorer.grads(u, vc, w, col, row_c, True)
    gfar = scorer.grads(ub, va, wb, col_b, row_a, True)
    ux = jnp.where(even, ub, ua)
    gx = scorer.grads(ux, vc, jnp.where(even, wb, wa), jnp.where(even, col_b, col_a), row_c, True)
    ta = scorer.grads(ua, v, wa, col_a, row, False)
    tb = scorer.grads(ub, v, wb, col_b, row, False)
    image_total_ref[...] = matmul(g0, v) + matmul(ga, va) + matmul(gb, vb) + matmul(gc, vc)
    text_total_ref[...] = t_matmul(g0, u) + t_matmul(ta, ua) + t_matmul(tb, ub)
    far_ref[...] = matmul(gx, vc)
    down_ref[...] = matmul(gfar, va)
    up_ref[...] = t_matmul(gfar, ub)
    sums_ref[...] = jnp.zeros_like(sums_ref)
    for at in range(3):
        sums_ref[at : at + 1, :] = jnp.sum(scorer.sums[at], axis=0, keepdims=True)


def relay_kernel(
    scal_ref, place_ref, label_ref, own_ref, after_ref, before_ref, relay_ref, early_ref,
    near_ref, far_ref, sums_ref,
):
    width = relay_ref.shape[1]
    scorer = Scorer(scal_ref, label_ref, place_ref)
    side = scorer.side()
    even = side == 1
    vr = relay_ref[...]
    row_r = scorer.label_row(-side)
    col = as_column(scorer.label_row(0).astype(F32))
    col_x = as_column(scorer.label_row(2 * side).astype(F32))
    near_ref[...] = scorer.grads(own_ref[:, :width], vr, weight_of(own_ref, width), col, row_r, True)
    ux = jnp.where(even, after_ref[:, :width], before_ref[:, :width])
    wx = jnp.where(even, weight_of(after_ref, width), weight_of(before_ref, width))
    far_ref[...] = scorer.grads(ux, vr, wx, col_x, row_r, True)
    lane = lax.broadcasted_iota(jnp.int32, (1, 128), 1)
    message = jnp.zeros((1, 128), F32)
    for at in range(3):
        total = jnp.sum(scorer.sums[at], axis=0, keepdims=True) + early_ref[at : at + 1, :]
        message = jnp.where(lane == at, jnp.sum(total, axis=1, keepdims=True), message)
    sums_ref[...] = message


def late_kernel(
    scal_ref, place_ref, label_ref, own_ref, after_ref, before_ref, cross_ref, relay_ref, relay_v_ref,
    near_ref, far_g_ref, far_ref, down_in_ref, up_in_ref, image_in_ref, text_in_ref,
    up_ref, down_ref, image_total_ref, text_total_ref,
):
    width = relay_v_ref.shape[1]
    rows = relay_v_ref.shape[0]
    scorer = Scorer(scal_ref, label_ref, place_ref)
    side = scorer.side()
    even = side == 1
    v = own_ref[:, width + 128 :]
    va, vb = after_ref[:, width + 128 :], before_ref[:, width + 128 :]
    uc, ur = cross_ref[:, :width], relay_ref[:, :width]
    wc, wr = weight_of(cross_ref, width), weight_of(relay_ref, width)
    col_c = as_column(scorer.label_row(side).astype(F32))
    col_r = as_column(scorer.label_row(-side).astype(F32))
    row, row_a, row_b = scorer.label_row(0), scorer.label_row(2), scorer.label_row(-2)
    gcx = scorer.grads(uc, jnp.where(even, vb, va), wc, col_c, jnp.where(even, row_b, row_a), False)
    grx = scorer.grads(ur, jnp.where(even, va, vb), wr, col_r, jnp.where(even, row_a, row_b), False)
    far_text_c = t_matmul(gcx, uc)
    far_text_r = t_matmul(grx, ur)
    far_image_c = far_ref[...]
    far_image_r = matmul(far_g_ref[...], relay_v_ref[...])
    up_ref[:rows, :] = jnp.where(even, far_image_r, far_image_c).astype(BF16)
    up_ref[rows:, :] = (up_in_ref[...] + jnp.where(even, far_text_r, far_text_c)).astype(BF16)
    down_ref[:rows, :] = (down_in_ref[...] + jnp.where(even, far_image_c, far_image_r)).astype(BF16)
    down_ref[rows:, :] = jnp.where(even, far_text_c, far_text_r).astype(BF16)
    gc = scorer.grads(uc, v, wc, col_c, row, False)
    gr = scorer.grads(ur, v, wr, col_r, row, False)
    image_total_ref[...] = image_in_ref[...] + matmul(near_ref[...], relay_v_ref[...])
    text_total_ref[...] = text_in_ref[...] + t_matmul(gc, uc) + t_matmul(gr, ur)


def final_kernel(scal_ref, image_ref, text_ref, image_total_ref, text_total_ref, up_ref, down_ref, image_grad_ref, text_grad_ref):
    rows, width = image_ref.shape
    temper = jnp.exp(jnp.full((1, 128), scal_ref[0], F32))[:, :1]
    for raw_ref, total_ref, out_ref, at in (
        (image_ref, image_total_ref, image_grad_ref, 0),
        (text_ref, text_total_ref, text_grad_ref, rows),
    ):
        total = total_ref[...] + up_ref[at : at + rows, :].astype(F32) + down_ref[at : at + rows, :].astype(F32)
        unit, scale = normalize(raw_ref[...])
        out_ref[...] = norm_back(unit, scale, temper * total).astype(BF16)


def call(kernel, ins, outs, name):
    return pl.pallas_call(
        kernel,
        out_shape=outs,
        in_specs=ins,
        out_specs=jax.tree.map(lambda _: VMEM, outs),
        compiler_params=PARAMS,
        name=name,
    )


def summed_over(axis, row):
    count = lax.axis_size(axis)
    sent = jnp.broadcast_to(row.reshape(1, 1, 128), (count, 1, 128))
    return jnp.sum(lax.all_to_all(sent, axis, 0, 0), axis=0)


def per_device(images, texts, labels, weights, log_temp, bias):
    cycle = lax.axis_size("blk")
    groups = lax.axis_size("group")
    rows, width = images.shape
    place = lax.axis_index("blk").astype(jnp.int32).reshape(1)
    scal = jnp.concatenate([log_temp, bias])
    head = [SMEM, SMEM, VMEM]

    def passed(value, step_of):
        return lax.ppermute(value, "blk", [(p, (p + step_of(p)) % cycle) for p in range(cycle)])

    def across(value):
        return passed(value, lambda p: 1 - 2 * (p % 2))

    def relayed(value):
        return passed(value, lambda p: 2 - 4 * (p % 2))

    def upward(value):
        return passed(value, lambda p: 2)

    def downward(value):
        return passed(value, lambda p: -2)

    block = shape(rows, width, F32)
    text_unit, image_pack, both = call(
        prepare,
        [VMEM] * 3,
        (shape(rows, width, BF16), shape(rows, width + 128, BF16), shape(rows, 2 * width + 128, BF16)),
        "prepare",
    )(images, texts, weights.reshape(1, rows))
    cross_v = across(text_unit)
    after = downward(both)
    before = upward(both)
    cross_u = across(image_pack)
    relay_v = relayed(cross_v)
    image_total, text_total, far, far_down, far_up, early = call(
        early_kernel, head + [VMEM] * 4, (block,) * 5 + (shape(8, 128, F32),), "early"
    )(scal, place, labels, both, after, before, cross_v)
    relay_u = relayed(cross_u)
    near_g, far_g, sums = call(
        relay_kernel, head + [VMEM] * 5, (shape(rows, rows, BF16),) * 2 + (shape(1, 128, F32),), "relay"
    )(scal, place, labels, both, after, before, relay_v, early)
    sums = summed_over("group", sums)
    to_up, to_down, image_total, text_total = call(
        late_kernel, head + [VMEM] * 13, (shape(2 * rows, width, BF16),) * 2 + (block,) * 2, "late"
    )(scal, place, labels, both, after, before, cross_u, relay_u, relay_v, near_g, far_g, far, far_down, far_up, image_total, text_total)
    from_below = upward(to_up)
    from_above = downward(to_down)
    sums = summed_over("blk", sums)
    image_grad, text_grad = call(
        final_kernel, [SMEM] + [VMEM] * 6, (shape(rows, width, BF16),) * 2, "final"
    )(scal, images, texts, image_total, text_total, from_below, from_above)
    count = float(cycle * groups * rows) * float(rows) * 8.0
    return image_grad, text_grad, sums.reshape(128)[:3] / count


def solution(mesh):
    rows = P(("blk", "group"), None)
    in_specs = (rows, rows, P(None, "group"), P(("blk", "group")), P(), P())
    return jax.shard_map(per_device, mesh=mesh, in_specs=in_specs, out_specs=(rows, rows, P()), check_vma=False)
```

time: 525 us -> 118 us (0.22)
  waiting for transfers between devices: 199 us -> 23.3 us
  blocking collectives: 155 us -> 35.9 us
  starting transfers between devices: 134 us -> 41 us
  other arithmetic: 20 us -> 0.63 us
  matrix products: 9.62 us -> 0 us
  Pallas kernels: 0 us -> 8.16 us
    ppermute x16 -> x8, waiting for transfers between devices: 199 us -> 23.3 us  [passed(): lax.ppermute(value, 'blk', [(p, (p + step_of(p)) % cycle) for p in range(...]
    psum x1 -> x0, blocking collectives: 155 us -> none  [per_device(): summed = lax.psum(sums, ('blk', 'group'))]
    ppermute x16 -> x8, starting transfers between devices: 134 us -> 41 us  [passed(): lax.ppermute(value, 'blk', [(p, (p + step_of(p)) % cycle) for p in range(...]
    all_to_all x0 -> x2, blocking collectives: none -> 35.9 us  [summed_over(): return jnp.sum(lax.all_to_all(sent, axis, 0, 0), axis=0)]
    add x7 -> x0, other arithmetic: 15.9 us -> none  [the longest x1 15.6 us: per_device(): sums = sums + part_sums]
    dot_general x24 -> x0, matrix products: 9.62 us -> none  [the longest x8 3.55 us: score_side(): lax.dot_general(image_unit, text_block, (((1,), (1,)), ((), ())), preferr...]
    pallas_call x0 -> x5, Pallas kernels: none -> 8.16 us  [the longest x1 2.84 us: per_device(): call(late_kernel, head + [VMEM] * 13, (shape(2 * rows, width, BF16),) * 2...]
  transfers between devices with their start and end apart: 16 -> 8, of which waited for: 15 -> 2; matrix products, arithmetic and copies ran while one was open for 5% -> 1% of each run, Pallas kernels for 0% -> 3%
where the time goes in v1:
time: 118 us; the launch traced here: 117 us
  starting transfers between devices  41 us (35%)
  blocking collectives  35.9 us (30%)
  waiting for transfers between devices  23.3 us (20%)
  Pallas kernels  8.16 us (7%)
  local copies, waits for them, and re-layouts  6.22 us (5%)
  between operations  2.09 us (2%)
    ppermute x8, starting transfers between devices, passed(): lax.ppermute(value, 'blk', [(p, (p + step_of(p)) % cycle) for p in range(...  41 us
    all_to_all x2, blocking collectives, summed_over(): return jnp.sum(lax.all_to_all(sent, axis, 0, 0), axis=0)  35.9 us
    ppermute x8, waiting for transfers between devices, passed(): lax.ppermute(value, 'blk', [(p, (p + step_of(p)) % cycle) for p in range(...  23.3 us
    unnamed x24, local copies, waits for them, and re-layouts  6.19 us
    pallas_call x1, Pallas kernels, per_device(): call(late_kernel, head + [VMEM] * 13, (shape(2 * rows, width, BF16),) * 2...  2.84 us
  transfers between devices with their start and end apart: 8, of which 2 were waited for; matrix products, arithmetic and copies ran while one was open for 1% of the time, Pallas kernels for 3%

profile of v1, /device:TPU:1, one launch (start us, length us, event | category | flops | bytes accessed | tf_op | source)
XLA Modules:
  0.0 117.3 jit_solution(16292130663146143112)
XLA Ops:
  0.6 0.6 copy-done.11
  1.3 1.0 copy-done
  2.3 1.0 copy-done.2
  3.4 8.7 %collective-permute-start.2 = (bf16[128,1280]{1,0:T(8,128)(2,1)S(1)}, bf16[128,1280]{1,0:T(8,128)(2,1)S(1)}, u32[]{:S(2)}, u32[]{:S(2)}) collective-permute-start(bf16[128,1280]{1,0:T(8,128)(2,1)S(1)} %get-tuple-element.22), channel_id=1, source_target_pairs={{0,64},{64,0},{128,192},{192,128},{256,320},{320,256},{384,448},{4... | collective-permute-start | bytes 983048 | tf_op jit(solution)/shard_map/ppermute | solution.py:240
  12.2 4.9 %collective-permute-start.1 = (bf16[128,2432]{1,0:T(8,128)(2,1)S(1)}, bf16[128,2432]{1,0:T(8,128)(2,1)S(1)}, u32[]{:S(2)}, u32[]{:S(2)}) collective-permute-start(bf16[128,2432]{1,0:T(8,128)(2,1)S(1)} %get-tuple-element.21.own_ref), channel_id=1, source_target_pairs={{0,128},{64,192},{128,256},{192,320},{256,384},{320,448},{384,512}... | collective-permute-start | bytes 1867784 | tf_op jit(solution)/shard_map/ppermute | solution.py:240
  17.1 14.0 %collective-permute-start = (bf16[128,2432]{1,0:T(8,128)(2,1)S(1)}, bf16[128,2432]{1,0:T(8,128)(2,1)S(1)}, u32[]{:S(2)}, u32[]{:S(2)}) collective-permute-start(bf16[128,2432]{1,0:T(8,128)(2,1)S(1)} %get-tuple-element.21.own_ref), channel_id=1, source_target_pairs={{0,896},{64,960},{128,0},{192,64},{256,128},{320,192},{384,256},{4... | collective-permute-start | bytes 1867784 | tf_op jit(solution)/shard_map/ppermute | solution.py:240
  31.2 1.9 %collective-permute-start.4 = (bf16[128,1152]{1,0:T(8,128)(2,1)S(1)}, bf16[128,1152]{1,0:T(8,128)(2,1)S(1)}, u32[]{:S(2)}, u32[]{:S(2)}) collective-permute-start(bf16[128,1152]{1,0:T(8,128)(2,1)S(1)} %get-tuple-element.23), channel_id=1, source_target_pairs={{0,64},{64,0},{128,192},{192,128},{256,320},{320,256},{384,448},{4... | collective-permute-start | bytes 884744 | tf_op jit(solution)/shard_map/ppermute | solution.py:240
  33.1 1.9 %collective-permute-start.3 = (bf16[128,1280]{1,0:T(8,128)(2,1)S(1)}, bf16[128,1280]{1,0:T(8,128)(2,1)S(1)}, u32[]{:S(2)}, u32[]{:S(2)}) collective-permute-start(bf16[128,1280]{1,0:T(8,128)(2,1)S(1)} %collective-permute-done.2.cross_ref), channel_id=1, source_target_pairs={{0,128},{64,960},{128,256},{192,64},{256,384},{320,192},{384,512},... | collective-permute-start | bytes 983048 | tf_op jit(solution)/shard_map/ppermute | solution.py:240
  35.0 10.5 %collective-permute-done.4.cross_ref = bf16[128,1152]{1,0:T(8,128)(2,1)S(1)} collective-permute-done((bf16[128,1152]{1,0:T(8,128)(2,1)S(1)}, bf16[128,1152]{1,0:T(8,128)(2,1)S(1)}, u32[]{:S(2)}, u32[]{:S(2)}) %collective-permute-start.4) | collective-permute-done | bytes 294944 | tf_op jit(solution)/shard_map/ppermute | solution.py:240
  45.5 3.0 %collective-permute-start.5 = (bf16[128,1152]{1,0:T(8,128)(2,1)S(1)}, bf16[128,1152]{1,0:T(8,128)(2,1)S(1)}, u32[]{:S(2)}, u32[]{:S(2)}) collective-permute-start(bf16[128,1152]{1,0:T(8,128)(2,1)S(1)} %collective-permute-done.4.cross_ref), channel_id=1, source_target_pairs={{0,128},{64,960},{128,256},{192,64},{256,384},{320,192},{384,512},... | collective-permute-start | bytes 884744 | tf_op jit(solution)/shard_map/ppermute | solution.py:240
  49.9 2.2 %early.1 = (f32[128,1152]{1,0:T(8,128)S(1)}, f32[128,1152]{1,0:T(8,128)S(1)}, f32[128,1152]{1,0:T(8,128)S(1)}, f32[128,1152]{1,0:T(8,128)S(1)}, f32[128,1152]{1,0:T(8,128)S(1)}, /*index=5*/f32[8,128]{1,0:T(8,128)S(1)}) custom-call(f32[2]{0:T(128)S(1)} %pad_maximum_fusion.scal_ref, s32[1]{0:T(128)} %bitcast.place_ref, s32[16,128]{1,0:T(8,128)S(1)} %copy-done.10, ...), custom_call_target="tpu_custom_call" | custom-call | tf_op jit(solution)/shard_map/early/pallas_call | solution.py:266
  52.1 12.8 %collective-permute-done.5.relay_ref.relay_v_ref = bf16[128,1152]{1,0:T(8,128)(2,1)S(1)} collective-permute-done((bf16[128,1152]{1,0:T(8,128)(2,1)S(1)}, bf16[128,1152]{1,0:T(8,128)(2,1)S(1)}, u32[]{:S(2)}, u32[]{:S(2)}) %collective-permute-start.5) | collective-permute-done | bytes 294944 | tf_op jit(solution)/shard_map/ppermute | solution.py:240
  65.0 1.0 relay.1
  66.0 0.7 copy-done.8
  66.7 1.0 copy-done.9
  67.7 2.8 %late.1 = (bf16[256,1152]{1,0:T(8,128)(2,1)}, bf16[256,1152]{1,0:T(8,128)(2,1)}, f32[128,1152]{1,0:T(8,128)S(1)}, f32[128,1152]{1,0:T(8,128)S(1)}) custom-call(f32[2]{0:T(128)S(1)} %pad_maximum_fusion.scal_ref, s32[1]{0:T(128)} %bitcast.place_ref, s32[16,128]{1,0:T(8,128)S(1)} %copy-done.10, bf16[128,2432]{1,0:T(8,128)(2,1)S(1)} %get-tuple-element.21.own_ref, ...), custom_call_target="tpu_custom_call" | custom-call | tf_op jit(solution)/shard_map/late/pallas_call | solution.py:274
  70.6 0.8 copy-done.4
  71.4 1.9 %collective-permute-start.6 = (bf16[256,1152]{1,0:T(8,128)(2,1)}, bf16[256,1152]{1,0:T(8,128)(2,1)S(1)}, u32[]{:S(2)}, u32[]{:S(2)}) collective-permute-start(bf16[256,1152]{1,0:T(8,128)(2,1)} %get-tuple-element.34), channel_id=1, source_target_pairs={{0,128},{64,192},{128,256},{192,320},{256,384},{320,448},{384,512}... | collective-permute-start | bytes 1769480 | tf_op jit(solution)/shard_map/ppermute | solution.py:240
  73.3 4.6 %collective-permute-start.7 = (bf16[256,1152]{1,0:T(8,128)(2,1)}, bf16[256,1152]{1,0:T(8,128)(2,1)S(1)}, u32[]{:S(2)}, u32[]{:S(2)}) collective-permute-start(bf16[256,1152]{1,0:T(8,128)(2,1)} %get-tuple-element.35), channel_id=1, source_target_pairs={{0,896},{64,960},{128,0},{192,64},{256,128},{320,192},{384,256},{4... | collective-permute-start | bytes 1769480 | tf_op jit(solution)/shard_map/ppermute | solution.py:240
  77.9 19.1 %all_to_all.10 = f32[64,1,128]{2,1,0:T(1,128)S(1)} all-to-all(f32[64,1,128]{2,1,0:T(1,128)S(1)} %broadcast_in_dim.13), channel_id=1, replica_groups=mesh['blk'=16,'group'=64] {'group'}, dimensions={0} | all-to-all | bytes 65536 | tf_op jit(solution)/shard_map/all_to_all | solution.py:228
  97.1 16.8 %all_to_all.11 = f32[16,1,128]{2,1,0:T(1,128)S(1)} all-to-all(f32[16,1,128]{2,1,0:T(1,128)S(1)} %broadcast_in_dim.14), channel_id=1, replica_groups=mesh['blk'=16,'group'=64] {'blk'}, dimensions={0} | all-to-all | bytes 16384 | tf_op jit(solution)/shard_map/all_to_all | solution.py:228
  113.8 0.5 multiply_bitcast_fusion
  114.4 1.1 copy-done.5
  115.4 1.9 %final.1 = (bf16[128,1152]{1,0:T(8,128)(2,1)}, bf16[128,1152]{1,0:T(8,128)(2,1)}) custom-call(f32[2]{0:T(128)S(1)} %pad_maximum_fusion.scal_ref, bf16[128,1152]{1,0:T(8,128)(2,1)S(1)} %copy-done.1, bf16[128,1152]{1,0:T(8,128)(2,1)S(1)} %copy-done.3, f32[128,1152]{1,0:T(8,128)S(1)} %get-tuple-element.32.image_total_ref, f32[128,1152]{1,0:T(8,128)S(1)} %copy-done.5, ...), custom_call_target="tpu_custom_call" | custom-call | tf_op jit(solution)/shard_map/final/pallas_call | solution.py:280
  (29 shorter events, 0.4 us)
Async XLA Ops:
  0.6 0.7 copy-start.11
  1.3 1.0 copy-start
  2.2 1.0 copy-start.2
  3.4 29.7 %collective-permute-start.2 = (bf16[128,1280]{1,0:T(8,128)(2,1)S(1)}, bf16[128,1280]{1,0:T(8,128)(2,1)S(1)}, u32[]{:S(2)}, u32[]{:S(2)}) collective-permute-start(bf16[128,1280]{1,0:T(8,128)(2,1)S(1)} %get-tuple-element.22), channel_id=1, source_target_pairs={{0,64},{64,0},{128,192},{192,128},{256,320},{320,256},{384,448},{4... | collective-permute-start | bytes 983048 | tf_op jit(solution)/shard_map/ppermute | solution.py:240
  12.2 37.7 %collective-permute-start.1 = (bf16[128,2432]{1,0:T(8,128)(2,1)S(1)}, bf16[128,2432]{1,0:T(8,128)(2,1)S(1)}, u32[]{:S(2)}, u32[]{:S(2)}) collective-permute-start(bf16[128,2432]{1,0:T(8,128)(2,1)S(1)} %get-tuple-element.21.own_ref), channel_id=1, source_target_pairs={{0,128},{64,192},{128,256},{192,320},{256,384},{320,448},{384,512}... | collective-permute-start | bytes 1867784 | tf_op jit(solution)/shard_map/ppermute | solution.py:240
  17.1 32.8 %collective-permute-start = (bf16[128,2432]{1,0:T(8,128)(2,1)S(1)}, bf16[128,2432]{1,0:T(8,128)(2,1)S(1)}, u32[]{:S(2)}, u32[]{:S(2)}) collective-permute-start(bf16[128,2432]{1,0:T(8,128)(2,1)S(1)} %get-tuple-element.21.own_ref), channel_id=1, source_target_pairs={{0,896},{64,960},{128,0},{192,64},{256,128},{320,192},{384,256},{4... | collective-permute-start | bytes 1867784 | tf_op jit(solution)/shard_map/ppermute | solution.py:240
  31.1 18.8 %copy-start.10 = (s32[16,128]{1,0:T(8,128)S(1)}, s32[16,128]{1,0:T(8,128)}, u32[]{:S(2)}) copy-start(s32[16,128]{1,0:T(8,128)} %label_ref.5) | copy-start | bytes 24580
  31.2 14.4 %collective-permute-start.4 = (bf16[128,1152]{1,0:T(8,128)(2,1)S(1)}, bf16[128,1152]{1,0:T(8,128)(2,1)S(1)}, u32[]{:S(2)}, u32[]{:S(2)}) collective-permute-start(bf16[128,1152]{1,0:T(8,128)(2,1)S(1)} %get-tuple-element.23), channel_id=1, source_target_pairs={{0,64},{64,0},{128,192},{192,128},{256,320},{320,256},{384,448},{4... | collective-permute-start | bytes 884744 | tf_op jit(solution)/shard_map/ppermute | solution.py:240
  33.1 19.0 %copy-start.6 = (bf16[128,1280]{1,0:T(8,128)(2,1)}, bf16[128,1280]{1,0:T(8,128)(2,1)S(1)}, u32[]{:S(2)}) copy-start(bf16[128,1280]{1,0:T(8,128)(2,1)S(1)} %collective-permute-done.2.cross_ref) | copy-start | bytes 983044
  33.1 32.9 %collective-permute-start.3 = (bf16[128,1280]{1,0:T(8,128)(2,1)S(1)}, bf16[128,1280]{1,0:T(8,128)(2,1)S(1)}, u32[]{:S(2)}, u32[]{:S(2)}) collective-permute-start(bf16[128,1280]{1,0:T(8,128)(2,1)S(1)} %collective-permute-done.2.cross_ref), channel_id=1, source_target_pairs={{0,128},{64,960},{128,256},{192,64},{256,384},{320,192},{384,512},... | collective-permute-start | bytes 983048 | tf_op jit(solution)/shard_map/ppermute | solution.py:240
  45.5 19.4 %collective-permute-start.5 = (bf16[128,1152]{1,0:T(8,128)(2,1)S(1)}, bf16[128,1152]{1,0:T(8,128)(2,1)S(1)}, u32[]{:S(2)}, u32[]{:S(2)}) collective-permute-start(bf16[128,1152]{1,0:T(8,128)(2,1)S(1)} %collective-permute-done.4.cross_ref), channel_id=1, source_target_pairs={{0,128},{64,960},{128,256},{192,64},{256,384},{320,192},{384,512},... | collective-permute-start | bytes 884744 | tf_op jit(solution)/shard_map/ppermute | solution.py:240
  65.0 1.8 %copy-start.7 = (bf16[128,1280]{1,0:T(8,128)(2,1)S(1)}, bf16[128,1280]{1,0:T(8,128)(2,1)}, u32[]{:S(2)}) copy-start(bf16[128,1280]{1,0:T(8,128)(2,1)} %copy-done.6) | copy-start | bytes 983044
  66.0 0.7 copy-start.8
  66.7 1.0 copy-start.9
  67.7 46.6 %copy-start.1 = (bf16[128,1152]{1,0:T(8,128)(2,1)S(1)}, bf16[128,1152]{1,0:T(8,128)(2,1)}, u32[]{:S(2)}) copy-start(bf16[128,1152]{1,0:T(8,128)(2,1)} %image_ref.3) | copy-start | bytes 884740
  67.7 46.6 %copy-start.3 = (bf16[128,1152]{1,0:T(8,128)(2,1)S(1)}, bf16[128,1152]{1,0:T(8,128)(2,1)}, u32[]{:S(2)}) copy-start(bf16[128,1152]{1,0:T(8,128)(2,1)} %text_ref.3) | copy-start | bytes 884740
  70.6 0.8 copy-start.4
  71.4 43.0 %collective-permute-start.6 = (bf16[256,1152]{1,0:T(8,128)(2,1)}, bf16[256,1152]{1,0:T(8,128)(2,1)S(1)}, u32[]{:S(2)}, u32[]{:S(2)}) collective-permute-start(bf16[256,1152]{1,0:T(8,128)(2,1)} %get-tuple-element.34), channel_id=1, source_target_pairs={{0,128},{64,192},{128,256},{192,320},{256,384},{320,448},{384,512}... | collective-permute-start | bytes 1769480 | tf_op jit(solution)/shard_map/ppermute | solution.py:240
  73.3 41.0 %collective-permute-start.7 = (bf16[256,1152]{1,0:T(8,128)(2,1)}, bf16[256,1152]{1,0:T(8,128)(2,1)S(1)}, u32[]{:S(2)}, u32[]{:S(2)}) collective-permute-start(bf16[256,1152]{1,0:T(8,128)(2,1)} %get-tuple-element.35), channel_id=1, source_target_pairs={{0,896},{64,960},{128,0},{192,64},{256,128},{320,192},{384,256},{4... | collective-permute-start | bytes 1769480 | tf_op jit(solution)/shard_map/ppermute | solution.py:240
  114.4 1.1 copy-start.5

commit v2 on v1

--- a/solution.py
+++ b/solution.py
@@ -11,7 +11,7 @@
 SMEM = pl.BlockSpec(memory_space=pltpu.SMEM)
 F32 = jnp.float32
 BF16 = jnp.bfloat16
-PARAMS = pltpu.CompilerParams(vmem_limit_bytes=40 * 1024 * 1024)
+PARAMS = pltpu.CompilerParams(vmem_limit_bytes=16 * 1024 * 1024)
 
 
 def shape(rows, cols, dtype):
@@ -82,15 +82,23 @@
             self.sums = terms if self.sums is None else tuple(a + b for a, b in zip(self.sums, terms))
         return grad.astype(BF16)
 
+    def store_sums(self, out_ref, more_ref=None):
+        out_ref[...] = jnp.zeros_like(out_ref) if more_ref is None else more_ref[...]
+        for at in range(3):
+            out_ref[at : at + 1, :] += jnp.sum(self.sums[at], axis=0, keepdims=True)
+
 
 def weight_of(packed, width):
     parts = [packed[:, width + at : width + at + 1].astype(F32) for at in (0, 32, 64)]
     return parts[0] + parts[1] + parts[2]
 
 
-def prepare(image_ref, text_ref, weight_ref, text_unit_ref, image_pack_ref, both_ref):
+def text_kernel(text_ref, text_unit_ref):
+    text_unit_ref[...] = normalize(text_ref[...])[0].astype(BF16)
+
+
+def image_kernel(image_ref, weight_ref, text_unit_ref, image_pack_ref, both_ref):
     width = image_ref.shape[1]
-    v = normalize(text_ref[...])[0].astype(BF16)
     u = normalize(image_ref[...])[0].astype(BF16)
     weight = as_column(weight_ref[...])
     high = weight.astype(BF16)
@@ -99,16 +107,31 @@
     low = (rest - middle.astype(F32)).astype(BF16)
     lane = lax.broadcasted_iota(jnp.int32, weight.shape, 1)
     coded = jnp.where(lane < 32, high.astype(F32), jnp.where(lane < 64, middle.astype(F32), low.astype(F32))).astype(BF16)
-    text_unit_ref[...] = v
     image_pack_ref[:, :width] = u
     image_pack_ref[:, width:] = coded
     both_ref[:, :width] = u
     both_ref[:, width : width + 128] = coded
-    both_ref[:, width + 128 :] = v
+    both_ref[:, width + 128 :] = text_unit_ref[...]
+
+
+def own_kernel(scal_ref, place_ref, label_ref, own_ref, cross_ref, image_total_ref, text_total_ref, sums_ref):
+    width = cross_ref.shape[1]
+    scorer = Scorer(scal_ref, label_ref, place_ref)
+    u, v = own_ref[:, :width], own_ref[:, width + 128 :]
+    vc = cross_ref[...]
+    w = weight_of(own_ref, width)
+    row = scorer.label_row(0)
+    col = as_column(row.astype(F32))
+    g0 = scorer.grads(u, v, w, col, row, True)
+    gc = scorer.grads(u, vc, w, col, scorer.label_row(scorer.side()), True)
+    image_total_ref[...] = matmul(g0, v) + matmul(gc, vc)
+    text_total_ref[...] = t_matmul(g0, u)
+    scorer.store_sums(sums_ref)
 
 
 def early_kernel(
     scal_ref, place_ref, label_ref, own_ref, after_ref, before_ref, cross_ref,
+    image_in_ref, text_in_ref, sums_in_ref,
     image_total_ref, text_total_ref, far_ref, down_ref, up_ref, sums_ref,
 ):
     width = cross_ref.shape[1]
@@ -123,23 +146,19 @@
     row, row_a, row_b = scorer.label_row(0), scorer.label_row(2), scorer.label_row(-2)
     row_c = scorer.label_row(side)
     col, col_a, col_b = as_column(row.astype(F32)), as_column(row_a.astype(F32)), as_column(row_b.astype(F32))
-    g0 = scorer.grads(u, v, w, col, row, True)
     ga = scorer.grads(u, va, w, col, row_a, True)
     gb = scorer.grads(u, vb, w, col, row_b, True)
-    gc = scorer.grads(u, vc, w, col, row_c, True)
     gfar = scorer.grads(ub, va, wb, col_b, row_a, True)
     ux = jnp.where(even, ub, ua)
     gx = scorer.grads(ux, vc, jnp.where(even, wb, wa), jnp.where(even, col_b, col_a), row_c, True)
     ta = scorer.grads(ua, v, wa, col_a, row, False)
     tb = scorer.grads(ub, v, wb, col_b, row, False)
-    image_total_ref[...] = matmul(g0, v) + matmul(ga, va) + matmul(gb, vb) + matmul(gc, vc)
-    text_total_ref[...] = t_matmul(g0, u) + t_matmul(ta, ua) + t_matmul(tb, ub)
+    image_total_ref[...] = image_in_ref[...] + matmul(ga, va) + matmul(gb, vb)
+    text_total_ref[...] = text_in_ref[...] + t_matmul(ta, ua) + t_matmul(tb, ub)
     far_ref[...] = matmul(gx, vc)
     down_ref[...] = matmul(gfar, va)
     up_ref[...] = t_matmul(gfar, ub)
-    sums_ref[...] = jnp.zeros_like(sums_ref)
-    for at in range(3):
-        sums_ref[at : at + 1, :] = jnp.sum(scorer.sums[at], axis=0, keepdims=True)
+    scorer.store_sums(sums_ref, sums_in_ref)
 
 
 def relay_kernel(
@@ -168,8 +187,8 @@
 
 def late_kernel(
     scal_ref, place_ref, label_ref, own_ref, after_ref, before_ref, cross_ref, relay_ref, relay_v_ref,
-    near_ref, far_g_ref, far_ref, down_in_ref, up_in_ref, image_in_ref, text_in_ref,
-    up_ref, down_ref, image_total_ref, text_total_ref,
+    near_ref, far_g_ref, far_ref, down_in_ref, up_in_ref, image_in_ref, text_in_ref, got_ref,
+    up_ref, down_ref, image_total_ref, text_total_ref, sums_ref,
 ):
     width = relay_v_ref.shape[1]
     rows = relay_v_ref.shape[0]
@@ -197,9 +216,13 @@
     gr = scorer.grads(ur, v, wr, col_r, row, False)
     image_total_ref[...] = image_in_ref[...] + matmul(near_ref[...], relay_v_ref[...])
     text_total_ref[...] = text_in_ref[...] + t_matmul(gc, uc) + t_matmul(gr, ur)
-
-
-def final_kernel(scal_ref, image_ref, text_ref, image_total_ref, text_total_ref, up_ref, down_ref, image_grad_ref, text_grad_ref):
+    sums_ref[...] = jnp.sum(got_ref[...], axis=0, keepdims=True)
+
+
+def final_kernel(
+    count, scal_ref, image_ref, text_ref, image_total_ref, text_total_ref, up_ref, down_ref, got_ref,
+    image_grad_ref, text_grad_ref, stats_ref,
+):
     rows, width = image_ref.shape
     temper = jnp.exp(jnp.full((1, 128), scal_ref[0], F32))[:, :1]
     for raw_ref, total_ref, out_ref, at in (
@@ -209,23 +232,27 @@
         total = total_ref[...] + up_ref[at : at + rows, :].astype(F32) + down_ref[at : at + rows, :].astype(F32)
         unit, scale = normalize(raw_ref[...])
         out_ref[...] = norm_back(unit, scale, temper * total).astype(BF16)
-
-
-def call(kernel, ins, outs, name):
+    got = jnp.sum(got_ref[...], axis=0, keepdims=True) / count
+    for at in range(3):
+        stats_ref[at] = got[0, at]
+
+
+def call(kernel, ins, outs, name, work, out_specs=None):
     return pl.pallas_call(
         kernel,
         out_shape=outs,
         in_specs=ins,
-        out_specs=jax.tree.map(lambda _: VMEM, outs),
+        out_specs=jax.tree.map(lambda _: VMEM, outs) if out_specs is None else out_specs,
         compiler_params=PARAMS,
+        cost_estimate=pl.CostEstimate(flops=work, bytes_accessed=0, transcendentals=0),
         name=name,
     )
 
 
-def summed_over(axis, row):
+def exchanged(row, axis):
     count = lax.axis_size(axis)
     sent = jnp.broadcast_to(row.reshape(1, 1, 128), (count, 1, 128))
-    return jnp.sum(lax.all_to_all(sent, axis, 0, 0), axis=0)
+    return lax.all_to_all(sent, axis, 0, 0).reshape(count, 128)
 
 
 def per_device(images, texts, labels, weights, log_temp, bias):
@@ -235,6 +262,7 @@
     place = lax.axis_index("blk").astype(jnp.int32).reshape(1)
     scal = jnp.concatenate([log_temp, bias])
     head = [SMEM, SMEM, VMEM]
+    dot = 2 * rows * rows * width
 
     def passed(value, step_of):
         return lax.ppermute(value, "blk", [(p, (p + step_of(p)) % cycle) for p in range(cycle)])
@@ -252,36 +280,54 @@
         return passed(value, lambda p: -2)
 
     block = shape(rows, width, F32)
-    text_unit, image_pack, both = call(
-        prepare,
+    text_unit = call(text_kernel, [VMEM], shape(rows, width, BF16), "text", 10 * dot)(texts)
+    cross_v = across(text_unit)
+    image_pack, both = call(
+        image_kernel,
         [VMEM] * 3,
-        (shape(rows, width, BF16), shape(rows, width + 128, BF16), shape(rows, 2 * width + 128, BF16)),
-        "prepare",
-    )(images, texts, weights.reshape(1, rows))
-    cross_v = across(text_unit)
+        (shape(rows, width + 128, BF16), shape(rows, 2 * width + 128, BF16)),
+        "image",
+        10 * dot,
+    )(images, weights.reshape(1, rows), text_unit)
     after = downward(both)
     before = upward(both)
     cross_u = across(image_pack)
     relay_v = relayed(cross_v)
-    image_total, text_total, far, far_down, far_up, early = call(
-        early_kernel, head + [VMEM] * 4, (block,) * 5 + (shape(8, 128, F32),), "early"
-    )(scal, place, labels, both, after, before, cross_v)
+    image_total, text_total, sums = call(
+        own_kernel, head + [VMEM] * 2, (block,) * 2 + (shape(8, 128, F32),), "own", 150 * dot
+    )(scal, place, labels, both, cross_v)
+    image_total, text_total, far, far_down, far_up, sums = call(
+        early_kernel, head + [VMEM] * 7, (block,) * 5 + (shape(8, 128, F32),), "early", 20 * dot
+    )(scal, place, labels, both, after, before, cross_v, image_total, text_total, sums)
+    cross_u, sums = lax.optimization_barrier((cross_u, sums))
     relay_u = relayed(cross_u)
     near_g, far_g, sums = call(
-        relay_kernel, head + [VMEM] * 5, (shape(rows, rows, BF16),) * 2 + (shape(1, 128, F32),), "relay"
-    )(scal, place, labels, both, after, before, relay_v, early)
-    sums = summed_over("group", sums)
-    to_up, to_down, image_total, text_total = call(
-        late_kernel, head + [VMEM] * 13, (shape(2 * rows, width, BF16),) * 2 + (block,) * 2, "late"
-    )(scal, place, labels, both, after, before, cross_u, relay_u, relay_v, near_g, far_g, far, far_down, far_up, image_total, text_total)
+        relay_kernel, head + [VMEM] * 5, (shape(rows, rows, BF16),) * 2 + (shape(1, 128, F32),), "relay", 10 * dot
+    )(scal, place, labels, both, after, before, relay_v, sums)
+    got = exchanged(sums, "group")
+    to_up, to_down, image_total, text_total, sums = call(
+        late_kernel,
+        head + [VMEM] * 14,
+        (shape(2 * rows, width, BF16),) * 2 + (block,) * 2 + (shape(1, 128, F32),),
+        "late",
+        20 * dot,
+    )(
+        scal, place, labels, both, after, before, cross_u, relay_u, relay_v,
+        near_g, far_g, far, far_down, far_up, image_total, text_total, got,
+    )
     from_below = upward(to_up)
     from_above = downward(to_down)
-    sums = summed_over("blk", sums)
-    image_grad, text_grad = call(
-        final_kernel, [SMEM] + [VMEM] * 6, (shape(rows, width, BF16),) * 2, "final"
-    )(scal, images, texts, image_total, text_total, from_below, from_above)
+    got = exchanged(sums, "blk")
     count = float(cycle * groups * rows) * float(rows) * 8.0
-    return image_grad, text_grad, sums.reshape(128)[:3] / count
+    image_grad, text_grad, stats = call(
+        functools.partial(final_kernel, count),
+        [SMEM] + [VMEM] * 7,
+        (shape(rows, width, BF16),) * 2 + (jax.ShapeDtypeStruct((3,), F32),),
+        "final",
+        10 * dot,
+        (VMEM, VMEM, SMEM),
+    )(scal, images, texts, image_total, text_total, from_below, from_above, got)
+    return image_grad, text_grad, stats
 
 
 def solution(mesh):

time: 118 us -> 103 us (0.87)
  waiting for transfers between devices: 23.3 us -> 7.37 us
  blocking collectives: 35.9 us -> 41.6 us
  local copies, waits for them, and re-layouts: 6.22 us -> 1.05 us
    ppermute x8, waiting for transfers between devices: 23.3 us -> 7.37 us  [passed(): lax.ppermute(value, 'blk', [(p, (p + step_of(p)) % cycle) for p in range(...]
    all_to_all x2, blocking collectives: 35.9 us -> 41.6 us  [exchanged(): return lax.all_to_all(sent, axis, 0, 0).reshape(count, 128)]
    unnamed x24 -> x10, local copies, waits for them, and re-layouts: 6.19 us -> 1.02 us
    pallas_call x4 -> x6, Pallas kernels: 7.12 us -> 7.52 us  [the longest x1 2 us: per_device(): call(late_kernel, head + [VMEM] * 14, (shape(2 * rows, width, BF16),) * 2...]
  transfers between devices with their start and end apart: 8 -> 8, of which waited for: 2 -> 4; matrix products, arithmetic and copies ran while one was open for 1% -> 0% of each run, Pallas kernels for 3% -> 4%
where the time goes in v2:
time: 103 us
  starting transfers between devices  41.8 us (41%)
  blocking collectives  41.6 us (40%)
  Pallas kernels  8.56 us (8%)
  waiting for transfers between devices  7.37 us (7%)
  between operations  2.09 us (2%)
  local copies, waits for them, and re-layouts  1.05 us (1%)
    ppermute x8, starting transfers between devices, passed(): lax.ppermute(value, 'blk', [(p, (p + step_of(p)) % cycle) for p in range(...  41.8 us
    all_to_all x2, blocking collectives, exchanged(): return lax.all_to_all(sent, axis, 0, 0).reshape(count, 128)  41.6 us
    ppermute x8, waiting for transfers between devices, passed(): lax.ppermute(value, 'blk', [(p, (p + step_of(p)) % cycle) for p in range(...  7.37 us
  transfers between devices with their start and end apart: 8, of which 4 were waited for; matrix products, arithmetic and copies ran while one was open for 0% of the time, Pallas kernels for 4%

profile of v2, /device:TPU:1, one launch (start us, length us, event | category | flops | bytes accessed | tf_op | source)
XLA Modules:
  0.0 102.6 jit_solution(431629580384798147)
XLA Ops:
  0.7 1.0 copy-done.1
  1.6 0.1 text.1.text_unit_ref
  1.8 0.0 copy-start.4
  1.8 8.7 %collective-permute-start.3 = (bf16[128,1152]{1,0:T(8,128)(2,1)S(1)}, bf16[128,1152]{1,0:T(8,128)(2,1)S(1)}, u32[]{:S(2)}, u32[]{:S(2)}) collective-permute-start(bf16[128,1152]{1,0:T(8,128)(2,1)S(1)} %text.1.text_unit_ref), channel_id=1, source_target_pairs={{0,64},{64,0},{128,192},{192,128},{256,320},{320,256},{384,448},{4... | collective-permute-start | bytes 884744 | tf_op jit(solution)/shard_map/ppermute | solution.py:268
  10.6 0.2 image.1
  10.8 4.9 %collective-permute-start.1 = (bf16[128,2432]{1,0:T(8,128)(2,1)S(1)}, bf16[128,2432]{1,0:T(8,128)(2,1)S(1)}, u32[]{:S(2)}, u32[]{:S(2)}) collective-permute-start(bf16[128,2432]{1,0:T(8,128)(2,1)S(1)} %get-tuple-element.24.own_ref), channel_id=1, source_target_pairs={{0,128},{64,192},{128,256},{192,320},{256,384},{320,448},{384,512}... | collective-permute-start | bytes 1867784 | tf_op jit(solution)/shard_map/ppermute | solution.py:268
  15.7 14.2 %collective-permute-start = (bf16[128,2432]{1,0:T(8,128)(2,1)S(1)}, bf16[128,2432]{1,0:T(8,128)(2,1)S(1)}, u32[]{:S(2)}, u32[]{:S(2)}) collective-permute-start(bf16[128,2432]{1,0:T(8,128)(2,1)S(1)} %get-tuple-element.24.own_ref), channel_id=1, source_target_pairs={{0,896},{64,960},{128,0},{192,64},{256,128},{320,192},{384,256},{4... | collective-permute-start | bytes 1867784 | tf_op jit(solution)/shard_map/ppermute | solution.py:268
  29.9 1.9 %collective-permute-start.2 = (bf16[128,1280]{1,0:T(8,128)(2,1)S(1)}, bf16[128,1280]{1,0:T(8,128)(2,1)S(1)}, u32[]{:S(2)}, u32[]{:S(2)}) collective-permute-start(bf16[128,1280]{1,0:T(8,128)(2,1)S(1)} %get-tuple-element.25), channel_id=1, source_target_pairs={{0,64},{64,0},{128,192},{192,128},{256,320},{320,256},{384,448},{4... | collective-permute-start | bytes 983048 | tf_op jit(solution)/shard_map/ppermute | solution.py:268
  33.1 0.1 pad_maximum_fusion.scal_ref
  33.2 1.9 %collective-permute-start.5 = (bf16[128,1152]{1,0:T(8,128)(2,1)S(1)}, bf16[128,1152]{1,0:T(8,128)(2,1)S(1)}, u32[]{:S(2)}, u32[]{:S(2)}) collective-permute-start(bf16[128,1152]{1,0:T(8,128)(2,1)S(1)} %collective-permute-done.3.cross_ref), channel_id=1, source_target_pairs={{0,128},{64,960},{128,256},{192,64},{256,384},{320,192},{384,512},... | collective-permute-start | bytes 884744 | tf_op jit(solution)/shard_map/ppermute | solution.py:268
  35.1 1.3 %own.1 = (f32[128,1152]{1,0:T(8,128)S(1)}, f32[128,1152]{1,0:T(8,128)S(1)}, f32[8,128]{1,0:T(8,128)S(1)}) custom-call(f32[2]{0:T(128)S(1)} %pad_maximum_fusion.scal_ref, s32[1]{0:T(128)} %bitcast.place_ref, s32[16,128]{1,0:T(8,128)S(1)} %copy-done.3, bf16[128,2432]{1,0:T(8,128)(2,1)S(1)} %get-tuple-element.24.own_ref, ...), custom_call_target="tpu_custom_call" | custom-call | flops 5662310400 | tf_op jit(solution)/shard_map/own/pallas_call | solution.py:296
  36.4 4.9 %collective-permute-done.1.before_ref = bf16[128,2432]{1,0:T(8,128)(2,1)S(1)} collective-permute-done((bf16[128,2432]{1,0:T(8,128)(2,1)S(1)}, bf16[128,2432]{1,0:T(8,128)(2,1)S(1)}, u32[]{:S(2)}, u32[]{:S(2)}) %collective-permute-start.1) | collective-permute-done | bytes 622624 | tf_op jit(solution)/shard_map/ppermute | solution.py:268
  41.4 0.9 collective-permute-done.after_ref
  42.2 2.0 %early.1 = (f32[128,1152]{1,0:T(8,128)S(1)}, f32[128,1152]{1,0:T(8,128)S(1)}, f32[128,1152]{1,0:T(8,128)S(1)}, f32[128,1152]{1,0:T(8,128)S(1)}, f32[128,1152]{1,0:T(8,128)S(1)}, /*index=5*/f32[8,128]{1,0:T(8,128)S(1)}) custom-call(f32[2]{0:T(128)S(1)} %pad_maximum_fusion.scal_ref, s32[1]{0:T(128)} %bitcast.place_ref, s32[16,128]{1,0:T(8,128)S(1)} %copy-done.3, ...), custom_call_target="tpu_custom_call" | custom-call | flops 754974720 | tf_op jit(solution)/shard_map/early/pallas_call | solution.py:299
  44.2 1.0 %collective-permute-done.2.cross_ref = bf16[128,1280]{1,0:T(8,128)(2,1)S(1)} collective-permute-done((bf16[128,1280]{1,0:T(8,128)(2,1)S(1)}, bf16[128,1280]{1,0:T(8,128)(2,1)S(1)}, u32[]{:S(2)}, u32[]{:S(2)}) %collective-permute-start.2) | collective-permute-done | bytes 327712 | tf_op jit(solution)/shard_map/ppermute | solution.py:268
  45.2 1.9 %collective-permute-start.4 = (bf16[128,1280]{1,0:T(8,128)(2,1)S(1)}, bf16[128,1280]{1,0:T(8,128)(2,1)S(1)}, u32[]{:S(2)}, u32[]{:S(2)}) collective-permute-start(bf16[128,1280]{1,0:T(8,128)(2,1)S(1)} %collective-permute-done.2.cross_ref), channel_id=1, source_target_pairs={{0,128},{64,960},{128,256},{192,64},{256,384},{320,192},{384,512},... | collective-permute-start | bytes 983048 | tf_op jit(solution)/shard_map/ppermute | solution.py:268
  47.2 0.5 collective-permute-done.5.relay_ref.relay_v_ref
  47.7 1.0 %relay.1 = (bf16[128,128]{1,0:T(8,128)(2,1)S(1)}, bf16[128,128]{1,0:T(8,128)(2,1)S(1)}, f32[1,128]{1,0:T(1,128)S(1)}) custom-call(f32[2]{0:T(128)S(1)} %pad_maximum_fusion.scal_ref, s32[1]{0:T(128)} %bitcast.place_ref, s32[16,128]{1,0:T(8,128)S(1)} %copy-done.3, bf16[128,2432]{1,0:T(8,128)(2,1)S(1)} %get-tuple-element.24.own_ref, ...), custom_call_target="tpu_custom_call" | custom-call | flops 377487360 | tf_op jit(solution)/shard_map/relay/pallas_call | solution.py:304
  48.8 24.1 %all_to_all.10 = f32[64,1,128]{2,1,0:T(1,128)S(1)} all-to-all(f32[64,1,128]{2,1,0:T(1,128)S(1)} %broadcast_in_dim.15), channel_id=1, replica_groups=mesh['blk'=16,'group'=64] {'group'}, dimensions={0} | all-to-all | bytes 65536 | tf_op jit(solution)/shard_map/all_to_all | solution.py:255
  72.8 2.0 %late.1 = (bf16[256,1152]{1,0:T(8,128)(2,1)S(1)}, bf16[256,1152]{1,0:T(8,128)(2,1)S(1)}, f32[128,1152]{1,0:T(8,128)S(1)}, f32[128,1152]{1,0:T(8,128)S(1)}, f32[1,128]{1,0:T(1,128)S(1)}) custom-call(f32[2]{0:T(128)S(1)} %pad_maximum_fusion.scal_ref, s32[1]{0:T(128)} %bitcast.place_ref, s32[16,128]{1,0:T(8,128)S(1)} %copy-done.3, ...), custom_call_target="tpu_custom_call" | custom-call | flops 754974720 | tf_op jit(solution)/shard_map/late/pallas_call | solution.py:308
  74.8 1.9 %collective-permute-start.6 = (bf16[256,1152]{1,0:T(8,128)(2,1)S(1)}, bf16[256,1152]{1,0:T(8,128)(2,1)S(1)}, u32[]{:S(2)}, u32[]{:S(2)}) collective-permute-start(bf16[256,1152]{1,0:T(8,128)(2,1)S(1)} %get-tuple-element.42), channel_id=1, source_target_pairs={{0,128},{64,192},{128,256},{192,320},{256,384},{320,448},{384,512}... | collective-permute-start | bytes 1769480 | tf_op jit(solution)/shard_map/ppermute | solution.py:268
  76.8 6.3 %collective-permute-start.7 = (bf16[256,1152]{1,0:T(8,128)(2,1)S(1)}, bf16[256,1152]{1,0:T(8,128)(2,1)S(1)}, u32[]{:S(2)}, u32[]{:S(2)}) collective-permute-start(bf16[256,1152]{1,0:T(8,128)(2,1)S(1)} %get-tuple-element.43), channel_id=1, source_target_pairs={{0,896},{64,960},{128,0},{192,64},{256,128},{320,192},{384,256},{4... | collective-permute-start | bytes 1769480 | tf_op jit(solution)/shard_map/ppermute | solution.py:268
  83.1 17.5 %all_to_all.11 = f32[16,1,128]{2,1,0:T(1,128)S(1)} all-to-all(f32[16,1,128]{2,1,0:T(1,128)S(1)} %broadcast_in_dim.17), channel_id=1, replica_groups=mesh['blk'=16,'group'=64] {'blk'}, dimensions={0} | all-to-all | bytes 16384 | tf_op jit(solution)/shard_map/all_to_all | solution.py:255
  100.6 1.9 %final.1 = (bf16[128,1152]{1,0:T(8,128)(2,1)}, bf16[128,1152]{1,0:T(8,128)(2,1)}, f32[3]{0:T(128)}) custom-call(f32[2]{0:T(128)S(1)} %pad_maximum_fusion.scal_ref, bf16[128,1152]{1,0:T(8,128)(2,1)S(1)} %copy-done, bf16[128,1152]{1,0:T(8,128)(2,1)S(1)} %copy-done.2, f32[128,1152]{1,0:T(8,128)S(1)} %get-tuple-element.40.image_total_ref, ...), custom_call_target="tpu_custom_call" | custom-call | flops 377487360 | tf_op jit(solution)/shard_map/final/pallas_call | solution.py:322
  (14 shorter events, 0.1 us)
Async XLA Ops:
  0.6 9.9 %copy-start = (bf16[128,1152]{1,0:T(8,128)(2,1)S(1)}, bf16[128,1152]{1,0:T(8,128)(2,1)}, u32[]{:S(2)}) copy-start(bf16[128,1152]{1,0:T(8,128)(2,1)} %image_ref.3) | copy-start | bytes 884740
  0.6 1.0 copy-start.1
  1.8 8.8 %copy-start.4 = (f32[128]{0:T(128)S(1)}, f32[128]{0:T(128)}, u32[]{:S(2)}) copy-start(f32[128]{0:T(128)} %param.9) | copy-start | bytes 1540
  1.8 31.4 %collective-permute-start.3 = (bf16[128,1152]{1,0:T(8,128)(2,1)S(1)}, bf16[128,1152]{1,0:T(8,128)(2,1)S(1)}, u32[]{:S(2)}, u32[]{:S(2)}) collective-permute-start(bf16[128,1152]{1,0:T(8,128)(2,1)S(1)} %text.1.text_unit_ref), channel_id=1, source_target_pairs={{0,64},{64,0},{128,192},{192,128},{256,320},{320,256},{384,448},{4... | collective-permute-start | bytes 884744 | tf_op jit(solution)/shard_map/ppermute | solution.py:268
  10.8 30.6 %collective-permute-start.1 = (bf16[128,2432]{1,0:T(8,128)(2,1)S(1)}, bf16[128,2432]{1,0:T(8,128)(2,1)S(1)}, u32[]{:S(2)}, u32[]{:S(2)}) collective-permute-start(bf16[128,2432]{1,0:T(8,128)(2,1)S(1)} %get-tuple-element.24.own_ref), channel_id=1, source_target_pairs={{0,128},{64,192},{128,256},{192,320},{256,384},{320,448},{384,512}... | collective-permute-start | bytes 1867784 | tf_op jit(solution)/shard_map/ppermute | solution.py:268
  15.7 26.5 %collective-permute-start = (bf16[128,2432]{1,0:T(8,128)(2,1)S(1)}, bf16[128,2432]{1,0:T(8,128)(2,1)S(1)}, u32[]{:S(2)}, u32[]{:S(2)}) collective-permute-start(bf16[128,2432]{1,0:T(8,128)(2,1)S(1)} %get-tuple-element.24.own_ref), channel_id=1, source_target_pairs={{0,896},{64,960},{128,0},{192,64},{256,128},{320,192},{384,256},{4... | collective-permute-start | bytes 1867784 | tf_op jit(solution)/shard_map/ppermute | solution.py:268
  29.9 5.2 %copy-start.3 = (s32[16,128]{1,0:T(8,128)S(1)}, s32[16,128]{1,0:T(8,128)}, u32[]{:S(2)}) copy-start(s32[16,128]{1,0:T(8,128)} %label_ref.7) | copy-start | bytes 24580
  29.9 15.4 %collective-permute-start.2 = (bf16[128,1280]{1,0:T(8,128)(2,1)S(1)}, bf16[128,1280]{1,0:T(8,128)(2,1)S(1)}, u32[]{:S(2)}, u32[]{:S(2)}) collective-permute-start(bf16[128,1280]{1,0:T(8,128)(2,1)S(1)} %get-tuple-element.25), channel_id=1, source_target_pairs={{0,64},{64,0},{128,192},{192,128},{256,320},{320,256},{384,448},{4... | collective-permute-start | bytes 983048 | tf_op jit(solution)/shard_map/ppermute | solution.py:268
  33.2 14.5 %collective-permute-start.5 = (bf16[128,1152]{1,0:T(8,128)(2,1)S(1)}, bf16[128,1152]{1,0:T(8,128)(2,1)S(1)}, u32[]{:S(2)}, u32[]{:S(2)}) collective-permute-start(bf16[128,1152]{1,0:T(8,128)(2,1)S(1)} %collective-permute-done.3.cross_ref), channel_id=1, source_target_pairs={{0,128},{64,960},{128,256},{192,64},{256,384},{320,192},{384,512},... | collective-permute-start | bytes 884744 | tf_op jit(solution)/shard_map/ppermute | solution.py:268
  45.2 27.6 %collective-permute-start.4 = (bf16[128,1280]{1,0:T(8,128)(2,1)S(1)}, bf16[128,1280]{1,0:T(8,128)(2,1)S(1)}, u32[]{:S(2)}, u32[]{:S(2)}) collective-permute-start(bf16[128,1280]{1,0:T(8,128)(2,1)S(1)} %collective-permute-done.2.cross_ref), channel_id=1, source_target_pairs={{0,128},{64,960},{128,256},{192,64},{256,384},{320,192},{384,512},... | collective-permute-start | bytes 983048 | tf_op jit(solution)/shard_map/ppermute | solution.py:268
  72.8 27.8 %copy-start.2 = (bf16[128,1152]{1,0:T(8,128)(2,1)S(1)}, bf16[128,1152]{1,0:T(8,128)(2,1)}, u32[]{:S(2)}) copy-start(bf16[128,1152]{1,0:T(8,128)(2,1)} %text_ref.3) | copy-start | bytes 884740
  74.8 25.8 %collective-permute-start.6 = (bf16[256,1152]{1,0:T(8,128)(2,1)S(1)}, bf16[256,1152]{1,0:T(8,128)(2,1)S(1)}, u32[]{:S(2)}, u32[]{:S(2)}) collective-permute-start(bf16[256,1152]{1,0:T(8,128)(2,1)S(1)} %get-tuple-element.42), channel_id=1, source_target_pairs={{0,128},{64,192},{128,256},{192,320},{256,384},{320,448},{384,512}... | collective-permute-start | bytes 1769480 | tf_op jit(solution)/shard_map/ppermute | solution.py:268
  76.8 23.9 %collective-permute-start.7 = (bf16[256,1152]{1,0:T(8,128)(2,1)S(1)}, bf16[256,1152]{1,0:T(8,128)(2,1)S(1)}, u32[]{:S(2)}, u32[]{:S(2)}) collective-permute-start(bf16[256,1152]{1,0:T(8,128)(2,1)S(1)} %get-tuple-element.43), channel_id=1, source_target_pairs={{0,896},{64,960},{128,0},{192,64},{256,128},{320,192},{384,256},{4... | collective-permute-start | bytes 1769480 | tf_op jit(solution)/shard_map/ppermute | solution.py:268

commit v3 on v2

--- a/solution.py
+++ b/solution.py
@@ -97,24 +97,24 @@
     text_unit_ref[...] = normalize(text_ref[...])[0].astype(BF16)
 
 
-def image_kernel(image_ref, weight_ref, text_unit_ref, image_pack_ref, both_ref):
+def image_kernel(image_ref, weight_ref, text_unit_ref, both_ref):
     width = image_ref.shape[1]
-    u = normalize(image_ref[...])[0].astype(BF16)
     weight = as_column(weight_ref[...])
     high = weight.astype(BF16)
     rest = weight - high.astype(F32)
     middle = rest.astype(BF16)
     low = (rest - middle.astype(F32)).astype(BF16)
     lane = lax.broadcasted_iota(jnp.int32, weight.shape, 1)
-    coded = jnp.where(lane < 32, high.astype(F32), jnp.where(lane < 64, middle.astype(F32), low.astype(F32))).astype(BF16)
-    image_pack_ref[:, :width] = u
-    image_pack_ref[:, width:] = coded
-    both_ref[:, :width] = u
-    both_ref[:, width : width + 128] = coded
+    coded = jnp.where(lane < 32, high.astype(F32), jnp.where(lane < 64, middle.astype(F32), low.astype(F32)))
+    both_ref[:, :width] = normalize(image_ref[...])[0].astype(BF16)
+    both_ref[:, width : width + 128] = coded.astype(BF16)
     both_ref[:, width + 128 :] = text_unit_ref[...]
 
 
-def own_kernel(scal_ref, place_ref, label_ref, own_ref, cross_ref, image_total_ref, text_total_ref, sums_ref):
+def own_kernel(
+    scal_ref, place_ref, label_ref, own_ref, cross_ref,
+    image_total_ref, text_total_ref, cross_total_ref, sums_ref,
+):
     width = cross_ref.shape[1]
     scorer = Scorer(scal_ref, label_ref, place_ref)
     u, v = own_ref[:, :width], own_ref[:, width + 128 :]
@@ -126,13 +126,14 @@
     gc = scorer.grads(u, vc, w, col, scorer.label_row(scorer.side()), True)
     image_total_ref[...] = matmul(g0, v) + matmul(gc, vc)
     text_total_ref[...] = t_matmul(g0, u)
+    cross_total_ref[...] = t_matmul(gc, u)
     scorer.store_sums(sums_ref)
 
 
 def early_kernel(
     scal_ref, place_ref, label_ref, own_ref, after_ref, before_ref, cross_ref,
-    image_in_ref, text_in_ref, sums_in_ref,
-    image_total_ref, text_total_ref, far_ref, down_ref, up_ref, sums_ref,
+    image_in_ref, text_in_ref, cross_in_ref, sums_in_ref,
+    image_total_ref, text_total_ref, cross_total_ref, far_ref, down_ref, up_ref, sums_ref,
 ):
     width = cross_ref.shape[1]
     scorer = Scorer(scal_ref, label_ref, place_ref)
@@ -146,30 +147,33 @@
     row, row_a, row_b = scorer.label_row(0), scorer.label_row(2), scorer.label_row(-2)
     row_c = scorer.label_row(side)
     col, col_a, col_b = as_column(row.astype(F32)), as_column(row_a.astype(F32)), as_column(row_b.astype(F32))
+    ux, wx, col_x = jnp.where(even, ub, ua), jnp.where(even, wb, wa), jnp.where(even, col_b, col_a)
+    un, wn, col_n = jnp.where(even, ua, ub), jnp.where(even, wa, wb), jnp.where(even, col_a, col_b)
+    gx = scorer.grads(ux, vc, wx, col_x, row_c, True)
+    gn = scorer.grads(un, vc, wn, col_n, row_c, False)
+    cross_total_ref[...] = (cross_in_ref[...] + t_matmul(gx, ux) + t_matmul(gn, un)).astype(BF16)
+    far_ref[...] = matmul(gx, vc)
     ga = scorer.grads(u, va, w, col, row_a, True)
     gb = scorer.grads(u, vb, w, col, row_b, True)
     gfar = scorer.grads(ub, va, wb, col_b, row_a, True)
-    ux = jnp.where(even, ub, ua)
-    gx = scorer.grads(ux, vc, jnp.where(even, wb, wa), jnp.where(even, col_b, col_a), row_c, True)
     ta = scorer.grads(ua, v, wa, col_a, row, False)
     tb = scorer.grads(ub, v, wb, col_b, row, False)
     image_total_ref[...] = image_in_ref[...] + matmul(ga, va) + matmul(gb, vb)
     text_total_ref[...] = text_in_ref[...] + t_matmul(ta, ua) + t_matmul(tb, ub)
-    far_ref[...] = matmul(gx, vc)
     down_ref[...] = matmul(gfar, va)
-    up_ref[...] = t_matmul(gfar, ub)
+    up_ref[...] = t_matmul(gfar, ub).astype(BF16)
     scorer.store_sums(sums_ref, sums_in_ref)
 
 
-def relay_kernel(
-    scal_ref, place_ref, label_ref, own_ref, after_ref, before_ref, relay_ref, early_ref,
+def diagonal_kernel(
+    scal_ref, place_ref, label_ref, own_ref, after_ref, before_ref, diagonal_ref, early_ref,
     near_ref, far_ref, sums_ref,
 ):
-    width = relay_ref.shape[1]
+    width = diagonal_ref.shape[1]
     scorer = Scorer(scal_ref, label_ref, place_ref)
     side = scorer.side()
     even = side == 1
-    vr = relay_ref[...]
+    vr = diagonal_ref[...]
     row_r = scorer.label_row(-side)
     col = as_column(scorer.label_row(0).astype(F32))
     col_x = as_column(scorer.label_row(2 * side).astype(F32))
@@ -186,50 +190,35 @@
 
 
 def late_kernel(
-    scal_ref, place_ref, label_ref, own_ref, after_ref, before_ref, cross_ref, relay_ref, relay_v_ref,
-    near_ref, far_g_ref, far_ref, down_in_ref, up_in_ref, image_in_ref, text_in_ref, got_ref,
-    up_ref, down_ref, image_total_ref, text_total_ref, sums_ref,
-):
-    width = relay_v_ref.shape[1]
-    rows = relay_v_ref.shape[0]
-    scorer = Scorer(scal_ref, label_ref, place_ref)
-    side = scorer.side()
-    even = side == 1
-    v = own_ref[:, width + 128 :]
-    va, vb = after_ref[:, width + 128 :], before_ref[:, width + 128 :]
-    uc, ur = cross_ref[:, :width], relay_ref[:, :width]
-    wc, wr = weight_of(cross_ref, width), weight_of(relay_ref, width)
-    col_c = as_column(scorer.label_row(side).astype(F32))
-    col_r = as_column(scorer.label_row(-side).astype(F32))
-    row, row_a, row_b = scorer.label_row(0), scorer.label_row(2), scorer.label_row(-2)
-    gcx = scorer.grads(uc, jnp.where(even, vb, va), wc, col_c, jnp.where(even, row_b, row_a), False)
-    grx = scorer.grads(ur, jnp.where(even, va, vb), wr, col_r, jnp.where(even, row_a, row_b), False)
-    far_text_c = t_matmul(gcx, uc)
-    far_text_r = t_matmul(grx, ur)
-    far_image_c = far_ref[...]
-    far_image_r = matmul(far_g_ref[...], relay_v_ref[...])
-    up_ref[:rows, :] = jnp.where(even, far_image_r, far_image_c).astype(BF16)
-    up_ref[rows:, :] = (up_in_ref[...] + jnp.where(even, far_text_r, far_text_c)).astype(BF16)
-    down_ref[:rows, :] = (down_in_ref[...] + jnp.where(even, far_image_c, far_image_r)).astype(BF16)
-    down_ref[rows:, :] = jnp.where(even, far_text_c, far_text_r).astype(BF16)
-    gc = scorer.grads(uc, v, wc, col_c, row, False)
-    gr = scorer.grads(ur, v, wr, col_r, row, False)
-    image_total_ref[...] = image_in_ref[...] + matmul(near_ref[...], relay_v_ref[...])
-    text_total_ref[...] = text_in_ref[...] + t_matmul(gc, uc) + t_matmul(gr, ur)
+    place_ref, after_ref, before_ref, diagonal_ref, near_g_ref, far_g_ref, far_ref, down_in_ref, up_in_ref, image_in_ref,
+    text_in_ref, cross_ref, got_ref,
+    up_ref, down_ref, back_ref, image_total_ref, text_total_ref, sums_ref,
+):
+    rows, width = diagonal_ref.shape
+    even = lax.rem(place_ref[0], 2) == 0
+    vr = diagonal_ref[...]
+    g = far_g_ref[...]
+    back_ref[...] = t_matmul(g, jnp.where(even, after_ref[:, :width], before_ref[:, :width])).astype(BF16)
+    far_cross = far_ref[...]
+    far_diagonal = matmul(g, vr)
+    up_ref[:rows, :] = jnp.where(even, far_diagonal, far_cross).astype(BF16)
+    up_ref[rows:, :] = up_in_ref[...]
+    down_ref[...] = (down_in_ref[...] + jnp.where(even, far_cross, far_diagonal)).astype(BF16)
+    image_total_ref[...] = image_in_ref[...] + matmul(near_g_ref[...], vr)
+    text_total_ref[...] = text_in_ref[...] + cross_ref[...].astype(F32)
     sums_ref[...] = jnp.sum(got_ref[...], axis=0, keepdims=True)
 
 
 def final_kernel(
-    count, scal_ref, image_ref, text_ref, image_total_ref, text_total_ref, up_ref, down_ref, got_ref,
+    count, scal_ref, image_ref, text_ref, image_total_ref, text_total_ref,
+    up_ref, down_ref, back_ref, got_ref,
     image_grad_ref, text_grad_ref, stats_ref,
 ):
     rows, width = image_ref.shape
     temper = jnp.exp(jnp.full((1, 128), scal_ref[0], F32))[:, :1]
-    for raw_ref, total_ref, out_ref, at in (
-        (image_ref, image_total_ref, image_grad_ref, 0),
-        (text_ref, text_total_ref, text_grad_ref, rows),
-    ):
-        total = total_ref[...] + up_ref[at : at + rows, :].astype(F32) + down_ref[at : at + rows, :].astype(F32)
+    image_total = image_total_ref[...] + up_ref[:rows, :].astype(F32) + down_ref[...].astype(F32)
+    text_total = text_total_ref[...] + up_ref[rows:, :].astype(F32) + back_ref[...].astype(F32)
+    for raw_ref, total, out_ref in ((image_ref, image_total, image_grad_ref), (text_ref, text_total, text_grad_ref)):
         unit, scale = normalize(raw_ref[...])
         out_ref[...] = norm_back(unit, scale, temper * total).astype(BF16)
     got = jnp.sum(got_ref[...], axis=0, keepdims=True) / count
@@ -270,8 +259,8 @@
     def across(value):
         return passed(value, lambda p: 1 - 2 * (p % 2))
 
-    def relayed(value):
-        return passed(value, lambda p: 2 - 4 * (p % 2))
+    def diagonally(value):
+        return passed(value, lambda p: 2 * (p % 2) - 1)
 
     def upward(value):
         return passed(value, lambda p: 2)
@@ -279,54 +268,53 @@
     def downward(value):
         return passed(value, lambda p: -2)
 
-    block = shape(rows, width, F32)
-    text_unit = call(text_kernel, [VMEM], shape(rows, width, BF16), "text", 10 * dot)(texts)
+    block, half = shape(rows, width, F32), shape(rows, width, BF16)
+    text_unit = call(text_kernel, [VMEM], half, "text", 10 * dot)(texts)
     cross_v = across(text_unit)
-    image_pack, both = call(
-        image_kernel,
-        [VMEM] * 3,
-        (shape(rows, width + 128, BF16), shape(rows, 2 * width + 128, BF16)),
-        "image",
-        10 * dot,
-    )(images, weights.reshape(1, rows), text_unit)
+    diagonal_v = diagonally(text_unit)
+    both = call(image_kernel, [VMEM] * 3, shape(rows, 2 * width + 128, BF16), "image", 10 * dot)(
+        images, weights.reshape(1, rows), text_unit
+    )
     after = downward(both)
     before = upward(both)
-    cross_u = across(image_pack)
-    relay_v = relayed(cross_v)
-    image_total, text_total, sums = call(
-        own_kernel, head + [VMEM] * 2, (block,) * 2 + (shape(8, 128, F32),), "own", 150 * dot
+    image_total, text_total, cross_total, sums = call(
+        own_kernel, head + [VMEM] * 2, (block,) * 3 + (shape(8, 128, F32),), "own", 200 * dot
     )(scal, place, labels, both, cross_v)
-    image_total, text_total, far, far_down, far_up, sums = call(
-        early_kernel, head + [VMEM] * 7, (block,) * 5 + (shape(8, 128, F32),), "early", 20 * dot
-    )(scal, place, labels, both, after, before, cross_v, image_total, text_total, sums)
-    cross_u, sums = lax.optimization_barrier((cross_u, sums))
-    relay_u = relayed(cross_u)
+    image_total, text_total, cross_total, far, far_down, far_up, sums = call(
+        early_kernel,
+        head + [VMEM] * 8,
+        (block, block, half, block, block, half, shape(8, 128, F32)),
+        "early",
+        20 * dot,
+    )(scal, place, labels, both, after, before, cross_v, image_total, text_total, cross_total, sums)
+    from_cross = across(cross_total)
     near_g, far_g, sums = call(
-        relay_kernel, head + [VMEM] * 5, (shape(rows, rows, BF16),) * 2 + (shape(1, 128, F32),), "relay", 10 * dot
-    )(scal, place, labels, both, after, before, relay_v, sums)
+        diagonal_kernel, head + [VMEM] * 5, (shape(rows, rows, BF16),) * 2 + (shape(1, 128, F32),), "diagonal", 10 * dot
+    )(scal, place, labels, both, after, before, diagonal_v, sums)
     got = exchanged(sums, "group")
-    to_up, to_down, image_total, text_total, sums = call(
+    to_up, to_down, to_back, image_total, text_total, sums = call(
         late_kernel,
-        head + [VMEM] * 14,
-        (shape(2 * rows, width, BF16),) * 2 + (block,) * 2 + (shape(1, 128, F32),),
+        [SMEM] + [VMEM] * 12,
+        (shape(2 * rows, width, BF16), half, half, block, block, shape(1, 128, F32)),
         "late",
         20 * dot,
     )(
-        scal, place, labels, both, after, before, cross_u, relay_u, relay_v,
-        near_g, far_g, far, far_down, far_up, image_total, text_total, got,
+        place, after, before, diagonal_v, near_g, far_g, far, far_down, far_up, image_total,
+        text_total, from_cross, got,
     )
+    from_diagonal = diagonally(to_back)
     from_below = upward(to_up)
     from_above = downward(to_down)
     got = exchanged(sums, "blk")
     count = float(cycle * groups * rows) * float(rows) * 8.0
     image_grad, text_grad, stats = call(
         functools.partial(final_kernel, count),
-        [SMEM] + [VMEM] * 7,
-        (shape(rows, width, BF16),) * 2 + (jax.ShapeDtypeStruct((3,), F32),),
+        [SMEM] + [VMEM] * 8,
+        (half, half, jax.ShapeDtypeStruct((3,), F32)),
         "final",
         10 * dot,
         (VMEM, VMEM, SMEM),
-    )(scal, images, texts, image_total, text_total, from_below, from_above, got)
+    )(scal, images, texts, image_total, text_total, from_below, from_above, from_diagonal, got)
     return image_grad, text_grad, stats
 
 

time: 103 us -> 114 us (1.11)
  waiting for transfers between devices: 7.37 us -> 15.2 us
  starting transfers between devices: 41.8 us -> 47.8 us
  blocking collectives: 41.6 us -> 39.3 us
  Pallas kernels: 8.56 us -> 7.4 us
    ppermute x8, waiting for transfers between devices: 7.37 us -> 15.2 us  [passed(): lax.ppermute(value, 'blk', [(p, (p + step_of(p)) % cycle) for p in range(...]
    ppermute x8, starting transfers between devices: 41.8 us -> 47.8 us  [passed(): lax.ppermute(value, 'blk', [(p, (p + step_of(p)) % cycle) for p in range(...]
    all_to_all x2, blocking collectives: 41.6 us -> 39.3 us  [exchanged(): return lax.all_to_all(sent, axis, 0, 0).reshape(count, 128)]
    pallas_call x7, Pallas kernels: 8.56 us -> 7.4 us  [the longest x1 2.28 us: per_device(): call(early_kernel, head + [VMEM] * 8, (block, block, half, block, block,...]
  transfers between devices with their start and end apart: 8 -> 8, of which waited for: 4 -> 1; matrix products, arithmetic and copies ran while one was open for 0% -> 0% of each run, Pallas kernels for 4% -> 4%
where the time goes in v3:
time: 114 us; the launch traced here: 113 us
  starting transfers between devices  47.8 us (42%)
  blocking collectives  39.3 us (34%)
  waiting for transfers between devices  15.2 us (13%)
  Pallas kernels  7.4 us (6%)
  between operations  2.11 us (2%)
    ppermute x8, starting transfers between devices, passed(): lax.ppermute(value, 'blk', [(p, (p + step_of(p)) % cycle) for p in range(...  47.8 us
    all_to_all x2, blocking collectives, exchanged(): return lax.all_to_all(sent, axis, 0, 0).reshape(count, 128)  39.3 us
    ppermute x8, waiting for transfers between devices, passed(): lax.ppermute(value, 'blk', [(p, (p + step_of(p)) % cycle) for p in range(...  15.2 us
  transfers between devices with their start and end apart: 8, of which 1 were waited for; matrix products, arithmetic and copies ran while one was open for 0% of the time, Pallas kernels for 4%

profile of v3, /device:TPU:1, one launch (start us, length us, event | category | flops | bytes accessed | tf_op | source)
XLA Modules:
  0.0 112.9 jit_solution(14190097296980263141)
XLA Ops:
  0.6 0.0 copy-start.1
  0.7 1.0 copy-done.1
  1.6 0.1 text.1.text_unit_ref
  1.8 0.0 copy-start.4
  1.8 8.7 %collective-permute-start.3 = (bf16[128,1152]{1,0:T(8,128)(2,1)S(1)}, bf16[128,1152]{1,0:T(8,128)(2,1)S(1)}, u32[]{:S(2)}, u32[]{:S(2)}) collective-permute-start(bf16[128,1152]{1,0:T(8,128)(2,1)S(1)} %text.1.text_unit_ref), channel_id=1, source_target_pairs={{0,64},{64,0},{128,192},{192,128},{256,320},{320,256},{384,448},{4... | collective-permute-start | bytes 884744 | tf_op jit(solution)/shard_map/ppermute | solution.py:257
  10.6 16.9 %collective-permute-start.2 = (bf16[128,1152]{1,0:T(8,128)(2,1)S(1)}, bf16[128,1152]{1,0:T(8,128)(2,1)S(1)}, u32[]{:S(2)}, u32[]{:S(2)}) collective-permute-start(bf16[128,1152]{1,0:T(8,128)(2,1)S(1)} %text.1.text_unit_ref), channel_id=1, source_target_pairs={{0,960},{64,128},{128,64},{192,256},{256,192},{320,384},{384,320},... | collective-permute-start | bytes 884744 | tf_op jit(solution)/shard_map/ppermute | solution.py:257
  27.5 0.2 image.1.own_ref
  27.7 0.0 copy-start.3
  27.7 1.9 %collective-permute-start.1 = (bf16[128,2432]{1,0:T(8,128)(2,1)S(1)}, bf16[128,2432]{1,0:T(8,128)(2,1)S(1)}, u32[]{:S(2)}, u32[]{:S(2)}) collective-permute-start(bf16[128,2432]{1,0:T(8,128)(2,1)S(1)} %image.1.own_ref), channel_id=1, source_target_pairs={{0,128},{64,192},{128,256},{192,320},{256,384},{320,448},{384,512}... | collective-permute-start | bytes 1867784 | tf_op jit(solution)/shard_map/ppermute | solution.py:257
  29.6 4.6 %collective-permute-start = (bf16[128,2432]{1,0:T(8,128)(2,1)S(1)}, bf16[128,2432]{1,0:T(8,128)(2,1)S(1)}, u32[]{:S(2)}, u32[]{:S(2)}) collective-permute-start(bf16[128,2432]{1,0:T(8,128)(2,1)S(1)} %image.1.own_ref), channel_id=1, source_target_pairs={{0,896},{64,960},{128,0},{192,64},{256,128},{320,192},{384,256},{4... | collective-permute-start | bytes 1867784 | tf_op jit(solution)/shard_map/ppermute | solution.py:257
  35.5 0.1 pad_maximum_fusion.scal_ref
  35.6 0.0 collective-permute-done.3.cross_ref
  35.6 1.4 %own.1 = (f32[128,1152]{1,0:T(8,128)S(1)}, f32[128,1152]{1,0:T(8,128)S(1)}, f32[128,1152]{1,0:T(8,128)S(1)}, f32[8,128]{1,0:T(8,128)S(1)}) custom-call(f32[2]{0:T(128)S(1)} %pad_maximum_fusion.scal_ref, s32[1]{0:T(128)} %bitcast.place_ref, s32[16,128]{1,0:T(8,128)S(1)} %copy-done.3, bf16[128,2432]{1,0:T(8,128)(2,1)S(1)} %image.1.own_ref, ...), custom_call_target="tpu_custom_call" | custom-call | flops 7549747200 | tf_op jit(solution)/shard_map/own/pallas_call | solution.py:280
  36.9 15.2 %collective-permute-done.1.before_ref = bf16[128,2432]{1,0:T(8,128)(2,1)S(1)} collective-permute-done((bf16[128,2432]{1,0:T(8,128)(2,1)S(1)}, bf16[128,2432]{1,0:T(8,128)(2,1)S(1)}, u32[]{:S(2)}, u32[]{:S(2)}) %collective-permute-start.1) | collective-permute-done | bytes 622624 | tf_op jit(solution)/shard_map/ppermute | solution.py:257
  52.2 2.3 %early.1 = (f32[128,1152]{1,0:T(8,128)S(1)}, f32[128,1152]{1,0:T(8,128)S(1)}, bf16[128,1152]{1,0:T(8,128)(2,1)S(1)}, f32[128,1152]{1,0:T(8,128)S(1)}, f32[128,11...) custom-call(f32[2]{0:T(128)S(1)} %pad_maximum_fusion.scal_ref, s32[1]{0:T(128)} %bitcast.place_ref, ...), custom_call_target="tpu_custom_call" | custom-call | flops 754974720 | tf_op jit(solution)/shard_map/early/pallas_call | solution.py:283
  54.4 1.9 %collective-permute-start.4 = (bf16[128,1152]{1,0:T(8,128)(2,1)S(1)}, bf16[128,1152]{1,0:T(8,128)(2,1)S(1)}, u32[]{:S(2)}, u32[]{:S(2)}) collective-permute-start(bf16[128,1152]{1,0:T(8,128)(2,1)S(1)} %get-tuple-element.35), channel_id=1, source_target_pairs={{0,64},{64,0},{128,192},{192,128},{256,320},{320,256},{384,448},{4... | collective-permute-start | bytes 884744 | tf_op jit(solution)/shard_map/ppermute | solution.py:257
  56.4 1.0 diagonal.1
  57.4 20.8 %all_to_all.10 = f32[64,1,128]{2,1,0:T(1,128)S(1)} all-to-all(f32[64,1,128]{2,1,0:T(1,128)S(1)} %broadcast_in_dim.15), channel_id=1, replica_groups=mesh['blk'=16,'group'=64] {'group'}, dimensions={0} | all-to-all | bytes 65536 | tf_op jit(solution)/shard_map/all_to_all | solution.py:244
  78.2 0.5 late.1
  78.7 2.7 %collective-permute-start.5 = (bf16[256,1152]{1,0:T(8,128)(2,1)S(1)}, bf16[256,1152]{1,0:T(8,128)(2,1)S(1)}, u32[]{:S(2)}, u32[]{:S(2)}) collective-permute-start(bf16[256,1152]{1,0:T(8,128)(2,1)S(1)} %get-tuple-element.39), channel_id=1, source_target_pairs={{0,128},{64,192},{128,256},{192,320},{256,384},{320,448},{384,512}... | collective-permute-start | bytes 1769480 | tf_op jit(solution)/shard_map/ppermute | solution.py:257
  81.5 4.6 %collective-permute-start.6 = (bf16[128,1152]{1,0:T(8,128)(2,1)S(1)}, bf16[128,1152]{1,0:T(8,128)(2,1)S(1)}, u32[]{:S(2)}, u32[]{:S(2)}) collective-permute-start(bf16[128,1152]{1,0:T(8,128)(2,1)S(1)} %get-tuple-element.40), channel_id=1, source_target_pairs={{0,896},{64,960},{128,0},{192,64},{256,128},{320,192},{384,256},{4... | collective-permute-start | bytes 884744 | tf_op jit(solution)/shard_map/ppermute | solution.py:257
  86.1 6.4 %collective-permute-start.7 = (bf16[128,1152]{1,0:T(8,128)(2,1)S(1)}, bf16[128,1152]{1,0:T(8,128)(2,1)S(1)}, u32[]{:S(2)}, u32[]{:S(2)}) collective-permute-start(bf16[128,1152]{1,0:T(8,128)(2,1)S(1)} %get-tuple-element.41), channel_id=1, source_target_pairs={{0,960},{64,128},{128,64},{192,256},{256,192},{320,384},{384,320},... | collective-permute-start | bytes 884744 | tf_op jit(solution)/shard_map/ppermute | solution.py:257
  92.5 18.5 %all_to_all.11 = f32[16,1,128]{2,1,0:T(1,128)S(1)} all-to-all(f32[16,1,128]{2,1,0:T(1,128)S(1)} %broadcast_in_dim.17), channel_id=1, replica_groups=mesh['blk'=16,'group'=64] {'blk'}, dimensions={0} | all-to-all | bytes 16384 | tf_op jit(solution)/shard_map/all_to_all | solution.py:244
  111.0 1.9 %final.1 = (bf16[128,1152]{1,0:T(8,128)(2,1)}, bf16[128,1152]{1,0:T(8,128)(2,1)}, f32[3]{0:T(128)}) custom-call(f32[2]{0:T(128)S(1)} %pad_maximum_fusion.scal_ref, bf16[128,1152]{1,0:T(8,128)(2,1)S(1)} %copy-done, bf16[128,1152]{1,0:T(8,128)(2,1)S(1)} %copy-done.2, f32[128,1152]{1,0:T(8,128)S(1)} %get-tuple-element.37.image_total_ref, ...), custom_call_target="tpu_custom_call" | custom-call | flops 377487360 | tf_op jit(solution)/shard_map/final/pallas_call | solution.py:310
  (14 shorter events, 0.1 us)
Async XLA Ops:
  0.6 26.8 %copy-start = (bf16[128,1152]{1,0:T(8,128)(2,1)S(1)}, bf16[128,1152]{1,0:T(8,128)(2,1)}, u32[]{:S(2)}) copy-start(bf16[128,1152]{1,0:T(8,128)(2,1)} %image_ref.3) | copy-start | bytes 884740
  0.6 1.0 copy-start.1
  1.8 25.7 %copy-start.4 = (f32[128]{0:T(128)S(1)}, f32[128]{0:T(128)}, u32[]{:S(2)}) copy-start(f32[128]{0:T(128)} %param.9) | copy-start | bytes 1540
  1.8 33.8 %collective-permute-start.3 = (bf16[128,1152]{1,0:T(8,128)(2,1)S(1)}, bf16[128,1152]{1,0:T(8,128)(2,1)S(1)}, u32[]{:S(2)}, u32[]{:S(2)}) collective-permute-start(bf16[128,1152]{1,0:T(8,128)(2,1)S(1)} %text.1.text_unit_ref), channel_id=1, source_target_pairs={{0,64},{64,0},{128,192},{192,128},{256,320},{320,256},{384,448},{4... | collective-permute-start | bytes 884744 | tf_op jit(solution)/shard_map/ppermute | solution.py:257
  10.6 45.8 %collective-permute-start.2 = (bf16[128,1152]{1,0:T(8,128)(2,1)S(1)}, bf16[128,1152]{1,0:T(8,128)(2,1)S(1)}, u32[]{:S(2)}, u32[]{:S(2)}) collective-permute-start(bf16[128,1152]{1,0:T(8,128)(2,1)S(1)} %text.1.text_unit_ref), channel_id=1, source_target_pairs={{0,960},{64,128},{128,64},{192,256},{256,192},{320,384},{384,320},... | collective-permute-start | bytes 884744 | tf_op jit(solution)/shard_map/ppermute | solution.py:257
  27.7 7.9 %copy-start.3 = (s32[16,128]{1,0:T(8,128)S(1)}, s32[16,128]{1,0:T(8,128)}, u32[]{:S(2)}) copy-start(s32[16,128]{1,0:T(8,128)} %label_ref.5) | copy-start | bytes 24580
  27.7 24.5 %collective-permute-start.1 = (bf16[128,2432]{1,0:T(8,128)(2,1)S(1)}, bf16[128,2432]{1,0:T(8,128)(2,1)S(1)}, u32[]{:S(2)}, u32[]{:S(2)}) collective-permute-start(bf16[128,2432]{1,0:T(8,128)(2,1)S(1)} %image.1.own_ref), channel_id=1, source_target_pairs={{0,128},{64,192},{128,256},{192,320},{256,384},{320,448},{384,512}... | collective-permute-start | bytes 1867784 | tf_op jit(solution)/shard_map/ppermute | solution.py:257
  29.6 22.6 %collective-permute-start = (bf16[128,2432]{1,0:T(8,128)(2,1)S(1)}, bf16[128,2432]{1,0:T(8,128)(2,1)S(1)}, u32[]{:S(2)}, u32[]{:S(2)}) collective-permute-start(bf16[128,2432]{1,0:T(8,128)(2,1)S(1)} %image.1.own_ref), channel_id=1, source_target_pairs={{0,896},{64,960},{128,0},{192,64},{256,128},{320,192},{384,256},{4... | collective-permute-start | bytes 1867784 | tf_op jit(solution)/shard_map/ppermute | solution.py:257
  54.4 23.8 %collective-permute-start.4 = (bf16[128,1152]{1,0:T(8,128)(2,1)S(1)}, bf16[128,1152]{1,0:T(8,128)(2,1)S(1)}, u32[]{:S(2)}, u32[]{:S(2)}) collective-permute-start(bf16[128,1152]{1,0:T(8,128)(2,1)S(1)} %get-tuple-element.35), channel_id=1, source_target_pairs={{0,64},{64,0},{128,192},{192,128},{256,320},{320,256},{384,448},{4... | collective-permute-start | bytes 884744 | tf_op jit(solution)/shard_map/ppermute | solution.py:257
  78.2 32.8 %copy-start.2 = (bf16[128,1152]{1,0:T(8,128)(2,1)S(1)}, bf16[128,1152]{1,0:T(8,128)(2,1)}, u32[]{:S(2)}) copy-start(bf16[128,1152]{1,0:T(8,128)(2,1)} %text_ref.3) | copy-start | bytes 884740
  78.7 32.3 %collective-permute-start.5 = (bf16[256,1152]{1,0:T(8,128)(2,1)S(1)}, bf16[256,1152]{1,0:T(8,128)(2,1)S(1)}, u32[]{:S(2)}, u32[]{:S(2)}) collective-permute-start(bf16[256,1152]{1,0:T(8,128)(2,1)S(1)} %get-tuple-element.39), channel_id=1, source_target_pairs={{0,128},{64,192},{128,256},{192,320},{256,384},{320,448},{384,512}... | collective-permute-start | bytes 1769480 | tf_op jit(solution)/shard_map/ppermute | solution.py:257
  81.5 29.5 %collective-permute-start.6 = (bf16[128,1152]{1,0:T(8,128)(2,1)S(1)}, bf16[128,1152]{1,0:T(8,128)(2,1)S(1)}, u32[]{:S(2)}, u32[]{:S(2)}) collective-permute-start(bf16[128,1152]{1,0:T(8,128)(2,1)S(1)} %get-tuple-element.40), channel_id=1, source_target_pairs={{0,896},{64,960},{128,0},{192,64},{256,128},{320,192},{384,256},{4... | collective-permute-start | bytes 884744 | tf_op jit(solution)/shard_map/ppermute | solution.py:257
  86.1 24.9 %collective-permute-start.7 = (bf16[128,1152]{1,0:T(8,128)(2,1)S(1)}, bf16[128,1152]{1,0:T(8,128)(2,1)S(1)}, u32[]{:S(2)}, u32[]{:S(2)}) collective-permute-start(bf16[128,1152]{1,0:T(8,128)(2,1)S(1)} %get-tuple-element.41), channel_id=1, source_target_pairs={{0,960},{64,128},{128,64},{192,256},{256,192},{320,384},{384,320},... | collective-permute-start | bytes 884744 | tf_op jit(solution)/shard_map/ppermute | solution.py:257

commit v4 on v3

--- a/solution.py
+++ b/solution.py
@@ -133,9 +133,9 @@
 def early_kernel(
     scal_ref, place_ref, label_ref, own_ref, after_ref, before_ref, cross_ref,
     image_in_ref, text_in_ref, cross_in_ref, sums_in_ref,
-    image_total_ref, text_total_ref, cross_total_ref, far_ref, down_ref, up_ref, sums_ref,
-):
-    width = cross_ref.shape[1]
+    image_total_ref, text_total_ref, cross_total_ref, near_ref, image_far_ref, text_far_ref, sums_ref,
+):
+    rows, width = cross_ref.shape
     scorer = Scorer(scal_ref, label_ref, place_ref)
     side = scorer.side()
     even = side == 1
@@ -152,7 +152,6 @@
     gx = scorer.grads(ux, vc, wx, col_x, row_c, True)
     gn = scorer.grads(un, vc, wn, col_n, row_c, False)
     cross_total_ref[...] = (cross_in_ref[...] + t_matmul(gx, ux) + t_matmul(gn, un)).astype(BF16)
-    far_ref[...] = matmul(gx, vc)
     ga = scorer.grads(u, va, w, col, row_a, True)
     gb = scorer.grads(u, vb, w, col, row_b, True)
     gfar = scorer.grads(ub, va, wb, col_b, row_a, True)
@@ -160,64 +159,60 @@
     tb = scorer.grads(ub, v, wb, col_b, row, False)
     image_total_ref[...] = image_in_ref[...] + matmul(ga, va) + matmul(gb, vb)
     text_total_ref[...] = text_in_ref[...] + t_matmul(ta, ua) + t_matmul(tb, ub)
-    down_ref[...] = matmul(gfar, va)
-    up_ref[...] = t_matmul(gfar, ub).astype(BF16)
+    image_far, text_far = matmul(gfar, va), t_matmul(gfar, ub)
+    near_ref[:rows, :] = (matmul(gx, vc) + jnp.where(even, image_far, 0.0)).astype(BF16)
+    near_ref[rows:, :] = jnp.where(even, 0.0, text_far).astype(BF16)
+    image_far_ref[...] = jnp.where(even, 0.0, image_far)
+    text_far_ref[...] = jnp.where(even, text_far, 0.0).astype(BF16)
     scorer.store_sums(sums_ref, sums_in_ref)
 
 
-def diagonal_kernel(
-    scal_ref, place_ref, label_ref, own_ref, after_ref, before_ref, diagonal_ref, early_ref,
-    near_ref, far_ref, sums_ref,
-):
-    width = diagonal_ref.shape[1]
+def relay_kernel(
+    scal_ref, place_ref, label_ref, own_ref, after_ref, before_ref, relay_ref, early_ref,
+    image_in_ref, image_far_ref, text_far_ref,
+    image_total_ref, far_ref, diagonal_ref, sums_ref,
+):
+    rows, width = relay_ref.shape
     scorer = Scorer(scal_ref, label_ref, place_ref)
     side = scorer.side()
     even = side == 1
-    vr = diagonal_ref[...]
+    vr = relay_ref[...]
     row_r = scorer.label_row(-side)
     col = as_column(scorer.label_row(0).astype(F32))
     col_x = as_column(scorer.label_row(2 * side).astype(F32))
-    near_ref[...] = scorer.grads(own_ref[:, :width], vr, weight_of(own_ref, width), col, row_r, True)
     ux = jnp.where(even, after_ref[:, :width], before_ref[:, :width])
     wx = jnp.where(even, weight_of(after_ref, width), weight_of(before_ref, width))
-    far_ref[...] = scorer.grads(ux, vr, wx, col_x, row_r, True)
+    gr = scorer.grads(own_ref[:, :width], vr, weight_of(own_ref, width), col, row_r, True)
+    gx = scorer.grads(ux, vr, wx, col_x, row_r, True)
     lane = lax.broadcasted_iota(jnp.int32, (1, 128), 1)
     message = jnp.zeros((1, 128), F32)
     for at in range(3):
         total = jnp.sum(scorer.sums[at], axis=0, keepdims=True) + early_ref[at : at + 1, :]
         message = jnp.where(lane == at, jnp.sum(total, axis=1, keepdims=True), message)
     sums_ref[...] = message
-
-
-def late_kernel(
-    place_ref, after_ref, before_ref, diagonal_ref, near_g_ref, far_g_ref, far_ref, down_in_ref, up_in_ref, image_in_ref,
-    text_in_ref, cross_ref, got_ref,
-    up_ref, down_ref, back_ref, image_total_ref, text_total_ref, sums_ref,
-):
-    rows, width = diagonal_ref.shape
-    even = lax.rem(place_ref[0], 2) == 0
-    vr = diagonal_ref[...]
-    g = far_g_ref[...]
-    back_ref[...] = t_matmul(g, jnp.where(even, after_ref[:, :width], before_ref[:, :width])).astype(BF16)
-    far_cross = far_ref[...]
-    far_diagonal = matmul(g, vr)
-    up_ref[:rows, :] = jnp.where(even, far_diagonal, far_cross).astype(BF16)
-    up_ref[rows:, :] = up_in_ref[...]
-    down_ref[...] = (down_in_ref[...] + jnp.where(even, far_cross, far_diagonal)).astype(BF16)
-    image_total_ref[...] = image_in_ref[...] + matmul(near_g_ref[...], vr)
-    text_total_ref[...] = text_in_ref[...] + cross_ref[...].astype(F32)
+    diagonal_ref[...] = t_matmul(gx, ux).astype(BF16)
+    far_ref[:rows, :] = (image_far_ref[...] + matmul(gx, vr)).astype(BF16)
+    far_ref[rows:, :] = text_far_ref[...]
+    image_total_ref[...] = image_in_ref[...] + matmul(gr, vr)
+
+
+def middle_kernel(
+    image_in_ref, text_in_ref, near_ref, cross_ref, got_ref, image_total_ref, text_total_ref, sums_ref
+):
+    rows = cross_ref.shape[0]
+    image_total_ref[...] = image_in_ref[...] + near_ref[:rows, :].astype(F32)
+    text_total_ref[...] = text_in_ref[...] + near_ref[rows:, :].astype(F32) + cross_ref[...].astype(F32)
     sums_ref[...] = jnp.sum(got_ref[...], axis=0, keepdims=True)
 
 
 def final_kernel(
-    count, scal_ref, image_ref, text_ref, image_total_ref, text_total_ref,
-    up_ref, down_ref, back_ref, got_ref,
+    count, scal_ref, image_ref, text_ref, image_total_ref, text_total_ref, far_ref, diagonal_ref, got_ref,
     image_grad_ref, text_grad_ref, stats_ref,
 ):
     rows, width = image_ref.shape
     temper = jnp.exp(jnp.full((1, 128), scal_ref[0], F32))[:, :1]
-    image_total = image_total_ref[...] + up_ref[:rows, :].astype(F32) + down_ref[...].astype(F32)
-    text_total = text_total_ref[...] + up_ref[rows:, :].astype(F32) + back_ref[...].astype(F32)
+    image_total = image_total_ref[...] + far_ref[:rows, :].astype(F32)
+    text_total = text_total_ref[...] + far_ref[rows:, :].astype(F32) + diagonal_ref[...].astype(F32)
     for raw_ref, total, out_ref in ((image_ref, image_total, image_grad_ref), (text_ref, text_total, text_grad_ref)):
         unit, scale = normalize(raw_ref[...])
         out_ref[...] = norm_back(unit, scale, temper * total).astype(BF16)
@@ -262,6 +257,12 @@
     def diagonally(value):
         return passed(value, lambda p: 2 * (p % 2) - 1)
 
+    def far_side(value):
+        return passed(value, lambda p: 2 - 4 * (p % 2))
+
+    def near_side(value):
+        return passed(value, lambda p: 4 * (p % 2) - 2)
+
     def upward(value):
         return passed(value, lambda p: 2)
 
@@ -271,50 +272,44 @@
     block, half = shape(rows, width, F32), shape(rows, width, BF16)
     text_unit = call(text_kernel, [VMEM], half, "text", 10 * dot)(texts)
     cross_v = across(text_unit)
-    diagonal_v = diagonally(text_unit)
     both = call(image_kernel, [VMEM] * 3, shape(rows, 2 * width + 128, BF16), "image", 10 * dot)(
         images, weights.reshape(1, rows), text_unit
     )
     after = downward(both)
     before = upward(both)
+    relay_v = far_side(cross_v)
     image_total, text_total, cross_total, sums = call(
         own_kernel, head + [VMEM] * 2, (block,) * 3 + (shape(8, 128, F32),), "own", 200 * dot
     )(scal, place, labels, both, cross_v)
-    image_total, text_total, cross_total, far, far_down, far_up, sums = call(
+    pair = shape(2 * rows, width, BF16)
+    image_total, text_total, cross_total, near, image_far, text_far, sums = call(
         early_kernel,
         head + [VMEM] * 8,
-        (block, block, half, block, block, half, shape(8, 128, F32)),
+        (block, block, half, pair, block, half, shape(8, 128, F32)),
         "early",
         20 * dot,
     )(scal, place, labels, both, after, before, cross_v, image_total, text_total, cross_total, sums)
     from_cross = across(cross_total)
-    near_g, far_g, sums = call(
-        diagonal_kernel, head + [VMEM] * 5, (shape(rows, rows, BF16),) * 2 + (shape(1, 128, F32),), "diagonal", 10 * dot
-    )(scal, place, labels, both, after, before, diagonal_v, sums)
+    from_near = near_side(near)
+    image_total, far, diagonal, sums = call(
+        relay_kernel, head + [VMEM] * 8, (block, pair, half, shape(1, 128, F32)), "relay", 10 * dot
+    )(scal, place, labels, both, after, before, relay_v, sums, image_total, image_far, text_far)
+    from_diagonal = diagonally(diagonal)
+    from_far = far_side(far)
     got = exchanged(sums, "group")
-    to_up, to_down, to_back, image_total, text_total, sums = call(
-        late_kernel,
-        [SMEM] + [VMEM] * 12,
-        (shape(2 * rows, width, BF16), half, half, block, block, shape(1, 128, F32)),
-        "late",
-        20 * dot,
-    )(
-        place, after, before, diagonal_v, near_g, far_g, far, far_down, far_up, image_total,
-        text_total, from_cross, got,
-    )
-    from_diagonal = diagonally(to_back)
-    from_below = upward(to_up)
-    from_above = downward(to_down)
+    image_total, text_total, sums = call(
+        middle_kernel, [VMEM] * 5, (block, block, shape(1, 128, F32)), "middle", 10 * dot
+    )(image_total, text_total, from_near, from_cross, got)
     got = exchanged(sums, "blk")
     count = float(cycle * groups * rows) * float(rows) * 8.0
     image_grad, text_grad, stats = call(
         functools.partial(final_kernel, count),
-        [SMEM] + [VMEM] * 8,
+        [SMEM] + [VMEM] * 7,
         (half, half, jax.ShapeDtypeStruct((3,), F32)),
         "final",
         10 * dot,
         (VMEM, VMEM, SMEM),
-    )(scal, images, texts, image_total, text_total, from_below, from_above, from_diagonal, got)
+    )(scal, images, texts, image_total, text_total, from_far, from_diagonal, got)
     return image_grad, text_grad, stats
 
 

time: 114 us -> 109 us (0.956)
  blocking collectives: 39.3 us -> 22 us
  waiting for transfers between devices: 15.2 us -> 24.1 us
  starting transfers between devices: 47.8 us -> 49.8 us
    all_to_all x2 -> x1, blocking collectives: 39.3 us -> 22 us  [exchanged(): return lax.all_to_all(sent, axis, 0, 0).reshape(count, 128)]
    all_to_all x0 -> x1, waiting for transfers between devices: none -> 11.2 us  [exchanged(): return lax.all_to_all(sent, axis, 0, 0).reshape(count, 128)]
    all_to_all x0 -> x1, starting transfers between devices: none -> 4.63 us  [exchanged(): return lax.all_to_all(sent, axis, 0, 0).reshape(count, 128)]
    ppermute x8, starting transfers between devices: 47.8 us -> 45.1 us  [passed(): lax.ppermute(value, 'blk', [(p, (p + step_of(p)) % cycle) for p in range(...]
    ppermute x8, waiting for transfers between devices: 15.2 us -> 12.9 us  [passed(): lax.ppermute(value, 'blk', [(p, (p + step_of(p)) % cycle) for p in range(...]
  transfers between devices with their start and end apart: 8 -> 9, of which waited for: 1 -> 4; matrix products, arithmetic and copies ran while one was open for 0% -> 1% of each run, Pallas kernels for 4% -> 6%
where the time goes in v4:
time: 109 us; the launch traced here: 108 us
  starting transfers between devices  49.8 us (46%)
  waiting for transfers between devices  24.1 us (22%)
  blocking collectives  22 us (20%)
  Pallas kernels  7.92 us (7%)
  between operations  2.11 us (2%)
  local copies, waits for them, and re-layouts  1.65 us (2%)
    ppermute x8, starting transfers between devices, passed(): lax.ppermute(value, 'blk', [(p, (p + step_of(p)) % cycle) for p in range(...  45.1 us
    all_to_all x1, blocking collectives, exchanged(): return lax.all_to_all(sent, axis, 0, 0).reshape(count, 128)  22 us
    ppermute x8, waiting for transfers between devices, passed(): lax.ppermute(value, 'blk', [(p, (p + step_of(p)) % cycle) for p in range(...  12.9 us
    all_to_all x1, waiting for transfers between devices, exchanged(): return lax.all_to_all(sent, axis, 0, 0).reshape(count, 128)  11.2 us
    all_to_all x1, starting transfers between devices, exchanged(): return lax.all_to_all(sent, axis, 0, 0).reshape(count, 128)  4.63 us
    pallas_call x1, Pallas kernels, per_device(): call(early_kernel, head + [VMEM] * 8, (block, block, half, pair, block, h...  2.23 us
  transfers between devices with their start and end apart: 9, of which 4 were waited for; matrix products, arithmetic and copies ran while one was open for 1% of the time, Pallas kernels for 6%

profile of v4, /device:TPU:1, one launch (start us, length us, event | category | flops | bytes accessed | tf_op | source)
XLA Modules:
  0.0 107.6 jit_solution(15112633791553367005)
XLA Ops:
  0.7 1.0 copy-done.1
  1.6 0.1 text.1.text_unit_ref
  1.8 8.7 %collective-permute-start.2 = (bf16[128,1152]{1,0:T(8,128)(2,1)S(1)}, bf16[128,1152]{1,0:T(8,128)(2,1)S(1)}, u32[]{:S(2)}, u32[]{:S(2)}) collective-permute-start(bf16[128,1152]{1,0:T(8,128)(2,1)S(1)} %text.1.text_unit_ref), channel_id=1, source_target_pairs={{0,64},{64,0},{128,192},{192,128},{256,320},{320,256},{384,448},{4... | collective-permute-start | bytes 884744 | tf_op jit(solution)/shard_map/ppermute | solution.py:252
  10.6 0.2 image.1.own_ref
  10.8 17.2 %collective-permute-start = (bf16[128,2432]{1,0:T(8,128)(2,1)S(1)}, bf16[128,2432]{1,0:T(8,128)(2,1)S(1)}, u32[]{:S(2)}, u32[]{:S(2)}) collective-permute-start(bf16[128,2432]{1,0:T(8,128)(2,1)S(1)} %image.1.own_ref), channel_id=1, source_target_pairs={{0,896},{64,960},{128,0},{192,64},{256,128},{320,192},{384,256},{4... | collective-permute-start | bytes 1867784 | tf_op jit(solution)/shard_map/ppermute | solution.py:252
  27.9 1.9 %collective-permute-start.1 = (bf16[128,2432]{1,0:T(8,128)(2,1)S(1)}, bf16[128,2432]{1,0:T(8,128)(2,1)S(1)}, u32[]{:S(2)}, u32[]{:S(2)}) collective-permute-start(bf16[128,2432]{1,0:T(8,128)(2,1)S(1)} %image.1.own_ref), channel_id=1, source_target_pairs={{0,128},{64,192},{128,256},{192,320},{256,384},{320,448},{384,512}... | collective-permute-start | bytes 1867784 | tf_op jit(solution)/shard_map/ppermute | solution.py:252
  31.2 0.1 pad_maximum_fusion.scal_ref
  31.2 1.9 %collective-permute-start.3 = (bf16[128,1152]{1,0:T(8,128)(2,1)S(1)}, bf16[128,1152]{1,0:T(8,128)(2,1)S(1)}, u32[]{:S(2)}, u32[]{:S(2)}) collective-permute-start(bf16[128,1152]{1,0:T(8,128)(2,1)S(1)} %collective-permute-done.2.cross_ref), channel_id=1, source_target_pairs={{0,128},{64,960},{128,256},{192,64},{256,384},{320,192},{384,512},... | collective-permute-start | bytes 884744 | tf_op jit(solution)/shard_map/ppermute | solution.py:252
  33.2 1.4 %own.1 = (f32[128,1152]{1,0:T(8,128)S(1)}, f32[128,1152]{1,0:T(8,128)S(1)}, f32[128,1152]{1,0:T(8,128)S(1)}, f32[8,128]{1,0:T(8,128)S(1)}) custom-call(f32[2]{0:T(128)S(1)} %pad_maximum_fusion.scal_ref, s32[1]{0:T(128)} %bitcast.place_ref, s32[16,128]{1,0:T(8,128)S(1)} %copy-done.3, bf16[128,2432]{1,0:T(8,128)(2,1)S(1)} %image.1.own_ref, ...), custom_call_target="tpu_custom_call" | custom-call | flops 7549747200 | tf_op jit(solution)/shard_map/own/pallas_call | solution.py:281
  34.6 5.7 %collective-permute-done.after_ref = bf16[128,2432]{1,0:T(8,128)(2,1)S(1)} collective-permute-done((bf16[128,2432]{1,0:T(8,128)(2,1)S(1)}, bf16[128,2432]{1,0:T(8,128)(2,1)S(1)}, u32[]{:S(2)}, u32[]{:S(2)}) %collective-permute-start) | collective-permute-done | bytes 622624 | tf_op jit(solution)/shard_map/ppermute | solution.py:252
  40.3 5.0 %collective-permute-done.1.before_ref = bf16[128,2432]{1,0:T(8,128)(2,1)S(1)} collective-permute-done((bf16[128,2432]{1,0:T(8,128)(2,1)S(1)}, bf16[128,2432]{1,0:T(8,128)(2,1)S(1)}, u32[]{:S(2)}, u32[]{:S(2)}) %collective-permute-start.1) | collective-permute-done | bytes 622624 | tf_op jit(solution)/shard_map/ppermute | solution.py:252
  45.3 2.2 %early.1 = (f32[128,1152]{1,0:T(8,128)S(1)}, f32[128,1152]{1,0:T(8,128)S(1)}, bf16[128,1152]{1,0:T(8,128)(2,1)S(1)}, bf16[256,1152]{1,0:T(8,128)(2,1)S(1)}, f32[...) custom-call(f32[2]{0:T(128)S(1)} %pad_maximum_fusion.scal_ref, s32[1]{0:T(128)} %bitcast.place_ref, ...), custom_call_target="tpu_custom_call" | custom-call | flops 754974720 | tf_op jit(solution)/shard_map/early/pallas_call | solution.py:285
  47.6 1.9 %collective-permute-start.4 = (bf16[256,1152]{1,0:T(8,128)(2,1)S(1)}, bf16[256,1152]{1,0:T(8,128)(2,1)S(1)}, u32[]{:S(2)}, u32[]{:S(2)}) collective-permute-start(bf16[256,1152]{1,0:T(8,128)(2,1)S(1)} %get-tuple-element.31), channel_id=1, source_target_pairs={{0,896},{64,192},{128,0},{192,320},{256,128},{320,448},{384,256},{... | collective-permute-start | bytes 1769480 | tf_op jit(solution)/shard_map/ppermute | solution.py:252
  49.5 2.1 %collective-permute-done.3.relay_ref = bf16[128,1152]{1,0:T(8,128)(2,1)S(1)} collective-permute-done((bf16[128,1152]{1,0:T(8,128)(2,1)S(1)}, bf16[128,1152]{1,0:T(8,128)(2,1)S(1)}, u32[]{:S(2)}, u32[]{:S(2)}) %collective-permute-start.3) | collective-permute-done | bytes 294944 | tf_op jit(solution)/shard_map/ppermute | solution.py:252
  51.7 2.0 %relay.1 = (f32[128,1152]{1,0:T(8,128)S(1)}, bf16[256,1152]{1,0:T(8,128)(2,1)S(1)}, bf16[128,1152]{1,0:T(8,128)(2,1)}, f32[1,128]{1,0:T(1,128)S(1)}) custom-call(f32[2]{0:T(128)S(1)} %pad_maximum_fusion.scal_ref, s32[1]{0:T(128)} %bitcast.place_ref, s32[16,128]{1,0:T(8,128)S(1)} %copy-done.3, bf16[128,2432]{1,0:T(8,128)(2,1)S(1)} %image.1.own_ref, ...), custom_call_target="tpu_custom_call" | custom-call | flops 377487360 | tf_op jit(solution)/shard_map/relay/pallas_call | solution.py:294
  53.6 1.9 %collective-permute-start.6 = (bf16[256,1152]{1,0:T(8,128)(2,1)S(1)}, bf16[256,1152]{1,0:T(8,128)(2,1)S(1)}, u32[]{:S(2)}, u32[]{:S(2)}) collective-permute-start(bf16[256,1152]{1,0:T(8,128)(2,1)S(1)} %get-tuple-element.36), channel_id=1, source_target_pairs={{0,128},{64,960},{128,256},{192,64},{256,384},{320,192},{384,512},... | collective-permute-start | bytes 1769480 | tf_op jit(solution)/shard_map/ppermute | solution.py:252
  55.6 2.7 %collective-permute-start.5 = (bf16[128,1152]{1,0:T(8,128)(2,1)S(1)}, bf16[128,1152]{1,0:T(8,128)(2,1)S(1)}, u32[]{:S(2)}, u32[]{:S(2)}) collective-permute-start(bf16[128,1152]{1,0:T(8,128)(2,1)S(1)} %get-tuple-element.32), channel_id=1, source_target_pairs={{0,64},{64,0},{128,192},{192,128},{256,320},{320,256},{384,448},{4... | collective-permute-start | bytes 884744 | tf_op jit(solution)/shard_map/ppermute | solution.py:252
  58.3 8.8 %collective-permute-start.7 = (bf16[128,1152]{1,0:T(8,128)(2,1)}, bf16[128,1152]{1,0:T(8,128)(2,1)S(1)}, u32[]{:S(2)}, u32[]{:S(2)}) collective-permute-start(bf16[128,1152]{1,0:T(8,128)(2,1)} %get-tuple-element.37), channel_id=1, source_target_pairs={{0,960},{64,128},{128,64},{192,256},{256,192},{320,384},{384,320},... | collective-permute-start | bytes 884744 | tf_op jit(solution)/shard_map/ppermute | solution.py:252
  67.2 22.0 %all_to_all.10 = f32[64,1,128]{2,1,0:T(1,128)S(1)} all-to-all(f32[64,1,128]{2,1,0:T(1,128)S(1)} %broadcast_in_dim.15), channel_id=1, replica_groups=mesh['blk'=16,'group'=64] {'group'}, dimensions={0} | all-to-all | bytes 65536 | tf_op jit(solution)/shard_map/all_to_all | solution.py:239
  89.2 0.2 middle.1
  89.3 0.6 broadcast_in_dim.17
  89.9 4.6 %all-to-all-start.1 = ((f32[16,1,128]{2,1,0:T(1,128)}), f32[16,1,128]{2,1,0:T(1,128)S(1)}, u32[]{:S(2)}, u32[]{:S(2)}) async-start(f32[16,1,128]{2,1,0:T(1,128)} %broadcast_in_dim.17), calls=%async_computation.1 | async-start | bytes 16384 | tf_op jit(solution)/shard_map/all_to_all | solution.py:239
  94.6 11.2 %all-to-all-done.1 = f32[16,1,128]{2,1,0:T(1,128)S(1)} async-done(((f32[16,1,128]{2,1,0:T(1,128)}), f32[16,1,128]{2,1,0:T(1,128)S(1)}, u32[]{:S(2)}, u32[]{:S(2)}) %all-to-all-start.1) | async-done | bytes 8224 | tf_op jit(solution)/shard_map/all_to_all | solution.py:239
  105.7 1.8 %final.1 = (bf16[128,1152]{1,0:T(8,128)(2,1)}, bf16[128,1152]{1,0:T(8,128)(2,1)}, f32[3]{0:T(128)}) custom-call(f32[2]{0:T(128)S(1)} %pad_maximum_fusion.scal_ref, bf16[128,1152]{1,0:T(8,128)(2,1)S(1)} %copy-done, bf16[128,1152]{1,0:T(8,128)(2,1)S(1)} %copy-done.2, f32[128,1152]{1,0:T(8,128)S(1)} %get-tuple-element.34.image_total_ref, ...), custom_call_target="tpu_custom_call" | custom-call | flops 377487360 | tf_op jit(solution)/shard_map/final/pallas_call | solution.py:305
  (15 shorter events, 0.1 us)
Async XLA Ops:
  0.6 9.9 %copy-start = (bf16[128,1152]{1,0:T(8,128)(2,1)S(1)}, bf16[128,1152]{1,0:T(8,128)(2,1)}, u32[]{:S(2)}) copy-start(bf16[128,1152]{1,0:T(8,128)(2,1)} %image_ref.3) | copy-start | bytes 884740
  0.6 1.0 copy-start.1
  1.8 8.8 %copy-start.4 = (f32[128]{0:T(128)S(1)}, f32[128]{0:T(128)}, u32[]{:S(2)}) copy-start(f32[128]{0:T(128)} %param.9) | copy-start | bytes 1540
  1.8 29.4 %collective-permute-start.2 = (bf16[128,1152]{1,0:T(8,128)(2,1)S(1)}, bf16[128,1152]{1,0:T(8,128)(2,1)S(1)}, u32[]{:S(2)}, u32[]{:S(2)}) collective-permute-start(bf16[128,1152]{1,0:T(8,128)(2,1)S(1)} %text.1.text_unit_ref), channel_id=1, source_target_pairs={{0,64},{64,0},{128,192},{192,128},{256,320},{320,256},{384,448},{4... | collective-permute-start | bytes 884744 | tf_op jit(solution)/shard_map/ppermute | solution.py:252
  10.7 22.4 %copy-start.3 = (s32[16,128]{1,0:T(8,128)S(1)}, s32[16,128]{1,0:T(8,128)}, u32[]{:S(2)}) copy-start(s32[16,128]{1,0:T(8,128)} %label_ref.5) | copy-start | bytes 24580
  10.8 29.5 %collective-permute-start = (bf16[128,2432]{1,0:T(8,128)(2,1)S(1)}, bf16[128,2432]{1,0:T(8,128)(2,1)S(1)}, u32[]{:S(2)}, u32[]{:S(2)}) collective-permute-start(bf16[128,2432]{1,0:T(8,128)(2,1)S(1)} %image.1.own_ref), channel_id=1, source_target_pairs={{0,896},{64,960},{128,0},{192,64},{256,128},{320,192},{384,256},{4... | collective-permute-start | bytes 1867784 | tf_op jit(solution)/shard_map/ppermute | solution.py:252
  27.9 17.4 %collective-permute-start.1 = (bf16[128,2432]{1,0:T(8,128)(2,1)S(1)}, bf16[128,2432]{1,0:T(8,128)(2,1)S(1)}, u32[]{:S(2)}, u32[]{:S(2)}) collective-permute-start(bf16[128,2432]{1,0:T(8,128)(2,1)S(1)} %image.1.own_ref), channel_id=1, source_target_pairs={{0,128},{64,192},{128,256},{192,320},{256,384},{320,448},{384,512}... | collective-permute-start | bytes 1867784 | tf_op jit(solution)/shard_map/ppermute | solution.py:252
  31.2 20.4 %collective-permute-start.3 = (bf16[128,1152]{1,0:T(8,128)(2,1)S(1)}, bf16[128,1152]{1,0:T(8,128)(2,1)S(1)}, u32[]{:S(2)}, u32[]{:S(2)}) collective-permute-start(bf16[128,1152]{1,0:T(8,128)(2,1)S(1)} %collective-permute-done.2.cross_ref), channel_id=1, source_target_pairs={{0,128},{64,960},{128,256},{192,64},{256,384},{320,192},{384,512},... | collective-permute-start | bytes 884744 | tf_op jit(solution)/shard_map/ppermute | solution.py:252
  47.6 41.6 %collective-permute-start.4 = (bf16[256,1152]{1,0:T(8,128)(2,1)S(1)}, bf16[256,1152]{1,0:T(8,128)(2,1)S(1)}, u32[]{:S(2)}, u32[]{:S(2)}) collective-permute-start(bf16[256,1152]{1,0:T(8,128)(2,1)S(1)} %get-tuple-element.31), channel_id=1, source_target_pairs={{0,896},{64,192},{128,0},{192,320},{256,128},{320,448},{384,256},{... | collective-permute-start | bytes 1769480 | tf_op jit(solution)/shard_map/ppermute | solution.py:252
  53.6 40.9 %collective-permute-start.6 = (bf16[256,1152]{1,0:T(8,128)(2,1)S(1)}, bf16[256,1152]{1,0:T(8,128)(2,1)S(1)}, u32[]{:S(2)}, u32[]{:S(2)}) collective-permute-start(bf16[256,1152]{1,0:T(8,128)(2,1)S(1)} %get-tuple-element.36), channel_id=1, source_target_pairs={{0,128},{64,960},{128,256},{192,64},{256,384},{320,192},{384,512},... | collective-permute-start | bytes 1769480 | tf_op jit(solution)/shard_map/ppermute | solution.py:252
  55.6 33.6 %collective-permute-start.5 = (bf16[128,1152]{1,0:T(8,128)(2,1)S(1)}, bf16[128,1152]{1,0:T(8,128)(2,1)S(1)}, u32[]{:S(2)}, u32[]{:S(2)}) collective-permute-start(bf16[128,1152]{1,0:T(8,128)(2,1)S(1)} %get-tuple-element.32), channel_id=1, source_target_pairs={{0,64},{64,0},{128,192},{192,128},{256,320},{320,256},{384,448},{4... | collective-permute-start | bytes 884744 | tf_op jit(solution)/shard_map/ppermute | solution.py:252
  58.3 36.3 %collective-permute-start.7 = (bf16[128,1152]{1,0:T(8,128)(2,1)}, bf16[128,1152]{1,0:T(8,128)(2,1)S(1)}, u32[]{:S(2)}, u32[]{:S(2)}) collective-permute-start(bf16[128,1152]{1,0:T(8,128)(2,1)} %get-tuple-element.37), channel_id=1, source_target_pairs={{0,960},{64,128},{128,64},{192,256},{256,192},{320,384},{384,320},... | collective-permute-start | bytes 884744 | tf_op jit(solution)/shard_map/ppermute | solution.py:252
  89.2 16.6 %copy-start.2 = (bf16[128,1152]{1,0:T(8,128)(2,1)S(1)}, bf16[128,1152]{1,0:T(8,128)(2,1)}, u32[]{:S(2)}) copy-start(bf16[128,1152]{1,0:T(8,128)(2,1)} %text_ref.3) | copy-start | bytes 884740
  89.9 15.8 %all-to-all-start.1 = ((f32[16,1,128]{2,1,0:T(1,128)}), f32[16,1,128]{2,1,0:T(1,128)S(1)}, u32[]{:S(2)}, u32[]{:S(2)}) async-start(f32[16,1,128]{2,1,0:T(1,128)} %broadcast_in_dim.17), calls=%async_computation.1 | async-start | bytes 16384 | tf_op jit(solution)/shard_map/all_to_all | solution.py:239

commit v5 on v2

--- a/solution.py
+++ b/solution.py
@@ -187,8 +187,8 @@
 
 def late_kernel(
     scal_ref, place_ref, label_ref, own_ref, after_ref, before_ref, cross_ref, relay_ref, relay_v_ref,
-    near_ref, far_g_ref, far_ref, down_in_ref, up_in_ref, image_in_ref, text_in_ref, got_ref,
-    up_ref, down_ref, image_total_ref, text_total_ref, sums_ref,
+    near_ref, far_g_ref, far_ref, down_in_ref, up_in_ref, image_in_ref, text_in_ref,
+    up_ref, down_ref, image_total_ref, text_total_ref,
 ):
     width = relay_v_ref.shape[1]
     rows = relay_v_ref.shape[0]
@@ -216,6 +216,9 @@
     gr = scorer.grads(ur, v, wr, col_r, row, False)
     image_total_ref[...] = image_in_ref[...] + matmul(near_ref[...], relay_v_ref[...])
     text_total_ref[...] = text_in_ref[...] + t_matmul(gc, uc) + t_matmul(gr, ur)
+
+
+def middle_kernel(got_ref, sums_ref):
     sums_ref[...] = jnp.sum(got_ref[...], axis=0, keepdims=True)
 
 
@@ -305,18 +308,19 @@
         relay_kernel, head + [VMEM] * 5, (shape(rows, rows, BF16),) * 2 + (shape(1, 128, F32),), "relay", 10 * dot
     )(scal, place, labels, both, after, before, relay_v, sums)
     got = exchanged(sums, "group")
-    to_up, to_down, image_total, text_total, sums = call(
+    to_up, to_down, image_total, text_total = call(
         late_kernel,
-        head + [VMEM] * 14,
-        (shape(2 * rows, width, BF16),) * 2 + (block,) * 2 + (shape(1, 128, F32),),
+        head + [VMEM] * 13,
+        (shape(2 * rows, width, BF16),) * 2 + (block,) * 2,
         "late",
-        20 * dot,
+        400 * dot,
     )(
         scal, place, labels, both, after, before, cross_u, relay_u, relay_v,
-        near_g, far_g, far, far_down, far_up, image_total, text_total, got,
+        near_g, far_g, far, far_down, far_up, image_total, text_total,
     )
     from_below = upward(to_up)
     from_above = downward(to_down)
+    sums = call(middle_kernel, [VMEM], shape(1, 128, F32), "middle", 300 * dot)(got)
     got = exchanged(sums, "blk")
     count = float(cycle * groups * rows) * float(rows) * 8.0
     image_grad, text_grad, stats = call(

time: 103 us -> 103 us (level); the launches traced: 103 us -> 101 us
  blocking collectives: 41.6 us -> 16.5 us
  starting transfers between devices: 41.8 us -> 51 us
  local copies, waits for them, and re-layouts: 1.05 us -> 9.6 us
  waiting for transfers between devices: 7.37 us -> 11.7 us
  Pallas kernels: 8.56 us -> 10.4 us
    all_to_all x2 -> x1, blocking collectives: 41.6 us -> 16.5 us  [exchanged(): return lax.all_to_all(sent, axis, 0, 0).reshape(count, 128)]
    all_to_all x0 -> x1, starting transfers between devices: none -> 11 us  [exchanged(): return lax.all_to_all(sent, axis, 0, 0).reshape(count, 128)]
    unnamed x10 -> x34, local copies, waits for them, and re-layouts: 1.02 us -> 8.96 us
    ppermute x8, waiting for transfers between devices: 7.37 us -> 11.7 us  [passed(): lax.ppermute(value, 'blk', [(p, (p + step_of(p)) % cycle) for p in range(...]
    ppermute x8, starting transfers between devices: 41.8 us -> 40.1 us  [passed(): lax.ppermute(value, 'blk', [(p, (p + step_of(p)) % cycle) for p in range(...]
    pallas_call x1 -> x2, Pallas kernels: 2 us -> 3.13 us  [the longest x1 3.12 us: per_device(): call(late_kernel, head + [VMEM] * 13, (shape(2 * rows, width, BF16),) * 2...]
  transfers between devices with their start and end apart: 8 -> 9, of which waited for: 4 -> 4; matrix products, arithmetic and copies ran while one was open for 0% -> 1% of each run, Pallas kernels for 4% -> 8%
where the time goes in v5:
time: 103 us; the launch traced here: 101 us
  starting transfers between devices  51 us (50%)
  blocking collectives  16.5 us (16%)
  waiting for transfers between devices  11.7 us (11%)
  Pallas kernels  10.4 us (10%)
  local copies, waits for them, and re-layouts  9.6 us (9%)
  between operations  2.13 us (2%)
    ppermute x8, starting transfers between devices, passed(): lax.ppermute(value, 'blk', [(p, (p + step_of(p)) % cycle) for p in range(...  40.1 us
    all_to_all x1, blocking collectives, exchanged(): return lax.all_to_all(sent, axis, 0, 0).reshape(count, 128)  16.5 us
    ppermute x8, waiting for transfers between devices, passed(): lax.ppermute(value, 'blk', [(p, (p + step_of(p)) % cycle) for p in range(...  11.7 us
    all_to_all x1, starting transfers between devices, exchanged(): return lax.all_to_all(sent, axis, 0, 0).reshape(count, 128)  11 us
    unnamed x34, local copies, waits for them, and re-layouts  8.96 us
    pallas_call x1, Pallas kernels, per_device(): call(late_kernel, head + [VMEM] * 13, (shape(2 * rows, width, BF16),) * 2...  3.12 us
  transfers between devices with their start and end apart: 9, of which 4 were waited for; matrix products, arithmetic and copies ran while one was open for 1% of the time, Pallas kernels for 8%

profile of v5, /device:TPU:1, one launch (start us, length us, event | category | flops | bytes accessed | tf_op | source)
XLA Modules:
  0.0 101.4 jit_solution(8543625605730306981)
XLA Ops:
  0.7 1.0 copy-done.1
  1.8 8.7 %collective-permute-start.3 = (bf16[128,1152]{1,0:T(8,128)(2,1)S(1)}, bf16[128,1152]{1,0:T(8,128)(2,1)S(1)}, u32[]{:S(2)}, u32[]{:S(2)}) collective-permute-start(bf16[128,1152]{1,0:T(8,128)(2,1)S(1)} %text.1.text_unit_ref), channel_id=1, source_target_pairs={{0,64},{64,0},{128,192},{192,128},{256,320},{320,256},{384,448},{4... | collective-permute-start | bytes 884744 | tf_op jit(solution)/shard_map/ppermute | solution.py:271
  11.5 17.2 %collective-permute-start = (bf16[128,2432]{1,0:T(8,128)(2,1)S(1)}, bf16[128,2432]{1,0:T(8,128)(2,1)S(1)}, u32[]{:S(2)}, u32[]{:S(2)}) collective-permute-start(bf16[128,2432]{1,0:T(8,128)(2,1)S(1)} %get-tuple-element.23.own_ref), channel_id=1, source_target_pairs={{0,896},{64,960},{128,0},{192,64},{256,128},{320,192},{384,256},{4... | collective-permute-start | bytes 1867784 | tf_op jit(solution)/shard_map/ppermute | solution.py:271
  28.7 1.9 %collective-permute-start.1 = (bf16[128,2432]{1,0:T(8,128)(2,1)S(1)}, bf16[128,2432]{1,0:T(8,128)(2,1)S(1)}, u32[]{:S(2)}, u32[]{:S(2)}) collective-permute-start(bf16[128,2432]{1,0:T(8,128)(2,1)S(1)} %get-tuple-element.23.own_ref), channel_id=1, source_target_pairs={{0,128},{64,192},{128,256},{192,320},{256,384},{320,448},{384,512}... | collective-permute-start | bytes 1867784 | tf_op jit(solution)/shard_map/ppermute | solution.py:271
  30.6 1.9 %collective-permute-start.2 = (bf16[128,1280]{1,0:T(8,128)(2,1)}, bf16[128,1280]{1,0:T(8,128)(2,1)}, u32[]{:S(2)}, u32[]{:S(2)}) collective-permute-start(bf16[128,1280]{1,0:T(8,128)(2,1)} %get-tuple-element.24), channel_id=1, source_target_pairs={{0,64},{64,0},{128,192},{192,128},{256,320},{320,256},{384,448},{4... | collective-permute-start | bytes 983048 | tf_op jit(solution)/shard_map/ppermute | solution.py:271
  33.9 1.9 %collective-permute-start.5 = (bf16[128,1152]{1,0:T(8,128)(2,1)S(1)}, bf16[128,1152]{1,0:T(8,128)(2,1)S(1)}, u32[]{:S(2)}, u32[]{:S(2)}) collective-permute-start(bf16[128,1152]{1,0:T(8,128)(2,1)S(1)} %collective-permute-done.3.cross_ref), channel_id=1, source_target_pairs={{0,128},{64,960},{128,256},{192,64},{256,384},{320,192},{384,512},... | collective-permute-start | bytes 884744 | tf_op jit(solution)/shard_map/ppermute | solution.py:271
  35.8 1.3 %own.1 = (f32[128,1152]{1,0:T(8,128)S(1)}, f32[128,1152]{1,0:T(8,128)S(1)}, f32[8,128]{1,0:T(8,128)S(1)}) custom-call(f32[2]{0:T(128)S(1)} %pad_maximum_fusion.scal_ref, s32[1]{0:T(128)} %bitcast.place_ref, s32[16,128]{1,0:T(8,128)S(1)} %copy-done.5, bf16[128,2432]{1,0:T(8,128)(2,1)S(1)} %get-tuple-element.23.own_ref, ...), custom_call_target="tpu_custom_call" | custom-call | flops 5662310400 | tf_op jit(solution)/shard_map/own/pallas_call | solution.py:299
  37.1 3.9 %collective-permute-done.after_ref = bf16[128,2432]{1,0:T(8,128)(2,1)S(1)} collective-permute-done((bf16[128,2432]{1,0:T(8,128)(2,1)S(1)}, bf16[128,2432]{1,0:T(8,128)(2,1)S(1)}, u32[]{:S(2)}, u32[]{:S(2)}) %collective-permute-start) | collective-permute-done | bytes 622624 | tf_op jit(solution)/shard_map/ppermute | solution.py:271
  41.0 5.1 %collective-permute-done.1.before_ref = bf16[128,2432]{1,0:T(8,128)(2,1)S(1)} collective-permute-done((bf16[128,2432]{1,0:T(8,128)(2,1)S(1)}, bf16[128,2432]{1,0:T(8,128)(2,1)S(1)}, u32[]{:S(2)}, u32[]{:S(2)}) %collective-permute-start.1) | collective-permute-done | bytes 622624 | tf_op jit(solution)/shard_map/ppermute | solution.py:271
  46.2 2.0 %early.1 = (f32[128,1152]{1,0:T(8,128)S(1)}, f32[128,1152]{1,0:T(8,128)S(1)}, f32[128,1152]{1,0:T(8,128)S(1)}, f32[128,1152]{1,0:T(8,128)S(1)}, f32[128,1152]{1,0:T(8,128)S(1)}, /*index=5*/f32[8,128]{1,0:T(8,128)S(1)}) custom-call(f32[2]{0:T(128)S(1)} %pad_maximum_fusion.scal_ref, s32[1]{0:T(128)} %bitcast.place_ref, s32[16,128]{1,0:T(8,128)S(1)} %copy-done.5, ...), custom_call_target="tpu_custom_call" | custom-call | flops 754974720 | tf_op jit(solution)/shard_map/early/pallas_call | solution.py:302
  49.8 1.9 %collective-permute-start.4 = (bf16[128,1280]{1,0:T(8,128)(2,1)}, bf16[128,1280]{1,0:T(8,128)(2,1)}, u32[]{:S(2)}, u32[]{:S(2)}) collective-permute-start(bf16[128,1280]{1,0:T(8,128)(2,1)} %collective-permute-done.2.cross_ref), channel_id=1, source_target_pairs={{0,128},{64,960},{128,256},{192,64},{256,384},{320,192},{384,512},... | collective-permute-start | bytes 983048 | tf_op jit(solution)/shard_map/ppermute | solution.py:271
  52.5 1.0 %relay.1 = (bf16[128,128]{1,0:T(8,128)(2,1)S(1)}, bf16[128,128]{1,0:T(8,128)(2,1)S(1)}, f32[1,128]{1,0:T(1,128)S(1)}) custom-call(f32[2]{0:T(128)S(1)} %pad_maximum_fusion.scal_ref, s32[1]{0:T(128)} %bitcast.place_ref, s32[16,128]{1,0:T(8,128)S(1)} %copy-done.5, bf16[128,2432]{1,0:T(8,128)(2,1)S(1)} %get-tuple-element.23.own_ref, ...), custom_call_target="tpu_custom_call" | custom-call | flops 377487360 | tf_op jit(solution)/shard_map/relay/pallas_call | solution.py:307
  54.2 11.0 %all-to-all-start = ((f32[64,1,128]{2,1,0:T(1,128)}), f32[64,1,128]{2,1,0:T(1,128)S(1)}, u32[]{:S(2)}, u32[]{:S(2)}) async-start(f32[64,1,128]{2,1,0:T(1,128)} %broadcast_in_dim.15), calls=%async_computation | async-start | bytes 65536 | tf_op jit(solution)/shard_map/all_to_all | solution.py:258
  65.2 1.9 %collective-permute-done.4.relay_ref = bf16[128,1280]{1,0:T(8,128)(2,1)} collective-permute-done((bf16[128,1280]{1,0:T(8,128)(2,1)}, bf16[128,1280]{1,0:T(8,128)(2,1)}, u32[]{:S(2)}, u32[]{:S(2)}) %collective-permute-start.4) | collective-permute-done | bytes 327712 | tf_op jit(solution)/shard_map/ppermute | solution.py:271
  68.0 1.1 %copy-done.7 = f32[128,1152]{1,0:T(8,128)S(1)} copy-done((f32[128,1152]{1,0:T(8,128)S(1)}, f32[128,1152]{1,0:T(8,128)}, u32[]{:S(2)}) %copy-start.7) | copy-done | bytes 589848
  69.1 1.1 %copy-done.9 = f32[128,1152]{1,0:T(8,128)S(1)} copy-done((f32[128,1152]{1,0:T(8,128)S(1)}, f32[128,1152]{1,0:T(8,128)}, u32[]{:S(2)}) %copy-start.9) | copy-done | bytes 589848
  70.2 1.1 %copy-done.11 = f32[128,1152]{1,0:T(8,128)S(1)} copy-done((f32[128,1152]{1,0:T(8,128)S(1)}, f32[128,1152]{1,0:T(8,128)}, u32[]{:S(2)}) %copy-start.11) | copy-done | bytes 589848
  71.2 1.1 %copy-done.13 = f32[128,1152]{1,0:T(8,128)S(1)} copy-done((f32[128,1152]{1,0:T(8,128)S(1)}, f32[128,1152]{1,0:T(8,128)}, u32[]{:S(2)}) %copy-start.13) | copy-done | bytes 589848
  72.3 1.1 %copy-done.15 = f32[128,1152]{1,0:T(8,128)S(1)} copy-done((f32[128,1152]{1,0:T(8,128)S(1)}, f32[128,1152]{1,0:T(8,128)}, u32[]{:S(2)}) %copy-start.15) | copy-done | bytes 589848
  73.4 3.1 %late.1 = (bf16[256,1152]{1,0:T(8,128)(2,1)}, bf16[256,1152]{1,0:T(8,128)(2,1)}, f32[128,1152]{1,0:T(8,128)S(1)}, f32[128,1152]{1,0:T(8,128)S(1)}) custom-call(f32[2]{0:T(128)S(1)} %pad_maximum_fusion.scal_ref, s32[1]{0:T(128)} %bitcast.place_ref, s32[16,128]{1,0:T(8,128)S(1)} %copy-done.5, bf16[128,2432]{1,0:T(8,128)(2,1)S(1)} %get-tuple-element.23.own_ref, ...), custom_call_target="tpu_custom_call" | custom-call | flops 15099494400 | tf_op jit(solution)/shard_map/late/pallas_call | solution.py:311
  76.5 1.9 %collective-permute-start.6 = (bf16[256,1152]{1,0:T(8,128)(2,1)}, bf16[256,1152]{1,0:T(8,128)(2,1)S(1)}, u32[]{:S(2)}, u32[]{:S(2)}) collective-permute-start(bf16[256,1152]{1,0:T(8,128)(2,1)} %get-tuple-element.40), channel_id=1, source_target_pairs={{0,128},{64,192},{128,256},{192,320},{256,384},{320,448},{384,512}... | collective-permute-start | bytes 1769480 | tf_op jit(solution)/shard_map/ppermute | solution.py:271
  78.4 4.6 %collective-permute-start.7 = (bf16[256,1152]{1,0:T(8,128)(2,1)}, bf16[256,1152]{1,0:T(8,128)(2,1)S(1)}, u32[]{:S(2)}, u32[]{:S(2)}) collective-permute-start(bf16[256,1152]{1,0:T(8,128)(2,1)} %get-tuple-element.41), channel_id=1, source_target_pairs={{0,896},{64,960},{128,0},{192,64},{256,128},{320,192},{384,256},{4... | collective-permute-start | bytes 1769480 | tf_op jit(solution)/shard_map/ppermute | solution.py:271
  83.0 16.5 %all_to_all.10 = f32[16,1,128]{2,1,0:T(1,128)S(1)} all-to-all(f32[16,1,128]{2,1,0:T(1,128)S(1)} %broadcast_in_dim.17), channel_id=1, replica_groups=mesh['blk'=16,'group'=64] {'blk'}, dimensions={0} | all-to-all | bytes 16384 | tf_op jit(solution)/shard_map/all_to_all | solution.py:258
  99.5 1.9 %final.1 = (bf16[128,1152]{1,0:T(8,128)(2,1)}, bf16[128,1152]{1,0:T(8,128)(2,1)}, f32[3]{0:T(128)}) custom-call(f32[2]{0:T(128)S(1)} %pad_maximum_fusion.scal_ref, bf16[128,1152]{1,0:T(8,128)(2,1)S(1)} %copy-done, bf16[128,1152]{1,0:T(8,128)(2,1)S(1)} %copy-done.2, f32[128,1152]{1,0:T(8,128)S(1)} %get-tuple-element.38.image_total_ref, ...), custom_call_target="tpu_custom_call" | custom-call | flops 377487360 | tf_op jit(solution)/shard_map/final/pallas_call | solution.py:326
  (40 shorter events, 5.2 us)
Async XLA Ops:
  0.6 9.9 %copy-start = (bf16[128,1152]{1,0:T(8,128)(2,1)S(1)}, bf16[128,1152]{1,0:T(8,128)(2,1)}, u32[]{:S(2)}) copy-start(bf16[128,1152]{1,0:T(8,128)(2,1)} %image_ref.3) | copy-start | bytes 884740
  0.6 1.0 copy-start.1
  1.8 8.8 %copy-start.16 = (f32[128]{0:T(128)S(1)}, f32[128]{0:T(128)}, u32[]{:S(2)}) copy-start(f32[128]{0:T(128)} %param.9) | copy-start | bytes 1540
  1.8 32.1 %collective-permute-start.3 = (bf16[128,1152]{1,0:T(8,128)(2,1)S(1)}, bf16[128,1152]{1,0:T(8,128)(2,1)S(1)}, u32[]{:S(2)}, u32[]{:S(2)}) collective-permute-start(bf16[128,1152]{1,0:T(8,128)(2,1)S(1)} %text.1.text_unit_ref), channel_id=1, source_target_pairs={{0,64},{64,0},{128,192},{192,128},{256,320},{320,256},{384,448},{4... | collective-permute-start | bytes 884744 | tf_op jit(solution)/shard_map/ppermute | solution.py:271
  11.5 29.5 %collective-permute-start = (bf16[128,2432]{1,0:T(8,128)(2,1)S(1)}, bf16[128,2432]{1,0:T(8,128)(2,1)S(1)}, u32[]{:S(2)}, u32[]{:S(2)}) collective-permute-start(bf16[128,2432]{1,0:T(8,128)(2,1)S(1)} %get-tuple-element.23.own_ref), channel_id=1, source_target_pairs={{0,896},{64,960},{128,0},{192,64},{256,128},{320,192},{384,256},{4... | collective-permute-start | bytes 1867784 | tf_op jit(solution)/shard_map/ppermute | solution.py:271
  28.7 17.5 %collective-permute-start.1 = (bf16[128,2432]{1,0:T(8,128)(2,1)S(1)}, bf16[128,2432]{1,0:T(8,128)(2,1)S(1)}, u32[]{:S(2)}, u32[]{:S(2)}) collective-permute-start(bf16[128,2432]{1,0:T(8,128)(2,1)S(1)} %get-tuple-element.23.own_ref), channel_id=1, source_target_pairs={{0,128},{64,192},{128,256},{192,320},{256,384},{320,448},{384,512}... | collective-permute-start | bytes 1867784 | tf_op jit(solution)/shard_map/ppermute | solution.py:271
  30.6 5.2 %copy-start.5 = (s32[16,128]{1,0:T(8,128)S(1)}, s32[16,128]{1,0:T(8,128)}, u32[]{:S(2)}) copy-start(s32[16,128]{1,0:T(8,128)} %label_ref.7) | copy-start | bytes 24580
  30.6 19.2 %collective-permute-start.2 = (bf16[128,1280]{1,0:T(8,128)(2,1)}, bf16[128,1280]{1,0:T(8,128)(2,1)}, u32[]{:S(2)}, u32[]{:S(2)}) collective-permute-start(bf16[128,1280]{1,0:T(8,128)(2,1)} %get-tuple-element.24), channel_id=1, source_target_pairs={{0,64},{64,0},{128,192},{192,128},{256,320},{320,256},{384,448},{4... | collective-permute-start | bytes 983048 | tf_op jit(solution)/shard_map/ppermute | solution.py:271
  33.9 18.6 %collective-permute-start.5 = (bf16[128,1152]{1,0:T(8,128)(2,1)S(1)}, bf16[128,1152]{1,0:T(8,128)(2,1)S(1)}, u32[]{:S(2)}, u32[]{:S(2)}) collective-permute-start(bf16[128,1152]{1,0:T(8,128)(2,1)S(1)} %collective-permute-done.3.cross_ref), channel_id=1, source_target_pairs={{0,128},{64,960},{128,256},{192,64},{256,384},{320,192},{384,512},... | collective-permute-start | bytes 884744 | tf_op jit(solution)/shard_map/ppermute | solution.py:271
  49.8 3.7 %copy-start.6 = (f32[128,1152]{1,0:T(8,128)}, f32[128,1152]{1,0:T(8,128)S(1)}, u32[]{:S(2)}) copy-start(f32[128,1152]{1,0:T(8,128)S(1)} %get-tuple-element.36.image_in_ref) | copy-start | bytes 1769476
  49.8 3.7 %copy-start.8 = (f32[128,1152]{1,0:T(8,128)}, f32[128,1152]{1,0:T(8,128)S(1)}, u32[]{:S(2)}) copy-start(f32[128,1152]{1,0:T(8,128)S(1)} %get-tuple-element.37.text_in_ref) | copy-start | bytes 1769476
  49.8 3.7 %copy-start.12 = (f32[128,1152]{1,0:T(8,128)}, f32[128,1152]{1,0:T(8,128)S(1)}, u32[]{:S(2)}) copy-start(f32[128,1152]{1,0:T(8,128)S(1)} %get-tuple-element.34.down_in_ref) | copy-start | bytes 1769476
  49.8 17.3 %collective-permute-start.4 = (bf16[128,1280]{1,0:T(8,128)(2,1)}, bf16[128,1280]{1,0:T(8,128)(2,1)}, u32[]{:S(2)}, u32[]{:S(2)}) collective-permute-start(bf16[128,1280]{1,0:T(8,128)(2,1)} %collective-permute-done.2.cross_ref), channel_id=1, source_target_pairs={{0,128},{64,960},{128,256},{192,64},{256,384},{320,192},{384,512},... | collective-permute-start | bytes 983048 | tf_op jit(solution)/shard_map/ppermute | solution.py:271
  52.5 1.1 %copy-start.3 = (bf16[128,1152]{1,0:T(8,128)(2,1)}, bf16[128,1152]{1,0:T(8,128)(2,1)S(1)}, u32[]{:S(2)}) copy-start(bf16[128,1152]{1,0:T(8,128)(2,1)S(1)} %collective-permute-done.5.relay_ref.relay_v_ref) | copy-start | bytes 884740
  54.2 28.8 %all-to-all-start = ((f32[64,1,128]{2,1,0:T(1,128)}), f32[64,1,128]{2,1,0:T(1,128)S(1)}, u32[]{:S(2)}, u32[]{:S(2)}) async-start(f32[64,1,128]{2,1,0:T(1,128)} %broadcast_in_dim.15), calls=%async_computation | async-start | bytes 65536 | tf_op jit(solution)/shard_map/all_to_all | solution.py:258
  67.1 1.0 copy-start.4
  68.0 1.1 %copy-start.7 = (f32[128,1152]{1,0:T(8,128)S(1)}, f32[128,1152]{1,0:T(8,128)}, u32[]{:S(2)}) copy-start(f32[128,1152]{1,0:T(8,128)} %copy-done.6) | copy-start | bytes 1769476
  69.1 1.1 %copy-start.9 = (f32[128,1152]{1,0:T(8,128)S(1)}, f32[128,1152]{1,0:T(8,128)}, u32[]{:S(2)}) copy-start(f32[128,1152]{1,0:T(8,128)} %copy-done.8) | copy-start | bytes 1769476
  70.2 1.1 %copy-start.11 = (f32[128,1152]{1,0:T(8,128)S(1)}, f32[128,1152]{1,0:T(8,128)}, u32[]{:S(2)}) copy-start(f32[128,1152]{1,0:T(8,128)} %copy-done.10) | copy-start | bytes 1769476
  71.2 1.1 %copy-start.13 = (f32[128,1152]{1,0:T(8,128)S(1)}, f32[128,1152]{1,0:T(8,128)}, u32[]{:S(2)}) copy-start(f32[128,1152]{1,0:T(8,128)} %copy-done.12) | copy-start | bytes 1769476
  72.3 1.1 %copy-start.15 = (f32[128,1152]{1,0:T(8,128)S(1)}, f32[128,1152]{1,0:T(8,128)}, u32[]{:S(2)}) copy-start(f32[128,1152]{1,0:T(8,128)} %copy-done.14) | copy-start | bytes 1769476
  76.5 23.0 %collective-permute-start.6 = (bf16[256,1152]{1,0:T(8,128)(2,1)}, bf16[256,1152]{1,0:T(8,128)(2,1)S(1)}, u32[]{:S(2)}, u32[]{:S(2)}) collective-permute-start(bf16[256,1152]{1,0:T(8,128)(2,1)} %get-tuple-element.40), channel_id=1, source_target_pairs={{0,128},{64,192},{128,256},{192,320},{256,384},{320,448},{384,512}... | collective-permute-start | bytes 1769480 | tf_op jit(solution)/shard_map/ppermute | solution.py:271
  78.4 21.1 %collective-permute-start.7 = (bf16[256,1152]{1,0:T(8,128)(2,1)}, bf16[256,1152]{1,0:T(8,128)(2,1)S(1)}, u32[]{:S(2)}, u32[]{:S(2)}) collective-permute-start(bf16[256,1152]{1,0:T(8,128)(2,1)} %get-tuple-element.41), channel_id=1, source_target_pairs={{0,896},{64,960},{128,0},{192,64},{256,128},{320,192},{384,256},{4... | collective-permute-start | bytes 1769480 | tf_op jit(solution)/shard_map/ppermute | solution.py:271
  83.0 16.5 %copy-start.2 = (bf16[128,1152]{1,0:T(8,128)(2,1)S(1)}, bf16[128,1152]{1,0:T(8,128)(2,1)}, u32[]{:S(2)}) copy-start(bf16[128,1152]{1,0:T(8,128)(2,1)} %text_ref.3) | copy-start | bytes 884740
  (2 other events, 1.6 us)

commit v6 on v5

--- a/solution.py
+++ b/solution.py
@@ -11,6 +11,7 @@
 SMEM = pl.BlockSpec(memory_space=pltpu.SMEM)
 F32 = jnp.float32
 BF16 = jnp.bfloat16
+HBM = pl.BlockSpec(memory_space=pltpu.HBM)
 PARAMS = pltpu.CompilerParams(vmem_limit_bytes=16 * 1024 * 1024)
 
 
@@ -132,9 +133,9 @@
 def early_kernel(
     scal_ref, place_ref, label_ref, own_ref, after_ref, before_ref, cross_ref,
     image_in_ref, text_in_ref, sums_in_ref,
-    image_total_ref, text_total_ref, far_ref, down_ref, up_ref, sums_ref,
+    image_total_ref, text_total_ref, far_g_ref, sums_ref,
 ):
-    width = cross_ref.shape[1]
+    rows, width = cross_ref.shape
     scorer = Scorer(scal_ref, label_ref, place_ref)
     side = scorer.side()
     even = side == 1
@@ -155,14 +156,13 @@
     tb = scorer.grads(ub, v, wb, col_b, row, False)
     image_total_ref[...] = image_in_ref[...] + matmul(ga, va) + matmul(gb, vb)
     text_total_ref[...] = text_in_ref[...] + t_matmul(ta, ua) + t_matmul(tb, ub)
-    far_ref[...] = matmul(gx, vc)
-    down_ref[...] = matmul(gfar, va)
-    up_ref[...] = t_matmul(gfar, ub)
+    far_g_ref[:rows, :] = gx
+    far_g_ref[rows:, :] = gfar
     scorer.store_sums(sums_ref, sums_in_ref)
 
 
 def relay_kernel(
-    scal_ref, place_ref, label_ref, own_ref, after_ref, before_ref, relay_ref, early_ref,
+    scal_ref, place_ref, label_ref, own_ref, after_ref, before_ref, relay_ref, early_ref, far_in_ref,
     near_ref, far_ref, sums_ref,
 ):
     width = relay_ref.shape[1]
@@ -176,7 +176,9 @@
     near_ref[...] = scorer.grads(own_ref[:, :width], vr, weight_of(own_ref, width), col, row_r, True)
     ux = jnp.where(even, after_ref[:, :width], before_ref[:, :width])
     wx = jnp.where(even, weight_of(after_ref, width), weight_of(before_ref, width))
-    far_ref[...] = scorer.grads(ux, vr, wx, col_x, row_r, True)
+    rows = relay_ref.shape[0]
+    far_ref[:rows, :] = scorer.grads(ux, vr, wx, col_x, row_r, True)
+    far_ref[rows:, :] = far_in_ref[...]
     lane = lax.broadcasted_iota(jnp.int32, (1, 128), 1)
     message = jnp.zeros((1, 128), F32)
     for at in range(3):
@@ -186,36 +188,57 @@
 
 
 def late_kernel(
-    scal_ref, place_ref, label_ref, own_ref, after_ref, before_ref, cross_ref, relay_ref, relay_v_ref,
-    near_ref, far_g_ref, far_ref, down_in_ref, up_in_ref, image_in_ref, text_in_ref,
-    up_ref, down_ref, image_total_ref, text_total_ref,
+    scal_ref, place_ref, label_any, own_any, after_any, before_any, cross_any, relay_any, relay_v_any,
+    far_g_any, cross_v_any,
+    to_up_ref, to_down_ref, cross_g_ref, relay_g_ref,
+    label_ref, v_ref, va_ref, before_ref, cross_ref, relay_ref, relay_v_ref, far_g_ref, cross_v_ref,
+    sems,
 ):
-    width = relay_v_ref.shape[1]
-    rows = relay_v_ref.shape[0]
+    rows, width = relay_v_ref.shape
+    text_part = (slice(None), pl.ds(width + 128, width))
+    copies = [
+        pltpu.make_async_copy(source, target, sems.at[at])
+        for at, (source, target) in enumerate((
+            (label_any, label_ref),
+            (cross_any, cross_ref),
+            (before_any, before_ref),
+            (after_any.at[text_part], va_ref),
+            (own_any.at[text_part], v_ref),
+            (relay_any, relay_ref),
+            (far_g_any, far_g_ref),
+            (relay_v_any, relay_v_ref),
+            (cross_v_any, cross_v_ref),
+        ))
+    ]
+    for copy in copies:
+        copy.start()
+    for copy in copies[:5]:
+        copy.wait()
     scorer = Scorer(scal_ref, label_ref, place_ref)
     side = scorer.side()
     even = side == 1
-    v = own_ref[:, width + 128 :]
-    va, vb = after_ref[:, width + 128 :], before_ref[:, width + 128 :]
-    uc, ur = cross_ref[:, :width], relay_ref[:, :width]
-    wc, wr = weight_of(cross_ref, width), weight_of(relay_ref, width)
+    v, va, vb = v_ref[...], va_ref[...], before_ref[:, width + 128 :]
+    uc = cross_ref[:, :width]
+    wc = weight_of(cross_ref, width)
     col_c = as_column(scorer.label_row(side).astype(F32))
     col_r = as_column(scorer.label_row(-side).astype(F32))
     row, row_a, row_b = scorer.label_row(0), scorer.label_row(2), scorer.label_row(-2)
     gcx = scorer.grads(uc, jnp.where(even, vb, va), wc, col_c, jnp.where(even, row_b, row_a), False)
+    gc = scorer.grads(uc, v, wc, col_c, row, False)
+    for copy in copies[5:]:
+        copy.wait()
+    ur, wr = relay_ref[:, :width], weight_of(relay_ref, width)
     grx = scorer.grads(ur, jnp.where(even, va, vb), wr, col_r, jnp.where(even, row_a, row_b), False)
-    far_text_c = t_matmul(gcx, uc)
-    far_text_r = t_matmul(grx, ur)
-    far_image_c = far_ref[...]
-    far_image_r = matmul(far_g_ref[...], relay_v_ref[...])
-    up_ref[:rows, :] = jnp.where(even, far_image_r, far_image_c).astype(BF16)
-    up_ref[rows:, :] = (up_in_ref[...] + jnp.where(even, far_text_r, far_text_c)).astype(BF16)
-    down_ref[:rows, :] = (down_in_ref[...] + jnp.where(even, far_image_c, far_image_r)).astype(BF16)
-    down_ref[rows:, :] = jnp.where(even, far_text_c, far_text_r).astype(BF16)
-    gc = scorer.grads(uc, v, wc, col_c, row, False)
     gr = scorer.grads(ur, v, wr, col_r, row, False)
-    image_total_ref[...] = image_in_ref[...] + matmul(near_ref[...], relay_v_ref[...])
-    text_total_ref[...] = text_in_ref[...] + t_matmul(gc, uc) + t_matmul(gr, ur)
+    far_text_c, far_text_r = t_matmul(gcx, uc), t_matmul(grx, ur)
+    far_image_r = matmul(far_g_ref[:rows, :], relay_v_ref[...])
+    far_image_c = matmul(far_g_ref[rows : 2 * rows, :], cross_v_ref[...])
+    g = far_g_ref[2 * rows :, :]
+    to_up_ref[:rows, :] = jnp.where(even, far_image_r, far_image_c).astype(BF16)
+    to_up_ref[rows:, :] = (t_matmul(g, before_ref[:, :width]) + jnp.where(even, far_text_r, far_text_c)).astype(BF16)
+    to_down_ref[:rows, :] = (matmul(g, va) + jnp.where(even, far_image_c, far_image_r)).astype(BF16)
+    to_down_ref[rows:, :] = jnp.where(even, far_text_c, far_text_r).astype(BF16)
+    cross_g_ref[...], relay_g_ref[...] = gc, gr
 
 
 def middle_kernel(got_ref, sums_ref):
@@ -223,16 +246,19 @@
 
 
 def final_kernel(
-    count, scal_ref, image_ref, text_ref, image_total_ref, text_total_ref, up_ref, down_ref, got_ref,
+    count, scal_ref, image_ref, text_ref, image_total_ref, text_total_ref, near_g_ref, relay_v_ref,
+    cross_g_ref, cross_ref, relay_g_ref, relay_ref, up_ref, down_ref, got_ref,
     image_grad_ref, text_grad_ref, stats_ref,
 ):
     rows, width = image_ref.shape
     temper = jnp.exp(jnp.full((1, 128), scal_ref[0], F32))[:, :1]
-    for raw_ref, total_ref, out_ref, at in (
-        (image_ref, image_total_ref, image_grad_ref, 0),
-        (text_ref, text_total_ref, text_grad_ref, rows),
+    image_more = matmul(near_g_ref[...], relay_v_ref[...])
+    text_more = t_matmul(cross_g_ref[...], cross_ref[:, :width]) + t_matmul(relay_g_ref[...], relay_ref[:, :width])
+    for raw_ref, total_ref, more, out_ref, at in (
+        (image_ref, image_total_ref, image_more, image_grad_ref, 0),
+        (text_ref, text_total_ref, text_more, text_grad_ref, rows),
     ):
-        total = total_ref[...] + up_ref[at : at + rows, :].astype(F32) + down_ref[at : at + rows, :].astype(F32)
+        total = total_ref[...] + more + up_ref[at : at + rows, :].astype(F32) + down_ref[at : at + rows, :].astype(F32)
         unit, scale = normalize(raw_ref[...])
         out_ref[...] = norm_back(unit, scale, temper * total).astype(BF16)
     got = jnp.sum(got_ref[...], axis=0, keepdims=True) / count
@@ -240,12 +266,13 @@
         stats_ref[at] = got[0, at]
 
 
-def call(kernel, ins, outs, name, work, out_specs=None):
+def call(kernel, ins, outs, name, work, out_specs=None, scratch=()):
     return pl.pallas_call(
         kernel,
         out_shape=outs,
         in_specs=ins,
         out_specs=jax.tree.map(lambda _: VMEM, outs) if out_specs is None else out_specs,
+        scratch_shapes=scratch,
         compiler_params=PARAMS,
         cost_estimate=pl.CostEstimate(flops=work, bytes_accessed=0, transcendentals=0),
         name=name,
@@ -299,25 +326,29 @@
     image_total, text_total, sums = call(
         own_kernel, head + [VMEM] * 2, (block,) * 2 + (shape(8, 128, F32),), "own", 150 * dot
     )(scal, place, labels, both, cross_v)
-    image_total, text_total, far, far_down, far_up, sums = call(
-        early_kernel, head + [VMEM] * 7, (block,) * 5 + (shape(8, 128, F32),), "early", 20 * dot
+    image_total, text_total, far_g, sums = call(
+        early_kernel, head + [VMEM] * 7, (block, block, shape(2 * rows, rows, BF16), shape(8, 128, F32)), "early", 20 * dot
     )(scal, place, labels, both, after, before, cross_v, image_total, text_total, sums)
     cross_u, sums = lax.optimization_barrier((cross_u, sums))
     relay_u = relayed(cross_u)
     near_g, far_g, sums = call(
-        relay_kernel, head + [VMEM] * 5, (shape(rows, rows, BF16),) * 2 + (shape(1, 128, F32),), "relay", 10 * dot
-    )(scal, place, labels, both, after, before, relay_v, sums)
+        relay_kernel,
+        head + [VMEM] * 6,
+        (shape(rows, rows, BF16), shape(3 * rows, rows, BF16), shape(1, 128, F32)),
+        "relay", 10 * dot
+    )(scal, place, labels, both, after, before, relay_v, sums, far_g)
     got = exchanged(sums, "group")
-    to_up, to_down, image_total, text_total = call(
+    half, pack = pltpu.VMEM((rows, width), BF16), pltpu.VMEM((rows, width + 128), BF16)
+    scratch = [pltpu.VMEM(labels.shape, jnp.int32), half, half, pltpu.VMEM(both.shape, BF16), pack, pack, half]
+    scratch += [pltpu.VMEM((3 * rows, rows), BF16), half]
+    to_up, to_down, cross_g, relay_g = call(
         late_kernel,
-        head + [VMEM] * 13,
-        (shape(2 * rows, width, BF16),) * 2 + (block,) * 2,
+        [SMEM, SMEM] + [HBM] * 9,
+        (shape(2 * rows, width, BF16),) * 2 + (shape(rows, rows, BF16),) * 2,
         "late",
         400 * dot,
-    )(
-        scal, place, labels, both, after, before, cross_u, relay_u, relay_v,
-        near_g, far_g, far, far_down, far_up, image_total, text_total,
-    )
+        scratch=scratch + [pltpu.SemaphoreType.DMA((9,))],
+    )(scal, place, labels, both, after, before, cross_u, relay_u, relay_v, far_g, cross_v)
     from_below = upward(to_up)
     from_above = downward(to_down)
     sums = call(middle_kernel, [VMEM], shape(1, 128, F32), "middle", 300 * dot)(got)
@@ -325,12 +356,15 @@
     count = float(cycle * groups * rows) * float(rows) * 8.0
     image_grad, text_grad, stats = call(
         functools.partial(final_kernel, count),
-        [SMEM] + [VMEM] * 7,
+        [SMEM] + [VMEM] * 13,
         (shape(rows, width, BF16),) * 2 + (jax.ShapeDtypeStruct((3,), F32),),
         "final",
         10 * dot,
         (VMEM, VMEM, SMEM),
-    )(scal, images, texts, image_total, text_total, from_below, from_above, got)
+    )(
+        scal, images, texts, image_total, text_total, near_g, relay_v, cross_g, cross_u, relay_g, relay_u,
+        from_below, from_above, got,
+    )
     return image_grad, text_grad, stats
 
 

time: 103 us -> 99.8 us (0.969)
  local copies, waits for them, and re-layouts: 9.6 us -> 3.21 us
  Pallas kernels: 10.4 us -> 12.5 us
    unnamed x34 -> x16, local copies, waits for them, and re-layouts: 8.96 us -> 2.57 us
    pallas_call x4, Pallas kernels: 8.03 us -> 9.69 us  [the longest x1 3.88 us: per_device(): call(late_kernel, [SMEM, SMEM] + [HBM] * 9, (shape(2 * rows, width, BF16)...]
  transfers between devices with their start and end apart: 9 -> 9, of which waited for: 4 -> 4; matrix products, arithmetic and copies ran while one was open for 1% -> 1% of each run, Pallas kernels for 8% -> 10%
where the time goes in v6:
time: 99.8 us; the launch traced here: 98.2 us
  starting transfers between devices  51 us (51%)
  blocking collectives  17.1 us (17%)
  Pallas kernels  12.5 us (13%)
  waiting for transfers between devices  12.2 us (12%)
  local copies, waits for them, and re-layouts  3.21 us (3%)
  between operations  2.13 us (2%)
    ppermute x8, starting transfers between devices, passed(): lax.ppermute(value, 'blk', [(p, (p + step_of(p)) % cycle) for p in range(...  40.1 us
    all_to_all x1, blocking collectives, exchanged(): return lax.all_to_all(sent, axis, 0, 0).reshape(count, 128)  17.1 us
    ppermute x8, waiting for transfers between devices, passed(): lax.ppermute(value, 'blk', [(p, (p + step_of(p)) % cycle) for p in range(...  12.2 us
    all_to_all x1, starting transfers between devices, exchanged(): return lax.all_to_all(sent, axis, 0, 0).reshape(count, 128)  10.9 us
    pallas_call x1, Pallas kernels, per_device(): call(late_kernel, [SMEM, SMEM] + [HBM] * 9, (shape(2 * rows, width, BF16)...  3.88 us
    pallas_call x1, Pallas kernels, per_device(): call(functools.partial(final_kernel, count), [SMEM] + [VMEM] * 13, (shape...  2.61 us
    unnamed x16, local copies, waits for them, and re-layouts  2.57 us
    pallas_call x1, Pallas kernels, per_device(): call(early_kernel, head + [VMEM] * 7, (block, block, shape(2 * rows, rows...  2.16 us
  transfers between devices with their start and end apart: 9, of which 4 were waited for; matrix products, arithmetic and copies ran while one was open for 1% of the time, Pallas kernels for 10%

profile of v6, /device:TPU:1, one launch (start us, length us, event | category | flops | bytes accessed | tf_op | source)
XLA Modules:
  0.0 98.2 jit_solution(17550790068440918915)
XLA Ops:
  0.7 1.0 %copy-done.2 = bf16[128,1152]{1,0:T(8,128)(2,1)S(1)} copy-done((bf16[128,1152]{1,0:T(8,128)(2,1)S(1)}, bf16[128,1152]{1,0:T(8,128)(2,1)}, u32[]{:S(2)}) %copy-start.2) | copy-done | bytes 294936
  1.8 8.7 %collective-permute-start.2 = (bf16[128,1152]{1,0:T(8,128)(2,1)S(1)}, bf16[128,1152]{1,0:T(8,128)(2,1)}, u32[]{:S(2)}, u32[]{:S(2)}) collective-permute-start(bf16[128,1152]{1,0:T(8,128)(2,1)S(1)} %text.1.text_unit_ref), channel_id=1, source_target_pairs={{0,64},{64,0},{128,192},{192,128},{256,320},{320,256},{384,448},{4... | collective-permute-start | bytes 884744 | tf_op jit(solution)/shard_map/ppermute | solution.py:298
  10.6 0.9 image.1
  11.5 17.2 %collective-permute-start = (bf16[128,2432]{1,0:T(8,128)(2,1)S(1)}, bf16[128,2432]{1,0:T(8,128)(2,1)S(1)}, u32[]{:S(2)}, u32[]{:S(2)}) collective-permute-start(bf16[128,2432]{1,0:T(8,128)(2,1)S(1)} %get-tuple-element.21.own_ref.own_any), channel_id=1, source_target_pairs={{0,896},{64,960},{128,0},{192,64},{256,128},{320,192},{384,256},{4... | collective-permute-start | bytes 1867784 | tf_op jit(solution)/shard_map/ppermute | solution.py:298
  28.7 1.9 %collective-permute-start.1 = (bf16[128,2432]{1,0:T(8,128)(2,1)S(1)}, bf16[128,2432]{1,0:T(8,128)(2,1)S(1)}, u32[]{:S(2)}, u32[]{:S(2)}) collective-permute-start(bf16[128,2432]{1,0:T(8,128)(2,1)S(1)} %get-tuple-element.21.own_ref.own_any), channel_id=1, source_target_pairs={{0,128},{64,192},{128,256},{192,320},{256,384},{320,448},{384,512}... | collective-permute-start | bytes 1867784 | tf_op jit(solution)/shard_map/ppermute | solution.py:298
  30.6 1.9 %collective-permute-start.4 = (bf16[128,1280]{1,0:T(8,128)(2,1)}, bf16[128,1280]{1,0:T(8,128)(2,1)}, u32[]{:S(2)}, u32[]{:S(2)}) collective-permute-start(bf16[128,1280]{1,0:T(8,128)(2,1)} %get-tuple-element.27), channel_id=1, source_target_pairs={{0,64},{64,0},{128,192},{192,128},{256,320},{320,256},{384,448},{4... | collective-permute-start | bytes 983048 | tf_op jit(solution)/shard_map/ppermute | solution.py:298
  33.9 1.9 %collective-permute-start.3 = (bf16[128,1152]{1,0:T(8,128)(2,1)}, bf16[128,1152]{1,0:T(8,128)(2,1)S(1)}, u32[]{:S(2)}, u32[]{:S(2)}) collective-permute-start(bf16[128,1152]{1,0:T(8,128)(2,1)} %collective-permute-done.2.cross_ref.cross_v_any), channel_id=1, source_target_pairs={{0,128},{64,960},{128,256},{192,64},{256,384},{320,192},{384,512},... | collective-permute-start | bytes 884744 | tf_op jit(solution)/shard_map/ppermute | solution.py:298
  35.8 1.8 %own.1 = (f32[128,1152]{1,0:T(8,128)S(1)}, f32[128,1152]{1,0:T(8,128)S(1)}, f32[8,128]{1,0:T(8,128)S(1)}) custom-call(f32[2]{0:T(128)S(1)} %pad_maximum_fusion.scal_ref, s32[1]{0:T(128)} %bitcast.place_ref, s32[16,128]{1,0:T(8,128)S(1)} %copy-done.4, bf16[128,2432]{1,0:T(8,128)(2,1)S(1)} %get-tuple-element.21.own_ref.own_any, ...), custom_call_target="tpu_custom_call" | custom-call | flops 5662310400 | tf_op jit(solution)/shard_map/own/pallas_call | solution.py:326
  37.6 3.4 %collective-permute-done.after_ref.after_any = bf16[128,2432]{1,0:T(8,128)(2,1)S(1)} collective-permute-done((bf16[128,2432]{1,0:T(8,128)(2,1)S(1)}, bf16[128,2432]{1,0:T(8,128)(2,1)S(1)}, u32[]{:S(2)}, u32[]{:S(2)}) %collective-permute-start) | collective-permute-done | bytes 622624 | tf_op jit(solution)/shard_map/ppermute | solution.py:298
  41.0 5.1 %collective-permute-done.1.before_ref.before_any = bf16[128,2432]{1,0:T(8,128)(2,1)S(1)} collective-permute-done((bf16[128,2432]{1,0:T(8,128)(2,1)S(1)}, bf16[128,2432]{1,0:T(8,128)(2,1)S(1)}, u32[]{:S(2)}, u32[]{:S(2)}) %collective-permute-start.1) | collective-permute-done | bytes 622624 | tf_op jit(solution)/shard_map/ppermute | solution.py:298
  46.1 2.2 %early.1 = (f32[128,1152]{1,0:T(8,128)S(1)}, f32[128,1152]{1,0:T(8,128)S(1)}, bf16[256,128]{1,0:T(8,128)(2,1)S(1)}, f32[8,128]{1,0:T(8,128)S(1)}) custom-call(f32[2]{0:T(128)S(1)} %pad_maximum_fusion.scal_ref, s32[1]{0:T(128)} %bitcast.place_ref, s32[16,128]{1,0:T(8,128)S(1)} %copy-done.4, bf16[128,2432]{1,0:T(8,128)(2,1)S(1)} %get-tuple-element.21.own_ref.own_any, ...), custom_call_target="tpu_custom_call" | custom-call | flops 754974720 | tf_op jit(solution)/shard_map/early/pallas_call | solution.py:329
  48.3 1.9 %collective-permute-start.5 = (bf16[128,1280]{1,0:T(8,128)(2,1)}, bf16[128,1280]{1,0:T(8,128)(2,1)}, u32[]{:S(2)}, u32[]{:S(2)}) collective-permute-start(bf16[128,1280]{1,0:T(8,128)(2,1)} %collective-permute-done.4.cross_any.cross_ref), channel_id=1, source_target_pairs={{0,128},{64,960},{128,256},{192,64},{256,384},{320,192},{384,512},... | collective-permute-start | bytes 983048 | tf_op jit(solution)/shard_map/ppermute | solution.py:298
  50.3 2.2 %collective-permute-done.3.relay_ref.relay_v_any.relay_v_ref = bf16[128,1152]{1,0:T(8,128)(2,1)S(1)} collective-permute-done((bf16[128,1152]{1,0:T(8,128)(2,1)}, bf16[128,1152]{1,0:T(8,128)(2,1)S(1)}, u32[]{:S(2)}, u32[]{:S(2)}) %collective-permute-start.3) | collective-permute-done | bytes 294944 | tf_op jit(solution)/shard_map/ppermute | solution.py:298
  52.5 1.0 %relay.1 = (bf16[128,128]{1,0:T(8,128)(2,1)S(1)}, bf16[384,128]{1,0:T(8,128)(2,1)S(1)}, f32[1,128]{1,0:T(1,128)S(1)}) custom-call(f32[2]{0:T(128)S(1)} %pad_maximum_fusion.scal_ref, s32[1]{0:T(128)} %bitcast.place_ref, s32[16,128]{1,0:T(8,128)S(1)} %copy-done.4, bf16[128,2432]{1,0:T(8,128)(2,1)S(1)} %get-tuple-element.21.own_ref.own_any, ...), custom_call_target="tpu_custom_call" | custom-call | flops 377487360 | tf_op jit(solution)/shard_map/relay/pallas_call | solution.py:334
  53.5 0.6 copy-done.5
  54.1 0.6 broadcast_in_dim.15
  54.8 10.9 %all-to-all-start = ((f32[64,1,128]{2,1,0:T(1,128)}), f32[64,1,128]{2,1,0:T(1,128)S(1)}, u32[]{:S(2)}, u32[]{:S(2)}) async-start(f32[64,1,128]{2,1,0:T(1,128)} %broadcast_in_dim.15), calls=%async_computation | async-start | bytes 65536 | tf_op jit(solution)/shard_map/all_to_all | solution.py:285
  65.7 1.4 %collective-permute-done.5.relay_any.relay_ref = bf16[128,1280]{1,0:T(8,128)(2,1)} collective-permute-done((bf16[128,1280]{1,0:T(8,128)(2,1)}, bf16[128,1280]{1,0:T(8,128)(2,1)}, u32[]{:S(2)}, u32[]{:S(2)}) %collective-permute-start.5) | collective-permute-done | bytes 327712 | tf_op jit(solution)/shard_map/ppermute | solution.py:298
  67.1 0.9 copy-done.6
  68.0 3.9 %late.1 = (bf16[256,1152]{1,0:T(8,128)(2,1)}, bf16[256,1152]{1,0:T(8,128)(2,1)}, bf16[128,128]{1,0:T(8,128)(2,1)S(1)}, bf16[128,128]{1,0:T(8,128)(2,1)S(1)}) custom-call(f32[2]{0:T(128)S(1)} %pad_maximum_fusion.scal_ref, s32[1]{0:T(128)} %bitcast.place_ref, s32[16,128]{1,0:T(8,128)S(1)} %copy-done.4, ...), custom_call_target="tpu_custom_call" | custom-call | flops 15099494400 | tf_op jit(solution)/shard_map/late/pallas_call | solution.py:344
  71.9 1.9 %collective-permute-start.6 = (bf16[256,1152]{1,0:T(8,128)(2,1)}, bf16[256,1152]{1,0:T(8,128)(2,1)S(1)}, u32[]{:S(2)}, u32[]{:S(2)}) collective-permute-start(bf16[256,1152]{1,0:T(8,128)(2,1)} %get-tuple-element.36), channel_id=1, source_target_pairs={{0,128},{64,192},{128,256},{192,320},{256,384},{320,448},{384,512}... | collective-permute-start | bytes 1769480 | tf_op jit(solution)/shard_map/ppermute | solution.py:298
  73.8 4.6 %collective-permute-start.7 = (bf16[256,1152]{1,0:T(8,128)(2,1)}, bf16[256,1152]{1,0:T(8,128)(2,1)S(1)}, u32[]{:S(2)}, u32[]{:S(2)}) collective-permute-start(bf16[256,1152]{1,0:T(8,128)(2,1)} %get-tuple-element.37), channel_id=1, source_target_pairs={{0,896},{64,960},{128,0},{192,64},{256,128},{320,192},{384,256},{4... | collective-permute-start | bytes 1769480 | tf_op jit(solution)/shard_map/ppermute | solution.py:298
  78.4 17.1 %all_to_all.10 = f32[16,1,128]{2,1,0:T(1,128)S(1)} all-to-all(f32[16,1,128]{2,1,0:T(1,128)S(1)} %broadcast_in_dim.17), channel_id=1, replica_groups=mesh['blk'=16,'group'=64] {'blk'}, dimensions={0} | all-to-all | bytes 16384 | tf_op jit(solution)/shard_map/all_to_all | solution.py:285
  95.6 2.6 %final.1 = (bf16[128,1152]{1,0:T(8,128)(2,1)}, bf16[128,1152]{1,0:T(8,128)(2,1)}, f32[3]{0:T(128)}) custom-call(f32[2]{0:T(128)S(1)} %pad_maximum_fusion.scal_ref, bf16[128,1152]{1,0:T(8,128)(2,1)S(1)} %copy-done.1, bf16[128,1152]{1,0:T(8,128)(2,1)S(1)} %copy-done.3, f32[128,1152]{1,0:T(8,128)S(1)} %get-tuple-element.25.image_total_ref, ...), custom_call_target="tpu_custom_call" | custom-call | flops 377487360 | tf_op jit(solution)/shard_map/final/pallas_call | solution.py:357
  (22 shorter events, 0.3 us)
Async XLA Ops:
  0.6 9.9 %copy-start = (bf16[128,1152]{1,0:T(8,128)(2,1)S(1)}, bf16[128,1152]{1,0:T(8,128)(2,1)}, u32[]{:S(2)}) copy-start(bf16[128,1152]{1,0:T(8,128)(2,1)} %image_ref.3) | copy-start | bytes 884740
  0.6 1.0 %copy-start.2 = (bf16[128,1152]{1,0:T(8,128)(2,1)S(1)}, bf16[128,1152]{1,0:T(8,128)(2,1)}, u32[]{:S(2)}) copy-start(bf16[128,1152]{1,0:T(8,128)(2,1)} %text_ref.3) | copy-start | bytes 884740
  1.8 8.8 %copy-start.7 = (f32[128]{0:T(128)S(1)}, f32[128]{0:T(128)}, u32[]{:S(2)}) copy-start(f32[128]{0:T(128)} %param.9) | copy-start | bytes 1540
  1.8 32.1 %collective-permute-start.2 = (bf16[128,1152]{1,0:T(8,128)(2,1)S(1)}, bf16[128,1152]{1,0:T(8,128)(2,1)}, u32[]{:S(2)}, u32[]{:S(2)}) collective-permute-start(bf16[128,1152]{1,0:T(8,128)(2,1)S(1)} %text.1.text_unit_ref), channel_id=1, source_target_pairs={{0,64},{64,0},{128,192},{192,128},{256,320},{320,256},{384,448},{4... | collective-permute-start | bytes 884744 | tf_op jit(solution)/shard_map/ppermute | solution.py:298
  11.5 29.5 %collective-permute-start = (bf16[128,2432]{1,0:T(8,128)(2,1)S(1)}, bf16[128,2432]{1,0:T(8,128)(2,1)S(1)}, u32[]{:S(2)}, u32[]{:S(2)}) collective-permute-start(bf16[128,2432]{1,0:T(8,128)(2,1)S(1)} %get-tuple-element.21.own_ref.own_any), channel_id=1, source_target_pairs={{0,896},{64,960},{128,0},{192,64},{256,128},{320,192},{384,256},{4... | collective-permute-start | bytes 1867784 | tf_op jit(solution)/shard_map/ppermute | solution.py:298
  28.7 17.5 %collective-permute-start.1 = (bf16[128,2432]{1,0:T(8,128)(2,1)S(1)}, bf16[128,2432]{1,0:T(8,128)(2,1)S(1)}, u32[]{:S(2)}, u32[]{:S(2)}) collective-permute-start(bf16[128,2432]{1,0:T(8,128)(2,1)S(1)} %get-tuple-element.21.own_ref.own_any), channel_id=1, source_target_pairs={{0,128},{64,192},{128,256},{192,320},{256,384},{320,448},{384,512}... | collective-permute-start | bytes 1867784 | tf_op jit(solution)/shard_map/ppermute | solution.py:298
  30.6 5.2 %copy-start.4 = (s32[16,128]{1,0:T(8,128)S(1)}, s32[16,128]{1,0:T(8,128)}, u32[]{:S(2)}) copy-start(s32[16,128]{1,0:T(8,128)} %label_any.1) | copy-start | bytes 24580
  30.6 17.7 %collective-permute-start.4 = (bf16[128,1280]{1,0:T(8,128)(2,1)}, bf16[128,1280]{1,0:T(8,128)(2,1)}, u32[]{:S(2)}, u32[]{:S(2)}) collective-permute-start(bf16[128,1280]{1,0:T(8,128)(2,1)} %get-tuple-element.27), channel_id=1, source_target_pairs={{0,64},{64,0},{128,192},{192,128},{256,320},{320,256},{384,448},{4... | collective-permute-start | bytes 983048 | tf_op jit(solution)/shard_map/ppermute | solution.py:298
  33.9 18.6 %collective-permute-start.3 = (bf16[128,1152]{1,0:T(8,128)(2,1)}, bf16[128,1152]{1,0:T(8,128)(2,1)S(1)}, u32[]{:S(2)}, u32[]{:S(2)}) collective-permute-start(bf16[128,1152]{1,0:T(8,128)(2,1)} %collective-permute-done.2.cross_ref.cross_v_any), channel_id=1, source_target_pairs={{0,128},{64,960},{128,256},{192,64},{256,384},{320,192},{384,512},... | collective-permute-start | bytes 884744 | tf_op jit(solution)/shard_map/ppermute | solution.py:298
  48.3 18.8 %collective-permute-start.5 = (bf16[128,1280]{1,0:T(8,128)(2,1)}, bf16[128,1280]{1,0:T(8,128)(2,1)}, u32[]{:S(2)}, u32[]{:S(2)}) collective-permute-start(bf16[128,1280]{1,0:T(8,128)(2,1)} %collective-permute-done.4.cross_any.cross_ref), channel_id=1, source_target_pairs={{0,128},{64,960},{128,256},{192,64},{256,384},{320,192},{384,512},... | collective-permute-start | bytes 983048 | tf_op jit(solution)/shard_map/ppermute | solution.py:298
  53.5 0.6 copy-start.5
  54.8 23.6 %all-to-all-start = ((f32[64,1,128]{2,1,0:T(1,128)}), f32[64,1,128]{2,1,0:T(1,128)S(1)}, u32[]{:S(2)}, u32[]{:S(2)}) async-start(f32[64,1,128]{2,1,0:T(1,128)} %broadcast_in_dim.15), calls=%async_computation | async-start | bytes 65536 | tf_op jit(solution)/shard_map/all_to_all | solution.py:285
  67.1 0.9 copy-start.6
  71.9 23.7 %collective-permute-start.6 = (bf16[256,1152]{1,0:T(8,128)(2,1)}, bf16[256,1152]{1,0:T(8,128)(2,1)S(1)}, u32[]{:S(2)}, u32[]{:S(2)}) collective-permute-start(bf16[256,1152]{1,0:T(8,128)(2,1)} %get-tuple-element.36), channel_id=1, source_target_pairs={{0,128},{64,192},{128,256},{192,320},{256,384},{320,448},{384,512}... | collective-permute-start | bytes 1769480 | tf_op jit(solution)/shard_map/ppermute | solution.py:298
  73.8 21.8 %collective-permute-start.7 = (bf16[256,1152]{1,0:T(8,128)(2,1)}, bf16[256,1152]{1,0:T(8,128)(2,1)S(1)}, u32[]{:S(2)}, u32[]{:S(2)}) collective-permute-start(bf16[256,1152]{1,0:T(8,128)(2,1)} %get-tuple-element.37), channel_id=1, source_target_pairs={{0,896},{64,960},{128,0},{192,64},{256,128},{320,192},{384,256},{4... | collective-permute-start | bytes 1769480 | tf_op jit(solution)/shard_map/ppermute | solution.py:298
  78.4 17.2 %copy-start.1 = (bf16[128,1152]{1,0:T(8,128)(2,1)S(1)}, bf16[128,1152]{1,0:T(8,128)(2,1)}, u32[]{:S(2)}) copy-start(bf16[128,1152]{1,0:T(8,128)(2,1)} %image_ref.3) | copy-start | bytes 884740
  78.4 17.2 %copy-start.3 = (bf16[128,1152]{1,0:T(8,128)(2,1)S(1)}, bf16[128,1152]{1,0:T(8,128)(2,1)}, u32[]{:S(2)}) copy-start(bf16[128,1152]{1,0:T(8,128)(2,1)} %text_ref.3) | copy-start | bytes 884740

commit v7 on v4

--- a/solution.py
+++ b/solution.py
@@ -11,6 +11,7 @@
 SMEM = pl.BlockSpec(memory_space=pltpu.SMEM)
 F32 = jnp.float32
 BF16 = jnp.bfloat16
+HBM = pl.BlockSpec(memory_space=pltpu.HBM)
 PARAMS = pltpu.CompilerParams(vmem_limit_bytes=16 * 1024 * 1024)
 
 
@@ -162,15 +163,15 @@
     image_far, text_far = matmul(gfar, va), t_matmul(gfar, ub)
     near_ref[:rows, :] = (matmul(gx, vc) + jnp.where(even, image_far, 0.0)).astype(BF16)
     near_ref[rows:, :] = jnp.where(even, 0.0, text_far).astype(BF16)
-    image_far_ref[...] = jnp.where(even, 0.0, image_far)
+    image_far_ref[...] = jnp.where(even, 0.0, image_far).astype(BF16)
     text_far_ref[...] = jnp.where(even, text_far, 0.0).astype(BF16)
     scorer.store_sums(sums_ref, sums_in_ref)
 
 
 def relay_kernel(
     scal_ref, place_ref, label_ref, own_ref, after_ref, before_ref, relay_ref, early_ref,
-    image_in_ref, image_far_ref, text_far_ref,
-    image_total_ref, far_ref, diagonal_ref, sums_ref,
+    image_far_ref, text_far_ref,
+    near_g_ref, far_ref, diagonal_ref, sums_ref,
 ):
     rows, width = relay_ref.shape
     scorer = Scorer(scal_ref, label_ref, place_ref)
@@ -191,28 +192,26 @@
         message = jnp.where(lane == at, jnp.sum(total, axis=1, keepdims=True), message)
     sums_ref[...] = message
     diagonal_ref[...] = t_matmul(gx, ux).astype(BF16)
-    far_ref[:rows, :] = (image_far_ref[...] + matmul(gx, vr)).astype(BF16)
+    far_ref[:rows, :] = (image_far_ref[...].astype(F32) + matmul(gx, vr)).astype(BF16)
     far_ref[rows:, :] = text_far_ref[...]
-    image_total_ref[...] = image_in_ref[...] + matmul(gr, vr)
-
-
-def middle_kernel(
-    image_in_ref, text_in_ref, near_ref, cross_ref, got_ref, image_total_ref, text_total_ref, sums_ref
-):
-    rows = cross_ref.shape[0]
-    image_total_ref[...] = image_in_ref[...] + near_ref[:rows, :].astype(F32)
-    text_total_ref[...] = text_in_ref[...] + near_ref[rows:, :].astype(F32) + cross_ref[...].astype(F32)
+    near_g_ref[...] = gr
+
+
+def middle_kernel(near_any, cross_any, got_ref, sums_ref):
     sums_ref[...] = jnp.sum(got_ref[...], axis=0, keepdims=True)
 
 
 def final_kernel(
-    count, scal_ref, image_ref, text_ref, image_total_ref, text_total_ref, far_ref, diagonal_ref, got_ref,
+    count, scal_ref, image_ref, text_ref, image_total_ref, text_total_ref, near_g_ref, relay_ref,
+    near_ref, cross_ref, far_ref, diagonal_ref, got_ref,
     image_grad_ref, text_grad_ref, stats_ref,
 ):
     rows, width = image_ref.shape
     temper = jnp.exp(jnp.full((1, 128), scal_ref[0], F32))[:, :1]
-    image_total = image_total_ref[...] + far_ref[:rows, :].astype(F32)
-    text_total = text_total_ref[...] + far_ref[rows:, :].astype(F32) + diagonal_ref[...].astype(F32)
+    image_total = image_total_ref[...] + matmul(near_g_ref[...], relay_ref[...])
+    image_total += near_ref[:rows, :].astype(F32) + far_ref[:rows, :].astype(F32)
+    text_total = text_total_ref[...] + (near_ref[rows:, :].astype(F32) + far_ref[rows:, :].astype(F32))
+    text_total += cross_ref[...].astype(F32) + diagonal_ref[...].astype(F32)
     for raw_ref, total, out_ref in ((image_ref, image_total, image_grad_ref), (text_ref, text_total, text_grad_ref)):
         unit, scale = normalize(raw_ref[...])
         out_ref[...] = norm_back(unit, scale, temper * total).astype(BF16)
@@ -285,31 +284,32 @@
     image_total, text_total, cross_total, near, image_far, text_far, sums = call(
         early_kernel,
         head + [VMEM] * 8,
-        (block, block, half, pair, block, half, shape(8, 128, F32)),
+        (block, block, half, pair, half, half, shape(8, 128, F32)),
         "early",
         20 * dot,
     )(scal, place, labels, both, after, before, cross_v, image_total, text_total, cross_total, sums)
     from_cross = across(cross_total)
     from_near = near_side(near)
-    image_total, far, diagonal, sums = call(
-        relay_kernel, head + [VMEM] * 8, (block, pair, half, shape(1, 128, F32)), "relay", 10 * dot
-    )(scal, place, labels, both, after, before, relay_v, sums, image_total, image_far, text_far)
+    near_g, far, diagonal, sums = call(
+        relay_kernel, head + [VMEM] * 7, (shape(rows, rows, BF16), pair, half, shape(1, 128, F32)), "relay", 100 * dot
+    )(scal, place, labels, both, after, before, relay_v, sums, image_far, text_far)
     from_diagonal = diagonally(diagonal)
     from_far = far_side(far)
     got = exchanged(sums, "group")
-    image_total, text_total, sums = call(
-        middle_kernel, [VMEM] * 5, (block, block, shape(1, 128, F32)), "middle", 10 * dot
-    )(image_total, text_total, from_near, from_cross, got)
+    sums = call(middle_kernel, [HBM, HBM, VMEM], shape(1, 128, F32), "middle", 300 * dot)(from_near, from_cross, got)
     got = exchanged(sums, "blk")
     count = float(cycle * groups * rows) * float(rows) * 8.0
     image_grad, text_grad, stats = call(
         functools.partial(final_kernel, count),
-        [SMEM] + [VMEM] * 7,
+        [SMEM] + [VMEM] * 11,
         (half, half, jax.ShapeDtypeStruct((3,), F32)),
         "final",
         10 * dot,
         (VMEM, VMEM, SMEM),
-    )(scal, images, texts, image_total, text_total, from_far, from_diagonal, got)
+    )(
+        scal, images, texts, image_total, text_total, near_g, relay_v,
+        from_near, from_cross, from_far, from_diagonal, got,
+    )
     return image_grad, text_grad, stats
 
 

time: 109 us -> 101 us (0.927); the launches traced: 108 us -> 101 us
  blocking collectives: 22 us -> 0 us
  starting transfers between devices: 49.8 us -> 61.7 us
  local copies, waits for them, and re-layouts: 1.65 us -> 3.78 us
  Pallas kernels: 7.92 us -> 9.67 us
    all_to_all x1 -> x0, blocking collectives: 22 us -> none  [exchanged(): return lax.all_to_all(sent, axis, 0, 0).reshape(count, 128)]
    all_to_all x1 -> x2, starting transfers between devices: 4.63 us -> 20 us  [exchanged(): return lax.all_to_all(sent, axis, 0, 0).reshape(count, 128)]
    all_to_all x1 -> x2, waiting for transfers between devices: 11.2 us -> 7.18 us  [exchanged(): return lax.all_to_all(sent, axis, 0, 0).reshape(count, 128)]
    ppermute x8, starting transfers between devices: 45.1 us -> 41.7 us  [passed(): lax.ppermute(value, 'blk', [(p, (p + step_of(p)) % cycle) for p in range(...]
    ppermute x8, waiting for transfers between devices: 12.9 us -> 16.3 us  [passed(): lax.ppermute(value, 'blk', [(p, (p + step_of(p)) % cycle) for p in range(...]
    unnamed x10 -> x18, local copies, waits for them, and re-layouts: 1.02 us -> 2.55 us
    pallas_call x4, Pallas kernels: 6.23 us -> 7.51 us  [the longest x1 3.55 us: per_device(): call(early_kernel, head + [VMEM] * 8, (block, block, half, pair, half, ha...]
  transfers between devices with their start and end apart: 9 -> 10, of which waited for: 4 -> 6; matrix products, arithmetic and copies ran while one was open for 1% -> 1% of each run, Pallas kernels for 6% -> 7%
where the time goes in v7:
time: 101 us
  starting transfers between devices  61.7 us (61%)
  waiting for transfers between devices  23.4 us (23%)
  Pallas kernels  9.67 us (10%)
  local copies, waits for them, and re-layouts  3.78 us (4%)
  between operations  2.13 us (2%)
    ppermute x8, starting transfers between devices, passed(): lax.ppermute(value, 'blk', [(p, (p + step_of(p)) % cycle) for p in range(...  41.7 us
    all_to_all x2, starting transfers between devices, exchanged(): return lax.all_to_all(sent, axis, 0, 0).reshape(count, 128)  20 us
    ppermute x8, waiting for transfers between devices, passed(): lax.ppermute(value, 'blk', [(p, (p + step_of(p)) % cycle) for p in range(...  16.3 us
    all_to_all x2, waiting for transfers between devices, exchanged(): return lax.all_to_all(sent, axis, 0, 0).reshape(count, 128)  7.18 us
    pallas_call x1, Pallas kernels, per_device(): call(early_kernel, head + [VMEM] * 8, (block, block, half, pair, half, ha...  3.55 us
    pallas_call x1, Pallas kernels, per_device(): call(functools.partial(final_kernel, count), [SMEM] + [VMEM] * 11, (half,...  2.68 us
    unnamed x18, local copies, waits for them, and re-layouts  2.55 us
  transfers between devices with their start and end apart: 10, of which 6 were waited for; matrix products, arithmetic and copies ran while one was open for 1% of the time, Pallas kernels for 7%

profile of v7, /device:TPU:1, one launch (start us, length us, event | category | flops | bytes accessed | tf_op | source)
XLA Modules:
  0.0 100.8 jit_solution(12183727340654140183)
XLA Ops:
  0.7 1.0 copy-done.1
  1.8 8.7 %collective-permute-start.2 = (bf16[128,1152]{1,0:T(8,128)(2,1)S(1)}, bf16[128,1152]{1,0:T(8,128)(2,1)}, u32[]{:S(2)}, u32[]{:S(2)}) collective-permute-start(bf16[128,1152]{1,0:T(8,128)(2,1)S(1)} %text.1.text_unit_ref), channel_id=1, source_target_pairs={{0,64},{64,0},{128,192},{192,128},{256,320},{320,256},{384,448},{4... | collective-permute-start | bytes 884744 | tf_op jit(solution)/shard_map/ppermute | solution.py:251
  10.8 17.2 %collective-permute-start = (bf16[128,2432]{1,0:T(8,128)(2,1)S(1)}, bf16[128,2432]{1,0:T(8,128)(2,1)S(1)}, u32[]{:S(2)}, u32[]{:S(2)}) collective-permute-start(bf16[128,2432]{1,0:T(8,128)(2,1)S(1)} %image.1.own_ref), channel_id=1, source_target_pairs={{0,896},{64,960},{128,0},{192,64},{256,128},{320,192},{384,256},{4... | collective-permute-start | bytes 1867784 | tf_op jit(solution)/shard_map/ppermute | solution.py:251
  27.9 1.9 %collective-permute-start.1 = (bf16[128,2432]{1,0:T(8,128)(2,1)S(1)}, bf16[128,2432]{1,0:T(8,128)(2,1)S(1)}, u32[]{:S(2)}, u32[]{:S(2)}) collective-permute-start(bf16[128,2432]{1,0:T(8,128)(2,1)S(1)} %image.1.own_ref), channel_id=1, source_target_pairs={{0,128},{64,192},{128,256},{192,320},{256,384},{320,448},{384,512}... | collective-permute-start | bytes 1867784 | tf_op jit(solution)/shard_map/ppermute | solution.py:251
  31.2 1.9 %collective-permute-start.3 = (bf16[128,1152]{1,0:T(8,128)(2,1)}, bf16[128,1152]{1,0:T(8,128)(2,1)S(1)}, u32[]{:S(2)}, u32[]{:S(2)}) collective-permute-start(bf16[128,1152]{1,0:T(8,128)(2,1)} %collective-permute-done.2.cross_ref), channel_id=1, source_target_pairs={{0,128},{64,960},{128,256},{192,64},{256,384},{320,192},{384,512},... | collective-permute-start | bytes 884744 | tf_op jit(solution)/shard_map/ppermute | solution.py:251
  33.2 1.8 %own.1 = (f32[128,1152]{1,0:T(8,128)S(1)}, f32[128,1152]{1,0:T(8,128)S(1)}, f32[128,1152]{1,0:T(8,128)S(1)}, f32[8,128]{1,0:T(8,128)S(1)}) custom-call(f32[2]{0:T(128)S(1)} %pad_maximum_fusion.scal_ref, s32[1]{0:T(128)} %bitcast.place_ref, s32[16,128]{1,0:T(8,128)S(1)} %copy-done.5, bf16[128,2432]{1,0:T(8,128)(2,1)S(1)} %image.1.own_ref, ...), custom_call_target="tpu_custom_call" | custom-call | flops 7549747200 | tf_op jit(solution)/shard_map/own/pallas_call | solution.py:280
  35.0 5.3 %collective-permute-done.after_ref = bf16[128,2432]{1,0:T(8,128)(2,1)S(1)} collective-permute-done((bf16[128,2432]{1,0:T(8,128)(2,1)S(1)}, bf16[128,2432]{1,0:T(8,128)(2,1)S(1)}, u32[]{:S(2)}, u32[]{:S(2)}) %collective-permute-start) | collective-permute-done | bytes 622624 | tf_op jit(solution)/shard_map/ppermute | solution.py:251
  40.3 5.0 %collective-permute-done.1.before_ref = bf16[128,2432]{1,0:T(8,128)(2,1)S(1)} collective-permute-done((bf16[128,2432]{1,0:T(8,128)(2,1)S(1)}, bf16[128,2432]{1,0:T(8,128)(2,1)S(1)}, u32[]{:S(2)}, u32[]{:S(2)}) %collective-permute-start.1) | collective-permute-done | bytes 622624 | tf_op jit(solution)/shard_map/ppermute | solution.py:251
  45.3 3.5 %early.1 = (f32[128,1152]{1,0:T(8,128)S(1)}, f32[128,1152]{1,0:T(8,128)S(1)}, bf16[128,1152]{1,0:T(8,128)(2,1)}, bf16[256,1152]{1,0:T(8,128)(2,1)}, bf16[128,115...) custom-call(f32[2]{0:T(128)S(1)} %pad_maximum_fusion.scal_ref, s32[1]{0:T(128)} %bitcast.place_ref, ...), custom_call_target="tpu_custom_call" | custom-call | flops 754974720 | tf_op jit(solution)/shard_map/early/pallas_call | solution.py:284
  48.9 1.9 %collective-permute-start.4 = (bf16[256,1152]{1,0:T(8,128)(2,1)}, bf16[256,1152]{1,0:T(8,128)(2,1)}, u32[]{:S(2)}, u32[]{:S(2)}) collective-permute-start(bf16[256,1152]{1,0:T(8,128)(2,1)} %get-tuple-element.28), channel_id=1, source_target_pairs={{0,896},{64,192},{128,0},{192,320},{256,128},{320,448},{384,256},{... | collective-permute-start | bytes 1769480 | tf_op jit(solution)/shard_map/ppermute | solution.py:251
  50.8 2.2 %collective-permute-start.5 = (bf16[128,1152]{1,0:T(8,128)(2,1)}, bf16[128,1152]{1,0:T(8,128)(2,1)}, u32[]{:S(2)}, u32[]{:S(2)}) collective-permute-start(bf16[128,1152]{1,0:T(8,128)(2,1)} %get-tuple-element.29), channel_id=1, source_target_pairs={{0,64},{64,0},{128,192},{192,128},{256,320},{320,256},{384,448},{4... | collective-permute-start | bytes 884744 | tf_op jit(solution)/shard_map/ppermute | solution.py:251
  53.0 1.3 %relay.1 = (bf16[128,128]{1,0:T(8,128)(2,1)S(1)}, bf16[256,1152]{1,0:T(8,128)(2,1)S(1)}, bf16[128,1152]{1,0:T(8,128)(2,1)S(1)}, f32[1,128]{1,0:T(1,128)S(1)}) custom-call(f32[2]{0:T(128)S(1)} %pad_maximum_fusion.scal_ref, s32[1]{0:T(128)} %bitcast.place_ref, s32[16,128]{1,0:T(8,128)S(1)} %copy-done.5, bf16[128,2432]{1,0:T(8,128)(2,1)S(1)} %image.1.own_ref, ...), custom_call_target="tpu_custom_call" | custom-call | flops 3774873600 | tf_op jit(solution)/shard_map/relay/pallas_call | solution.py:293
  54.3 0.8 copy-done.6
  55.1 0.7 copy-done.7
  55.9 0.6 broadcast_in_dim.15
  56.5 12.2 %all-to-all-start = ((f32[64,1,128]{2,1,0:T(1,128)}), f32[64,1,128]{2,1,0:T(1,128)S(1)}, u32[]{:S(2)}, u32[]{:S(2)}) async-start(f32[64,1,128]{2,1,0:T(1,128)} %broadcast_in_dim.15), calls=%async_computation | async-start | bytes 65536 | tf_op jit(solution)/shard_map/all_to_all | solution.py:238
  68.6 3.0 %collective-permute-start.6 = (bf16[256,1152]{1,0:T(8,128)(2,1)}, bf16[256,1152]{1,0:T(8,128)(2,1)S(1)}, u32[]{:S(2)}, u32[]{:S(2)}) collective-permute-start(bf16[256,1152]{1,0:T(8,128)(2,1)} %copy-done.6), channel_id=1, source_target_pairs={{0,128},{64,960},{128,256},{192,64},{256,384},{320,192},{384,512},... | collective-permute-start | bytes 1769480 | tf_op jit(solution)/shard_map/ppermute | solution.py:251
  71.7 4.8 %collective-permute-start.7 = (bf16[128,1152]{1,0:T(8,128)(2,1)}, bf16[128,1152]{1,0:T(8,128)(2,1)S(1)}, u32[]{:S(2)}, u32[]{:S(2)}) collective-permute-start(bf16[128,1152]{1,0:T(8,128)(2,1)} %copy-done.7), channel_id=1, source_target_pairs={{0,960},{64,128},{128,64},{192,256},{256,192},{320,384},{384,320},... | collective-permute-start | bytes 884744 | tf_op jit(solution)/shard_map/ppermute | solution.py:251
  76.5 1.7 %all-to-all-done = f32[64,1,128]{2,1,0:T(1,128)S(1)} async-done(((f32[64,1,128]{2,1,0:T(1,128)}), f32[64,1,128]{2,1,0:T(1,128)S(1)}, u32[]{:S(2)}, u32[]{:S(2)}) %all-to-all-start) | async-done | bytes 32800 | tf_op jit(solution)/shard_map/all_to_all | solution.py:238
  78.9 7.8 %all-to-all-start.1 = ((f32[16,1,128]{2,1,0:T(1,128)}), f32[16,1,128]{2,1,0:T(1,128)S(1)}, u32[]{:S(2)}, u32[]{:S(2)}) async-start(f32[16,1,128]{2,1,0:T(1,128)} %broadcast_in_dim.17), calls=%async_computation.1 | async-start | bytes 16384 | tf_op jit(solution)/shard_map/all_to_all | solution.py:238
  86.7 1.0 collective-permute-done.7.diagonal_ref
  87.7 5.0 %collective-permute-done.6.far_ref = bf16[256,1152]{1,0:T(8,128)(2,1)S(1)} collective-permute-done((bf16[256,1152]{1,0:T(8,128)(2,1)}, bf16[256,1152]{1,0:T(8,128)(2,1)S(1)}, u32[]{:S(2)}, u32[]{:S(2)}) %collective-permute-start.6) | collective-permute-done | bytes 589856 | tf_op jit(solution)/shard_map/ppermute | solution.py:251
  92.6 5.4 %all-to-all-done.1 = f32[16,1,128]{2,1,0:T(1,128)S(1)} async-done(((f32[16,1,128]{2,1,0:T(1,128)}), f32[16,1,128]{2,1,0:T(1,128)S(1)}, u32[]{:S(2)}, u32[]{:S(2)}) %all-to-all-start.1) | async-done | bytes 8224 | tf_op jit(solution)/shard_map/all_to_all | solution.py:238
  98.1 2.7 %final.1 = (bf16[128,1152]{1,0:T(8,128)(2,1)}, bf16[128,1152]{1,0:T(8,128)(2,1)}, f32[3]{0:T(128)}) custom-call(f32[2]{0:T(128)S(1)} %pad_maximum_fusion.scal_ref, bf16[128,1152]{1,0:T(8,128)(2,1)S(1)} %copy-done, bf16[128,1152]{1,0:T(8,128)(2,1)S(1)} %copy-done.2, f32[128,1152]{1,0:T(8,128)S(1)} %get-tuple-element.22.image_total_ref, ...), custom_call_target="tpu_custom_call" | custom-call | flops 377487360 | tf_op jit(solution)/shard_map/final/pallas_call | solution.py:302
  (24 shorter events, 1.1 us)
Async XLA Ops:
  0.6 9.9 %copy-start = (bf16[128,1152]{1,0:T(8,128)(2,1)S(1)}, bf16[128,1152]{1,0:T(8,128)(2,1)}, u32[]{:S(2)}) copy-start(bf16[128,1152]{1,0:T(8,128)(2,1)} %image_ref.3) | copy-start | bytes 884740
  0.6 1.0 %copy-start.1 = (bf16[128,1152]{1,0:T(8,128)(2,1)S(1)}, bf16[128,1152]{1,0:T(8,128)(2,1)}, u32[]{:S(2)}) copy-start(bf16[128,1152]{1,0:T(8,128)(2,1)} %text_ref.3) | copy-start | bytes 884740
  1.8 8.8 %copy-start.8 = (f32[128]{0:T(128)S(1)}, f32[128]{0:T(128)}, u32[]{:S(2)}) copy-start(f32[128]{0:T(128)} %param.9) | copy-start | bytes 1540
  1.8 29.4 %collective-permute-start.2 = (bf16[128,1152]{1,0:T(8,128)(2,1)S(1)}, bf16[128,1152]{1,0:T(8,128)(2,1)}, u32[]{:S(2)}, u32[]{:S(2)}) collective-permute-start(bf16[128,1152]{1,0:T(8,128)(2,1)S(1)} %text.1.text_unit_ref), channel_id=1, source_target_pairs={{0,64},{64,0},{128,192},{192,128},{256,320},{320,256},{384,448},{4... | collective-permute-start | bytes 884744 | tf_op jit(solution)/shard_map/ppermute | solution.py:251
  10.7 22.4 %copy-start.5 = (s32[16,128]{1,0:T(8,128)S(1)}, s32[16,128]{1,0:T(8,128)}, u32[]{:S(2)}) copy-start(s32[16,128]{1,0:T(8,128)} %label_ref.5) | copy-start | bytes 24580
  10.8 29.5 %collective-permute-start = (bf16[128,2432]{1,0:T(8,128)(2,1)S(1)}, bf16[128,2432]{1,0:T(8,128)(2,1)S(1)}, u32[]{:S(2)}, u32[]{:S(2)}) collective-permute-start(bf16[128,2432]{1,0:T(8,128)(2,1)S(1)} %image.1.own_ref), channel_id=1, source_target_pairs={{0,896},{64,960},{128,0},{192,64},{256,128},{320,192},{384,256},{4... | collective-permute-start | bytes 1867784 | tf_op jit(solution)/shard_map/ppermute | solution.py:251
  27.9 17.4 %collective-permute-start.1 = (bf16[128,2432]{1,0:T(8,128)(2,1)S(1)}, bf16[128,2432]{1,0:T(8,128)(2,1)S(1)}, u32[]{:S(2)}, u32[]{:S(2)}) collective-permute-start(bf16[128,2432]{1,0:T(8,128)(2,1)S(1)} %image.1.own_ref), channel_id=1, source_target_pairs={{0,128},{64,192},{128,256},{192,320},{256,384},{320,448},{384,512}... | collective-permute-start | bytes 1867784 | tf_op jit(solution)/shard_map/ppermute | solution.py:251
  31.2 21.8 %collective-permute-start.3 = (bf16[128,1152]{1,0:T(8,128)(2,1)}, bf16[128,1152]{1,0:T(8,128)(2,1)S(1)}, u32[]{:S(2)}, u32[]{:S(2)}) collective-permute-start(bf16[128,1152]{1,0:T(8,128)(2,1)} %collective-permute-done.2.cross_ref), channel_id=1, source_target_pairs={{0,128},{64,960},{128,256},{192,64},{256,384},{320,192},{384,512},... | collective-permute-start | bytes 884744 | tf_op jit(solution)/shard_map/ppermute | solution.py:251
  48.9 29.3 %collective-permute-start.4 = (bf16[256,1152]{1,0:T(8,128)(2,1)}, bf16[256,1152]{1,0:T(8,128)(2,1)}, u32[]{:S(2)}, u32[]{:S(2)}) collective-permute-start(bf16[256,1152]{1,0:T(8,128)(2,1)} %get-tuple-element.28), channel_id=1, source_target_pairs={{0,896},{64,192},{128,0},{192,320},{256,128},{320,448},{384,256},{... | collective-permute-start | bytes 1769480 | tf_op jit(solution)/shard_map/ppermute | solution.py:251
  50.8 27.4 %collective-permute-start.5 = (bf16[128,1152]{1,0:T(8,128)(2,1)}, bf16[128,1152]{1,0:T(8,128)(2,1)}, u32[]{:S(2)}, u32[]{:S(2)}) collective-permute-start(bf16[128,1152]{1,0:T(8,128)(2,1)} %get-tuple-element.29), channel_id=1, source_target_pairs={{0,64},{64,0},{128,192},{192,128},{256,320},{320,256},{384,448},{4... | collective-permute-start | bytes 884744 | tf_op jit(solution)/shard_map/ppermute | solution.py:251
  53.0 1.3 %copy-start.3 = (bf16[128,1152]{1,0:T(8,128)(2,1)}, bf16[128,1152]{1,0:T(8,128)(2,1)S(1)}, u32[]{:S(2)}) copy-start(bf16[128,1152]{1,0:T(8,128)(2,1)S(1)} %collective-permute-done.3.relay_ref) | copy-start | bytes 884740
  54.3 0.8 copy-start.6
  55.1 0.7 copy-start.7
  56.5 21.8 %all-to-all-start = ((f32[64,1,128]{2,1,0:T(1,128)}), f32[64,1,128]{2,1,0:T(1,128)S(1)}, u32[]{:S(2)}, u32[]{:S(2)}) async-start(f32[64,1,128]{2,1,0:T(1,128)} %broadcast_in_dim.15), calls=%async_computation | async-start | bytes 65536 | tf_op jit(solution)/shard_map/all_to_all | solution.py:238
  68.6 24.0 %collective-permute-start.6 = (bf16[256,1152]{1,0:T(8,128)(2,1)}, bf16[256,1152]{1,0:T(8,128)(2,1)S(1)}, u32[]{:S(2)}, u32[]{:S(2)}) collective-permute-start(bf16[256,1152]{1,0:T(8,128)(2,1)} %copy-done.6), channel_id=1, source_target_pairs={{0,128},{64,960},{128,256},{192,64},{256,384},{320,192},{384,512},... | collective-permute-start | bytes 1769480 | tf_op jit(solution)/shard_map/ppermute | solution.py:251
  71.7 16.0 %collective-permute-start.7 = (bf16[128,1152]{1,0:T(8,128)(2,1)}, bf16[128,1152]{1,0:T(8,128)(2,1)S(1)}, u32[]{:S(2)}, u32[]{:S(2)}) collective-permute-start(bf16[128,1152]{1,0:T(8,128)(2,1)} %copy-done.7), channel_id=1, source_target_pairs={{0,960},{64,128},{128,64},{192,256},{256,192},{320,384},{384,320},... | collective-permute-start | bytes 884744 | tf_op jit(solution)/shard_map/ppermute | solution.py:251
  78.2 19.8 %copy-start.2 = (bf16[128,1152]{1,0:T(8,128)(2,1)S(1)}, bf16[128,1152]{1,0:T(8,128)(2,1)}, u32[]{:S(2)}) copy-start(bf16[128,1152]{1,0:T(8,128)(2,1)} %text_ref.3) | copy-start | bytes 884740
  78.2 19.8 %copy-start.4 = (bf16[128,1152]{1,0:T(8,128)(2,1)S(1)}, bf16[128,1152]{1,0:T(8,128)(2,1)}, u32[]{:S(2)}) copy-start(bf16[128,1152]{1,0:T(8,128)(2,1)} %copy-done.3) | copy-start | bytes 884740
  78.9 19.2 %all-to-all-start.1 = ((f32[16,1,128]{2,1,0:T(1,128)}), f32[16,1,128]{2,1,0:T(1,128)S(1)}, u32[]{:S(2)}, u32[]{:S(2)}) async-start(f32[16,1,128]{2,1,0:T(1,128)} %broadcast_in_dim.17), calls=%async_computation.1 | async-start | bytes 16384 | tf_op jit(solution)/shard_map/all_to_all | solution.py:238

commit v8 on v6

--- a/solution.py
+++ b/solution.py
@@ -133,7 +133,7 @@
 def early_kernel(
     scal_ref, place_ref, label_ref, own_ref, after_ref, before_ref, cross_ref,
     image_in_ref, text_in_ref, sums_in_ref,
-    image_total_ref, text_total_ref, far_g_ref, sums_ref,
+    image_total_ref, text_total_ref, cross_g_ref, four_g_ref, sums_ref,
 ):
     rows, width = cross_ref.shape
     scorer = Scorer(scal_ref, label_ref, place_ref)
@@ -156,13 +156,12 @@
     tb = scorer.grads(ub, v, wb, col_b, row, False)
     image_total_ref[...] = image_in_ref[...] + matmul(ga, va) + matmul(gb, vb)
     text_total_ref[...] = text_in_ref[...] + t_matmul(ta, ua) + t_matmul(tb, ub)
-    far_g_ref[:rows, :] = gx
-    far_g_ref[rows:, :] = gfar
+    cross_g_ref[...], four_g_ref[...] = gx, gfar
     scorer.store_sums(sums_ref, sums_in_ref)
 
 
 def relay_kernel(
-    scal_ref, place_ref, label_ref, own_ref, after_ref, before_ref, relay_ref, early_ref, far_in_ref,
+    scal_ref, place_ref, label_ref, own_ref, after_ref, before_ref, relay_ref, early_ref,
     near_ref, far_ref, sums_ref,
 ):
     width = relay_ref.shape[1]
@@ -176,22 +175,20 @@
     near_ref[...] = scorer.grads(own_ref[:, :width], vr, weight_of(own_ref, width), col, row_r, True)
     ux = jnp.where(even, after_ref[:, :width], before_ref[:, :width])
     wx = jnp.where(even, weight_of(after_ref, width), weight_of(before_ref, width))
-    rows = relay_ref.shape[0]
-    far_ref[:rows, :] = scorer.grads(ux, vr, wx, col_x, row_r, True)
-    far_ref[rows:, :] = far_in_ref[...]
+    far_ref[...] = scorer.grads(ux, vr, wx, col_x, row_r, True)
     lane = lax.broadcasted_iota(jnp.int32, (1, 128), 1)
     message = jnp.zeros((1, 128), F32)
     for at in range(3):
         total = jnp.sum(scorer.sums[at], axis=0, keepdims=True) + early_ref[at : at + 1, :]
         message = jnp.where(lane == at, jnp.sum(total, axis=1, keepdims=True), message)
-    sums_ref[...] = message
+    sums_ref[...] = jnp.broadcast_to(message.reshape(1, 1, 128), sums_ref.shape)
 
 
 def late_kernel(
     scal_ref, place_ref, label_any, own_any, after_any, before_any, cross_any, relay_any, relay_v_any,
-    far_g_any, cross_v_any,
+    far_g_any, cross_v_any, far_cross_any, four_any,
     to_up_ref, to_down_ref, cross_g_ref, relay_g_ref,
-    label_ref, v_ref, va_ref, before_ref, cross_ref, relay_ref, relay_v_ref, far_g_ref, cross_v_ref,
+    label_ref, v_ref, va_ref, before_ref, cross_ref, relay_ref, relay_v_ref, far_g_ref, cross_v_ref, far_cross_ref, four_ref,
     sems,
 ):
     rows, width = relay_v_ref.shape
@@ -208,6 +205,8 @@
             (far_g_any, far_g_ref),
             (relay_v_any, relay_v_ref),
             (cross_v_any, cross_v_ref),
+            (far_cross_any, far_cross_ref),
+            (four_any, four_ref),
         ))
     ]
     for copy in copies:
@@ -231,9 +230,9 @@
     grx = scorer.grads(ur, jnp.where(even, va, vb), wr, col_r, jnp.where(even, row_a, row_b), False)
     gr = scorer.grads(ur, v, wr, col_r, row, False)
     far_text_c, far_text_r = t_matmul(gcx, uc), t_matmul(grx, ur)
-    far_image_r = matmul(far_g_ref[:rows, :], relay_v_ref[...])
-    far_image_c = matmul(far_g_ref[rows : 2 * rows, :], cross_v_ref[...])
-    g = far_g_ref[2 * rows :, :]
+    far_image_r = matmul(far_g_ref[...], relay_v_ref[...])
+    far_image_c = matmul(far_cross_ref[...], cross_v_ref[...])
+    g = four_ref[...]
     to_up_ref[:rows, :] = jnp.where(even, far_image_r, far_image_c).astype(BF16)
     to_up_ref[rows:, :] = (t_matmul(g, before_ref[:, :width]) + jnp.where(even, far_text_r, far_text_c)).astype(BF16)
     to_down_ref[:rows, :] = (matmul(g, va) + jnp.where(even, far_image_c, far_image_r)).astype(BF16)
@@ -242,7 +241,8 @@
 
 
 def middle_kernel(got_ref, sums_ref):
-    sums_ref[...] = jnp.sum(got_ref[...], axis=0, keepdims=True)
+    total = jnp.sum(got_ref[...], axis=0, keepdims=True)
+    sums_ref[...] = jnp.broadcast_to(total.reshape(1, 1, 128), sums_ref.shape)
 
 
 def final_kernel(
@@ -279,10 +279,8 @@
     )
 
 
-def exchanged(row, axis):
-    count = lax.axis_size(axis)
-    sent = jnp.broadcast_to(row.reshape(1, 1, 128), (count, 1, 128))
-    return lax.all_to_all(sent, axis, 0, 0).reshape(count, 128)
+def exchanged(sent, axis):
+    return lax.all_to_all(sent, axis, 0, 0).reshape(sent.shape[0], 128)
 
 
 def per_device(images, texts, labels, weights, log_temp, bias):
@@ -309,7 +307,7 @@
     def downward(value):
         return passed(value, lambda p: -2)
 
-    block = shape(rows, width, F32)
+    block, square = shape(rows, width, F32), shape(rows, rows, BF16)
     text_unit = call(text_kernel, [VMEM], shape(rows, width, BF16), "text", 10 * dot)(texts)
     cross_v = across(text_unit)
     image_pack, both = call(
@@ -326,32 +324,33 @@
     image_total, text_total, sums = call(
         own_kernel, head + [VMEM] * 2, (block,) * 2 + (shape(8, 128, F32),), "own", 150 * dot
     )(scal, place, labels, both, cross_v)
-    image_total, text_total, far_g, sums = call(
-        early_kernel, head + [VMEM] * 7, (block, block, shape(2 * rows, rows, BF16), shape(8, 128, F32)), "early", 20 * dot
+    image_total, text_total, far_cross_g, four_g, sums = call(
+        early_kernel, head + [VMEM] * 7, (block, block, square, square, shape(8, 128, F32)), "early", 20 * dot
     )(scal, place, labels, both, after, before, cross_v, image_total, text_total, sums)
+    near_g, far_g, sums = call(
+        relay_kernel,
+        head + [VMEM] * 5,
+        (square, square, jax.ShapeDtypeStruct((groups, 1, 128), F32)),
+        "relay", 10 * dot
+    )(scal, place, labels, both, after, before, relay_v, sums)
     cross_u, sums = lax.optimization_barrier((cross_u, sums))
     relay_u = relayed(cross_u)
-    near_g, far_g, sums = call(
-        relay_kernel,
-        head + [VMEM] * 6,
-        (shape(rows, rows, BF16), shape(3 * rows, rows, BF16), shape(1, 128, F32)),
-        "relay", 10 * dot
-    )(scal, place, labels, both, after, before, relay_v, sums, far_g)
     got = exchanged(sums, "group")
     half, pack = pltpu.VMEM((rows, width), BF16), pltpu.VMEM((rows, width + 128), BF16)
     scratch = [pltpu.VMEM(labels.shape, jnp.int32), half, half, pltpu.VMEM(both.shape, BF16), pack, pack, half]
-    scratch += [pltpu.VMEM((3 * rows, rows), BF16), half]
+    block_g = pltpu.VMEM((rows, rows), BF16)
+    scratch += [block_g, half, block_g, block_g]
     to_up, to_down, cross_g, relay_g = call(
         late_kernel,
-        [SMEM, SMEM] + [HBM] * 9,
+        [SMEM, SMEM] + [HBM] * 11,
         (shape(2 * rows, width, BF16),) * 2 + (shape(rows, rows, BF16),) * 2,
         "late",
         400 * dot,
-        scratch=scratch + [pltpu.SemaphoreType.DMA((9,))],
-    )(scal, place, labels, both, after, before, cross_u, relay_u, relay_v, far_g, cross_v)
+        scratch=scratch + [pltpu.SemaphoreType.DMA((11,))],
+    )(scal, place, labels, both, after, before, cross_u, relay_u, relay_v, far_g, cross_v, far_cross_g, four_g)
     from_below = upward(to_up)
     from_above = downward(to_down)
-    sums = call(middle_kernel, [VMEM], shape(1, 128, F32), "middle", 300 * dot)(got)
+    sums = call(middle_kernel, [VMEM], jax.ShapeDtypeStruct((cycle, 1, 128), F32), "middle", 300 * dot)(got)
     got = exchanged(sums, "blk")
     count = float(cycle * groups * rows) * float(rows) * 8.0
     image_grad, text_grad, stats = call(

time: 99.8 us -> 102 us (1.022)
  blocking collectives: 17.1 us -> 19.6 us
    all_to_all x1, blocking collectives: 17.1 us -> 19.6 us  [exchanged(): return lax.all_to_all(sent, axis, 0, 0).reshape(sent.shape[0], 128)]
  transfers between devices with their start and end apart: 9 -> 9, of which waited for: 4 -> 4; matrix products, arithmetic and copies ran while one was open for 1% -> 0% of each run, Pallas kernels for 10% -> 10%
where the time goes in v8:
time: 102 us; the launch traced here: 101 us
  starting transfers between devices  50.7 us (50%)
  blocking collectives  19.6 us (19%)
  Pallas kernels  13.1 us (13%)
  waiting for transfers between devices  12.5 us (12%)
  local copies, waits for them, and re-layouts  2.4 us (2%)
  between operations  2.12 us (2%)
    ppermute x8, starting transfers between devices, passed(): lax.ppermute(value, 'blk', [(p, (p + step_of(p)) % cycle) for p in range(...  40.1 us
    all_to_all x1, blocking collectives, exchanged(): return lax.all_to_all(sent, axis, 0, 0).reshape(sent.shape[0], 128)  19.6 us
    ppermute x8, waiting for transfers between devices, passed(): lax.ppermute(value, 'blk', [(p, (p + step_of(p)) % cycle) for p in range(...  12.5 us
    all_to_all x1, starting transfers between devices, exchanged(): return lax.all_to_all(sent, axis, 0, 0).reshape(sent.shape[0], 128)  10.6 us
    pallas_call x1, Pallas kernels, per_device(): call(late_kernel, [SMEM, SMEM] + [HBM] * 11, (shape(2 * rows, width, BF16...  3.84 us
    pallas_call x1, Pallas kernels, per_device(): call(functools.partial(final_kernel, count), [SMEM] + [VMEM] * 13, (shape...  2.61 us
    unnamed x16, local copies, waits for them, and re-layouts  2.4 us
    pallas_call x1, Pallas kernels, per_device(): call(early_kernel, head + [VMEM] * 7, (block, block, square, square, shap...  2.17 us
  transfers between devices with their start and end apart: 9, of which 4 were waited for; matrix products, arithmetic and copies ran while one was open for 0% of the time, Pallas kernels for 10%

profile of v8, /device:TPU:1, one launch (start us, length us, event | category | flops | bytes accessed | tf_op | source)
XLA Modules:
  0.0 100.5 jit_solution(6072219069346305260)
XLA Ops:
  0.7 1.0 copy-done.2
  1.6 0.1 text.1.text_unit_ref
  1.8 8.7 %collective-permute-start.2 = (bf16[128,1152]{1,0:T(8,128)(2,1)S(1)}, bf16[128,1152]{1,0:T(8,128)(2,1)}, u32[]{:S(2)}, u32[]{:S(2)}) collective-permute-start(bf16[128,1152]{1,0:T(8,128)(2,1)S(1)} %text.1.text_unit_ref), channel_id=1, source_target_pairs={{0,64},{64,0},{128,192},{192,128},{256,320},{320,256},{384,448},{4... | collective-permute-start | bytes 884744 | tf_op jit(solution)/shard_map/ppermute | solution.py:296
  10.6 0.9 image.1
  11.5 4.9 %collective-permute-start.1 = (bf16[128,2432]{1,0:T(8,128)(2,1)S(1)}, bf16[128,2432]{1,0:T(8,128)(2,1)S(1)}, u32[]{:S(2)}, u32[]{:S(2)}) collective-permute-start(bf16[128,2432]{1,0:T(8,128)(2,1)S(1)} %get-tuple-element.22.own_ref.own_any), channel_id=1, source_target_pairs={{0,128},{64,192},{128,256},{192,320},{256,384},{320,448},{384,512}... | collective-permute-start | bytes 1867784 | tf_op jit(solution)/shard_map/ppermute | solution.py:296
  16.4 14.2 %collective-permute-start = (bf16[128,2432]{1,0:T(8,128)(2,1)S(1)}, bf16[128,2432]{1,0:T(8,128)(2,1)S(1)}, u32[]{:S(2)}, u32[]{:S(2)}) collective-permute-start(bf16[128,2432]{1,0:T(8,128)(2,1)S(1)} %get-tuple-element.22.own_ref.own_any), channel_id=1, source_target_pairs={{0,896},{64,960},{128,0},{192,64},{256,128},{320,192},{384,256},{4... | collective-permute-start | bytes 1867784 | tf_op jit(solution)/shard_map/ppermute | solution.py:296
  30.6 1.9 %collective-permute-start.4 = (bf16[128,1280]{1,0:T(8,128)(2,1)}, bf16[128,1280]{1,0:T(8,128)(2,1)}, u32[]{:S(2)}, u32[]{:S(2)}) collective-permute-start(bf16[128,1280]{1,0:T(8,128)(2,1)} %get-tuple-element.30), channel_id=1, source_target_pairs={{0,64},{64,0},{128,192},{192,128},{256,320},{320,256},{384,448},{4... | collective-permute-start | bytes 983048 | tf_op jit(solution)/shard_map/ppermute | solution.py:296
  33.9 1.9 %collective-permute-start.3 = (bf16[128,1152]{1,0:T(8,128)(2,1)}, bf16[128,1152]{1,0:T(8,128)(2,1)S(1)}, u32[]{:S(2)}, u32[]{:S(2)}) collective-permute-start(bf16[128,1152]{1,0:T(8,128)(2,1)} %collective-permute-done.2.cross_ref.cross_v_any), channel_id=1, source_target_pairs={{0,128},{64,960},{128,256},{192,64},{256,384},{320,192},{384,512},... | collective-permute-start | bytes 884744 | tf_op jit(solution)/shard_map/ppermute | solution.py:296
  35.8 1.8 %own.1 = (f32[128,1152]{1,0:T(8,128)S(1)}, f32[128,1152]{1,0:T(8,128)S(1)}, f32[8,128]{1,0:T(8,128)S(1)}) custom-call(f32[2]{0:T(128)S(1)} %pad_maximum_fusion.scal_ref, s32[1]{0:T(128)} %bitcast.place_ref, s32[16,128]{1,0:T(8,128)S(1)} %copy-done.4, bf16[128,2432]{1,0:T(8,128)(2,1)S(1)} %get-tuple-element.22.own_ref.own_any, ...), custom_call_target="tpu_custom_call" | custom-call | flops 5662310400 | tf_op jit(solution)/shard_map/own/pallas_call | solution.py:324
  37.6 4.6 %collective-permute-done.1.before_ref.before_any = bf16[128,2432]{1,0:T(8,128)(2,1)S(1)} collective-permute-done((bf16[128,2432]{1,0:T(8,128)(2,1)S(1)}, bf16[128,2432]{1,0:T(8,128)(2,1)S(1)}, u32[]{:S(2)}, u32[]{:S(2)}) %collective-permute-start.1) | collective-permute-done | bytes 622624 | tf_op jit(solution)/shard_map/ppermute | solution.py:296
  42.2 0.8 collective-permute-done.after_ref.after_any
  42.9 2.2 %early.1 = (f32[128,1152]{1,0:T(8,128)S(1)}, f32[128,1152]{1,0:T(8,128)S(1)}, bf16[128,128]{1,0:T(8,128)(2,1)S(1)}, bf16[128,128]{1,0:T(8,128)(2,1)S(1)}, f32[8,128]{1,0:T(8,128)S(1)}) custom-call(f32[2]{0:T(128)S(1)} %pad_maximum_fusion.scal_ref, s32[1]{0:T(128)} %bitcast.place_ref, s32[16,128]{1,0:T(8,128)S(1)} %copy-done.4, ...), custom_call_target="tpu_custom_call" | custom-call | flops 754974720 | tf_op jit(solution)/shard_map/early/pallas_call | solution.py:327
  45.1 3.4 %collective-permute-done.3.relay_ref.relay_v_any.relay_v_ref = bf16[128,1152]{1,0:T(8,128)(2,1)S(1)} collective-permute-done((bf16[128,1152]{1,0:T(8,128)(2,1)}, bf16[128,1152]{1,0:T(8,128)(2,1)S(1)}, u32[]{:S(2)}, u32[]{:S(2)}) %collective-permute-start.3) | collective-permute-done | bytes 294944 | tf_op jit(solution)/shard_map/ppermute | solution.py:296
  48.5 1.7 %relay.1 = (bf16[128,128]{1,0:T(8,128)(2,1)S(1)}, bf16[128,128]{1,0:T(8,128)(2,1)S(1)}, f32[64,1,128]{2,1,0:T(1,128)}) custom-call(f32[2]{0:T(128)S(1)} %pad_maximum_fusion.scal_ref, s32[1]{0:T(128)} %bitcast.place_ref, s32[16,128]{1,0:T(8,128)S(1)} %copy-done.4, bf16[128,2432]{1,0:T(8,128)(2,1)S(1)} %get-tuple-element.22.own_ref.own_any, ...), custom_call_target="tpu_custom_call" | custom-call | flops 377487360 | tf_op jit(solution)/shard_map/relay/pallas_call | solution.py:330
  50.2 0.6 copy-done.5
  50.8 1.9 %collective-permute-start.5 = (bf16[128,1280]{1,0:T(8,128)(2,1)}, bf16[128,1280]{1,0:T(8,128)(2,1)}, u32[]{:S(2)}, u32[]{:S(2)}) collective-permute-start(bf16[128,1280]{1,0:T(8,128)(2,1)} %collective-permute-done.4.cross_any.cross_ref), channel_id=1, source_target_pairs={{0,128},{64,960},{128,256},{192,64},{256,384},{320,192},{384,512},... | collective-permute-start | bytes 983048 | tf_op jit(solution)/shard_map/ppermute | solution.py:296
  52.7 10.6 %all-to-all-start = ((f32[64,1,128]{2,1,0:T(1,128)}), f32[64,1,128]{2,1,0:T(1,128)S(1)}, u32[]{:S(2)}, u32[]{:S(2)}) async-start(f32[64,1,128]{2,1,0:T(1,128)} %get-tuple-element.40), calls=%async_computation | async-start | bytes 65536 | tf_op jit(solution)/shard_map/all_to_all | solution.py:283
  63.4 3.8 %collective-permute-done.5.relay_any.relay_ref = bf16[128,1280]{1,0:T(8,128)(2,1)} collective-permute-done((bf16[128,1280]{1,0:T(8,128)(2,1)}, bf16[128,1280]{1,0:T(8,128)(2,1)}, u32[]{:S(2)}, u32[]{:S(2)}) %collective-permute-start.5) | collective-permute-done | bytes 327712 | tf_op jit(solution)/shard_map/ppermute | solution.py:296
  67.1 0.8 copy-done.6
  67.9 3.8 %late.1 = (bf16[256,1152]{1,0:T(8,128)(2,1)}, bf16[256,1152]{1,0:T(8,128)(2,1)}, bf16[128,128]{1,0:T(8,128)(2,1)S(1)}, bf16[128,128]{1,0:T(8,128)(2,1)S(1)}) custom-call(f32[2]{0:T(128)S(1)} %pad_maximum_fusion.scal_ref, s32[1]{0:T(128)} %bitcast.place_ref, s32[16,128]{1,0:T(8,128)S(1)} %copy-done.4, ...), custom_call_target="tpu_custom_call" | custom-call | flops 15099494400 | tf_op jit(solution)/shard_map/late/pallas_call | solution.py:343
  71.7 1.9 %collective-permute-start.6 = (bf16[256,1152]{1,0:T(8,128)(2,1)}, bf16[256,1152]{1,0:T(8,128)(2,1)S(1)}, u32[]{:S(2)}, u32[]{:S(2)}) collective-permute-start(bf16[256,1152]{1,0:T(8,128)(2,1)} %get-tuple-element.38), channel_id=1, source_target_pairs={{0,128},{64,192},{128,256},{192,320},{256,384},{320,448},{384,512}... | collective-permute-start | bytes 1769480 | tf_op jit(solution)/shard_map/ppermute | solution.py:296
  73.7 4.6 %collective-permute-start.7 = (bf16[256,1152]{1,0:T(8,128)(2,1)}, bf16[256,1152]{1,0:T(8,128)(2,1)S(1)}, u32[]{:S(2)}, u32[]{:S(2)}) collective-permute-start(bf16[256,1152]{1,0:T(8,128)(2,1)} %get-tuple-element.39), channel_id=1, source_target_pairs={{0,896},{64,960},{128,0},{192,64},{256,128},{320,192},{384,256},{4... | collective-permute-start | bytes 1769480 | tf_op jit(solution)/shard_map/ppermute | solution.py:296
  78.3 19.6 %all_to_all.10 = f32[16,1,128]{2,1,0:T(1,128)S(1)} all-to-all(f32[16,1,128]{2,1,0:T(1,128)S(1)} %middle.1), channel_id=1, replica_groups=mesh['blk'=16,'group'=64] {'blk'}, dimensions={0} | all-to-all | bytes 16384 | tf_op jit(solution)/shard_map/all_to_all | solution.py:283
  97.9 2.6 %final.1 = (bf16[128,1152]{1,0:T(8,128)(2,1)}, bf16[128,1152]{1,0:T(8,128)(2,1)}, f32[3]{0:T(128)}) custom-call(f32[2]{0:T(128)S(1)} %pad_maximum_fusion.scal_ref, bf16[128,1152]{1,0:T(8,128)(2,1)S(1)} %copy-done.1, bf16[128,1152]{1,0:T(8,128)(2,1)S(1)} %copy-done.3, f32[128,1152]{1,0:T(8,128)S(1)} %get-tuple-element.26.image_total_ref, ...), custom_call_target="tpu_custom_call" | custom-call | flops 377487360 | tf_op jit(solution)/shard_map/final/pallas_call | solution.py:356
  (20 shorter events, 0.1 us)
Async XLA Ops:
  0.6 9.9 %copy-start = (bf16[128,1152]{1,0:T(8,128)(2,1)S(1)}, bf16[128,1152]{1,0:T(8,128)(2,1)}, u32[]{:S(2)}) copy-start(bf16[128,1152]{1,0:T(8,128)(2,1)} %image_ref.3) | copy-start | bytes 884740
  0.6 1.0 %copy-start.2 = (bf16[128,1152]{1,0:T(8,128)(2,1)S(1)}, bf16[128,1152]{1,0:T(8,128)(2,1)}, u32[]{:S(2)}) copy-start(bf16[128,1152]{1,0:T(8,128)(2,1)} %text_ref.3) | copy-start | bytes 884740
  1.8 8.8 %copy-start.7 = (f32[128]{0:T(128)S(1)}, f32[128]{0:T(128)}, u32[]{:S(2)}) copy-start(f32[128]{0:T(128)} %param.9) | copy-start | bytes 1540
  1.8 32.1 %collective-permute-start.2 = (bf16[128,1152]{1,0:T(8,128)(2,1)S(1)}, bf16[128,1152]{1,0:T(8,128)(2,1)}, u32[]{:S(2)}, u32[]{:S(2)}) collective-permute-start(bf16[128,1152]{1,0:T(8,128)(2,1)S(1)} %text.1.text_unit_ref), channel_id=1, source_target_pairs={{0,64},{64,0},{128,192},{192,128},{256,320},{320,256},{384,448},{4... | collective-permute-start | bytes 884744 | tf_op jit(solution)/shard_map/ppermute | solution.py:296
  11.5 30.7 %collective-permute-start.1 = (bf16[128,2432]{1,0:T(8,128)(2,1)S(1)}, bf16[128,2432]{1,0:T(8,128)(2,1)S(1)}, u32[]{:S(2)}, u32[]{:S(2)}) collective-permute-start(bf16[128,2432]{1,0:T(8,128)(2,1)S(1)} %get-tuple-element.22.own_ref.own_any), channel_id=1, source_target_pairs={{0,128},{64,192},{128,256},{192,320},{256,384},{320,448},{384,512}... | collective-permute-start | bytes 1867784 | tf_op jit(solution)/shard_map/ppermute | solution.py:296
  16.4 26.5 %collective-permute-start = (bf16[128,2432]{1,0:T(8,128)(2,1)S(1)}, bf16[128,2432]{1,0:T(8,128)(2,1)S(1)}, u32[]{:S(2)}, u32[]{:S(2)}) collective-permute-start(bf16[128,2432]{1,0:T(8,128)(2,1)S(1)} %get-tuple-element.22.own_ref.own_any), channel_id=1, source_target_pairs={{0,896},{64,960},{128,0},{192,64},{256,128},{320,192},{384,256},{4... | collective-permute-start | bytes 1867784 | tf_op jit(solution)/shard_map/ppermute | solution.py:296
  30.6 5.2 %copy-start.4 = (s32[16,128]{1,0:T(8,128)S(1)}, s32[16,128]{1,0:T(8,128)}, u32[]{:S(2)}) copy-start(s32[16,128]{1,0:T(8,128)} %label_any.1) | copy-start | bytes 24580
  30.6 20.2 %collective-permute-start.4 = (bf16[128,1280]{1,0:T(8,128)(2,1)}, bf16[128,1280]{1,0:T(8,128)(2,1)}, u32[]{:S(2)}, u32[]{:S(2)}) collective-permute-start(bf16[128,1280]{1,0:T(8,128)(2,1)} %get-tuple-element.30), channel_id=1, source_target_pairs={{0,64},{64,0},{128,192},{192,128},{256,320},{320,256},{384,448},{4... | collective-permute-start | bytes 983048 | tf_op jit(solution)/shard_map/ppermute | solution.py:296
  33.9 14.6 %collective-permute-start.3 = (bf16[128,1152]{1,0:T(8,128)(2,1)}, bf16[128,1152]{1,0:T(8,128)(2,1)S(1)}, u32[]{:S(2)}, u32[]{:S(2)}) collective-permute-start(bf16[128,1152]{1,0:T(8,128)(2,1)} %collective-permute-done.2.cross_ref.cross_v_any), channel_id=1, source_target_pairs={{0,128},{64,960},{128,256},{192,64},{256,384},{320,192},{384,512},... | collective-permute-start | bytes 884744 | tf_op jit(solution)/shard_map/ppermute | solution.py:296
  50.2 0.6 copy-start.5
  50.8 16.3 %collective-permute-start.5 = (bf16[128,1280]{1,0:T(8,128)(2,1)}, bf16[128,1280]{1,0:T(8,128)(2,1)}, u32[]{:S(2)}, u32[]{:S(2)}) collective-permute-start(bf16[128,1280]{1,0:T(8,128)(2,1)} %collective-permute-done.4.cross_any.cross_ref), channel_id=1, source_target_pairs={{0,128},{64,960},{128,256},{192,64},{256,384},{320,192},{384,512},... | collective-permute-start | bytes 983048 | tf_op jit(solution)/shard_map/ppermute | solution.py:296
  52.7 25.5 %all-to-all-start = ((f32[64,1,128]{2,1,0:T(1,128)}), f32[64,1,128]{2,1,0:T(1,128)S(1)}, u32[]{:S(2)}, u32[]{:S(2)}) async-start(f32[64,1,128]{2,1,0:T(1,128)} %get-tuple-element.40), calls=%async_computation | async-start | bytes 65536 | tf_op jit(solution)/shard_map/all_to_all | solution.py:283
  67.1 0.8 copy-start.6
  71.7 26.2 %collective-permute-start.6 = (bf16[256,1152]{1,0:T(8,128)(2,1)}, bf16[256,1152]{1,0:T(8,128)(2,1)S(1)}, u32[]{:S(2)}, u32[]{:S(2)}) collective-permute-start(bf16[256,1152]{1,0:T(8,128)(2,1)} %get-tuple-element.38), channel_id=1, source_target_pairs={{0,128},{64,192},{128,256},{192,320},{256,384},{320,448},{384,512}... | collective-permute-start | bytes 1769480 | tf_op jit(solution)/shard_map/ppermute | solution.py:296
  73.7 24.2 %collective-permute-start.7 = (bf16[256,1152]{1,0:T(8,128)(2,1)}, bf16[256,1152]{1,0:T(8,128)(2,1)S(1)}, u32[]{:S(2)}, u32[]{:S(2)}) collective-permute-start(bf16[256,1152]{1,0:T(8,128)(2,1)} %get-tuple-element.39), channel_id=1, source_target_pairs={{0,896},{64,960},{128,0},{192,64},{256,128},{320,192},{384,256},{4... | collective-permute-start | bytes 1769480 | tf_op jit(solution)/shard_map/ppermute | solution.py:296
  78.2 19.7 %copy-start.1 = (bf16[128,1152]{1,0:T(8,128)(2,1)S(1)}, bf16[128,1152]{1,0:T(8,128)(2,1)}, u32[]{:S(2)}) copy-start(bf16[128,1152]{1,0:T(8,128)(2,1)} %image_ref.3) | copy-start | bytes 884740
  78.3 19.7 %copy-start.3 = (bf16[128,1152]{1,0:T(8,128)(2,1)S(1)}, bf16[128,1152]{1,0:T(8,128)(2,1)}, u32[]{:S(2)}) copy-start(bf16[128,1152]{1,0:T(8,128)(2,1)} %text_ref.3) | copy-start | bytes 884740

commit v9 on v8

--- a/solution.py
+++ b/solution.py
@@ -131,7 +131,7 @@
 
 
 def early_kernel(
-    scal_ref, place_ref, label_ref, own_ref, after_ref, before_ref, cross_ref,
+    scal_ref, place_ref, label_ref, own_ref, before_ref, after_ref, cross_ref,
     image_in_ref, text_in_ref, sums_in_ref,
     image_total_ref, text_total_ref, cross_g_ref, four_g_ref, sums_ref,
 ):
@@ -326,7 +326,7 @@
     )(scal, place, labels, both, cross_v)
     image_total, text_total, far_cross_g, four_g, sums = call(
         early_kernel, head + [VMEM] * 7, (block, block, square, square, shape(8, 128, F32)), "early", 20 * dot
-    )(scal, place, labels, both, after, before, cross_v, image_total, text_total, sums)
+    )(scal, place, labels, both, before, after, cross_v, image_total, text_total, sums)
     near_g, far_g, sums = call(
         relay_kernel,
         head + [VMEM] * 5,

time: 102 us -> 99 us (0.971)
  blocking collectives: 19.6 us -> 16.5 us
    all_to_all x1, blocking collectives: 19.6 us -> 16.5 us  [exchanged(): return lax.all_to_all(sent, axis, 0, 0).reshape(sent.shape[0], 128)]
  transfers between devices with their start and end apart: 9 -> 9, of which waited for: 4 -> 3; matrix products, arithmetic and copies ran while one was open for 0% -> 0% of each run, Pallas kernels for 10% -> 11%
where the time goes in v9:
time: 99 us; the launch traced here: 97.3 us
  starting transfers between devices  50.3 us (51%)
  blocking collectives  16.5 us (17%)
  Pallas kernels  13.1 us (13%)
  waiting for transfers between devices  12.7 us (13%)
  local copies, waits for them, and re-layouts  2.4 us (2%)
  between operations  2.14 us (2%)
    ppermute x8, starting transfers between devices, passed(): lax.ppermute(value, 'blk', [(p, (p + step_of(p)) % cycle) for p in range(...  40.3 us
    all_to_all x1, blocking collectives, exchanged(): return lax.all_to_all(sent, axis, 0, 0).reshape(sent.shape[0], 128)  16.5 us
    ppermute x8, waiting for transfers between devices, passed(): lax.ppermute(value, 'blk', [(p, (p + step_of(p)) % cycle) for p in range(...  12.7 us
    all_to_all x1, starting transfers between devices, exchanged(): return lax.all_to_all(sent, axis, 0, 0).reshape(sent.shape[0], 128)  9.97 us
    pallas_call x1, Pallas kernels, per_device(): call(late_kernel, [SMEM, SMEM] + [HBM] * 11, (shape(2 * rows, width, BF16...  3.84 us
    pallas_call x1, Pallas kernels, per_device(): call(functools.partial(final_kernel, count), [SMEM] + [VMEM] * 13, (shape...  2.61 us
    unnamed x16, local copies, waits for them, and re-layouts  2.4 us
    pallas_call x1, Pallas kernels, per_device(): call(early_kernel, head + [VMEM] * 7, (block, block, square, square, shap...  2.16 us
  transfers between devices with their start and end apart: 9, of which 3 were waited for; matrix products, arithmetic and copies ran while one was open for 0% of the time, Pallas kernels for 11%

profile of v9, /device:TPU:1, one launch (start us, length us, event | category | flops | bytes accessed | tf_op | source)
XLA Modules:
  0.0 97.3 jit_solution(16546285356288611661)
XLA Ops:
  0.7 1.0 %copy-done.2 = bf16[128,1152]{1,0:T(8,128)(2,1)S(1)} copy-done((bf16[128,1152]{1,0:T(8,128)(2,1)S(1)}, bf16[128,1152]{1,0:T(8,128)(2,1)}, u32[]{:S(2)}) %copy-start.2) | copy-done | bytes 294936
  1.6 0.1 text.1.text_unit_ref
  1.8 8.7 %collective-permute-start.2 = (bf16[128,1152]{1,0:T(8,128)(2,1)S(1)}, bf16[128,1152]{1,0:T(8,128)(2,1)}, u32[]{:S(2)}, u32[]{:S(2)}) collective-permute-start(bf16[128,1152]{1,0:T(8,128)(2,1)S(1)} %text.1.text_unit_ref), channel_id=1, source_target_pairs={{0,64},{64,0},{128,192},{192,128},{256,320},{320,256},{384,448},{4... | collective-permute-start | bytes 884744 | tf_op jit(solution)/shard_map/ppermute | solution.py:296
  10.6 0.9 image.1
  11.5 17.2 %collective-permute-start.1 = (bf16[128,2432]{1,0:T(8,128)(2,1)S(1)}, bf16[128,2432]{1,0:T(8,128)(2,1)S(1)}, u32[]{:S(2)}, u32[]{:S(2)}) collective-permute-start(bf16[128,2432]{1,0:T(8,128)(2,1)S(1)} %get-tuple-element.22.own_ref.own_any), channel_id=1, source_target_pairs={{0,896},{64,960},{128,0},{192,64},{256,128},{320,192},{384,256},{4... | collective-permute-start | bytes 1867784 | tf_op jit(solution)/shard_map/ppermute | solution.py:296
  28.7 1.9 %collective-permute-start = (bf16[128,2432]{1,0:T(8,128)(2,1)S(1)}, bf16[128,2432]{1,0:T(8,128)(2,1)S(1)}, u32[]{:S(2)}, u32[]{:S(2)}) collective-permute-start(bf16[128,2432]{1,0:T(8,128)(2,1)S(1)} %get-tuple-element.22.own_ref.own_any), channel_id=1, source_target_pairs={{0,128},{64,192},{128,256},{192,320},{256,384},{320,448},{384,512}... | collective-permute-start | bytes 1867784 | tf_op jit(solution)/shard_map/ppermute | solution.py:296
  30.6 1.9 %collective-permute-start.4 = (bf16[128,1280]{1,0:T(8,128)(2,1)}, bf16[128,1280]{1,0:T(8,128)(2,1)}, u32[]{:S(2)}, u32[]{:S(2)}) collective-permute-start(bf16[128,1280]{1,0:T(8,128)(2,1)} %get-tuple-element.30), channel_id=1, source_target_pairs={{0,64},{64,0},{128,192},{192,128},{256,320},{320,256},{384,448},{4... | collective-permute-start | bytes 983048 | tf_op jit(solution)/shard_map/ppermute | solution.py:296
  33.8 0.1 pad_maximum_fusion.scal_ref
  33.9 1.9 %collective-permute-start.3 = (bf16[128,1152]{1,0:T(8,128)(2,1)}, bf16[128,1152]{1,0:T(8,128)(2,1)S(1)}, u32[]{:S(2)}, u32[]{:S(2)}) collective-permute-start(bf16[128,1152]{1,0:T(8,128)(2,1)} %collective-permute-done.2.cross_ref.cross_v_any), channel_id=1, source_target_pairs={{0,128},{64,960},{128,256},{192,64},{256,384},{320,192},{384,512},... | collective-permute-start | bytes 884744 | tf_op jit(solution)/shard_map/ppermute | solution.py:296
  35.8 1.8 %own.1 = (f32[128,1152]{1,0:T(8,128)S(1)}, f32[128,1152]{1,0:T(8,128)S(1)}, f32[8,128]{1,0:T(8,128)S(1)}) custom-call(f32[2]{0:T(128)S(1)} %pad_maximum_fusion.scal_ref, s32[1]{0:T(128)} %bitcast.place_ref, s32[16,128]{1,0:T(8,128)S(1)} %copy-done.4, bf16[128,2432]{1,0:T(8,128)(2,1)S(1)} %get-tuple-element.22.own_ref.own_any, ...), custom_call_target="tpu_custom_call" | custom-call | flops 5662310400 | tf_op jit(solution)/shard_map/own/pallas_call | solution.py:324
  37.6 3.4 %collective-permute-done.1.after_ref.after_any = bf16[128,2432]{1,0:T(8,128)(2,1)S(1)} collective-permute-done((bf16[128,2432]{1,0:T(8,128)(2,1)S(1)}, bf16[128,2432]{1,0:T(8,128)(2,1)S(1)}, u32[]{:S(2)}, u32[]{:S(2)}) %collective-permute-start.1) | collective-permute-done | bytes 622624 | tf_op jit(solution)/shard_map/ppermute | solution.py:296
  41.0 5.1 %collective-permute-done.before_ref.before_any = bf16[128,2432]{1,0:T(8,128)(2,1)S(1)} collective-permute-done((bf16[128,2432]{1,0:T(8,128)(2,1)S(1)}, bf16[128,2432]{1,0:T(8,128)(2,1)S(1)}, u32[]{:S(2)}, u32[]{:S(2)}) %collective-permute-start) | collective-permute-done | bytes 622624 | tf_op jit(solution)/shard_map/ppermute | solution.py:296
  46.1 2.2 %early.1 = (f32[128,1152]{1,0:T(8,128)S(1)}, f32[128,1152]{1,0:T(8,128)S(1)}, bf16[128,128]{1,0:T(8,128)(2,1)S(1)}, bf16[128,128]{1,0:T(8,128)(2,1)S(1)}, f32[8,128]{1,0:T(8,128)S(1)}) custom-call(f32[2]{0:T(128)S(1)} %pad_maximum_fusion.scal_ref, s32[1]{0:T(128)} %bitcast.place_ref, s32[16,128]{1,0:T(8,128)S(1)} %copy-done.4, ...), custom_call_target="tpu_custom_call" | custom-call | flops 754974720 | tf_op jit(solution)/shard_map/early/pallas_call | solution.py:327
  48.3 4.2 %collective-permute-done.3.relay_ref.relay_v_any.relay_v_ref = bf16[128,1152]{1,0:T(8,128)(2,1)S(1)} collective-permute-done((bf16[128,1152]{1,0:T(8,128)(2,1)}, bf16[128,1152]{1,0:T(8,128)(2,1)S(1)}, u32[]{:S(2)}, u32[]{:S(2)}) %collective-permute-start.3) | collective-permute-done | bytes 294944 | tf_op jit(solution)/shard_map/ppermute | solution.py:296
  52.5 1.7 %relay.1 = (bf16[128,128]{1,0:T(8,128)(2,1)S(1)}, bf16[128,128]{1,0:T(8,128)(2,1)S(1)}, f32[64,1,128]{2,1,0:T(1,128)}) custom-call(f32[2]{0:T(128)S(1)} %pad_maximum_fusion.scal_ref, s32[1]{0:T(128)} %bitcast.place_ref, s32[16,128]{1,0:T(8,128)S(1)} %copy-done.4, bf16[128,2432]{1,0:T(8,128)(2,1)S(1)} %get-tuple-element.22.own_ref.own_any, ...), custom_call_target="tpu_custom_call" | custom-call | flops 377487360 | tf_op jit(solution)/shard_map/relay/pallas_call | solution.py:330
  54.1 0.6 copy-done.5
  54.8 1.9 %collective-permute-start.5 = (bf16[128,1280]{1,0:T(8,128)(2,1)}, bf16[128,1280]{1,0:T(8,128)(2,1)}, u32[]{:S(2)}, u32[]{:S(2)}) collective-permute-start(bf16[128,1280]{1,0:T(8,128)(2,1)} %collective-permute-done.4.cross_any.cross_ref), channel_id=1, source_target_pairs={{0,128},{64,960},{128,256},{192,64},{256,384},{320,192},{384,512},... | collective-permute-start | bytes 983048 | tf_op jit(solution)/shard_map/ppermute | solution.py:296
  56.7 10.0 %all-to-all-start = ((f32[64,1,128]{2,1,0:T(1,128)}), f32[64,1,128]{2,1,0:T(1,128)S(1)}, u32[]{:S(2)}, u32[]{:S(2)}) async-start(f32[64,1,128]{2,1,0:T(1,128)} %get-tuple-element.40), calls=%async_computation | async-start | bytes 65536 | tf_op jit(solution)/shard_map/all_to_all | solution.py:283
  66.7 0.7 copy-done.6
  67.4 3.8 %late.1 = (bf16[256,1152]{1,0:T(8,128)(2,1)}, bf16[256,1152]{1,0:T(8,128)(2,1)}, bf16[128,128]{1,0:T(8,128)(2,1)S(1)}, bf16[128,128]{1,0:T(8,128)(2,1)S(1)}) custom-call(f32[2]{0:T(128)S(1)} %pad_maximum_fusion.scal_ref, s32[1]{0:T(128)} %bitcast.place_ref, s32[16,128]{1,0:T(8,128)S(1)} %copy-done.4, ...), custom_call_target="tpu_custom_call" | custom-call | flops 15099494400 | tf_op jit(solution)/shard_map/late/pallas_call | solution.py:343
  71.3 1.9 %collective-permute-start.6 = (bf16[256,1152]{1,0:T(8,128)(2,1)}, bf16[256,1152]{1,0:T(8,128)(2,1)S(1)}, u32[]{:S(2)}, u32[]{:S(2)}) collective-permute-start(bf16[256,1152]{1,0:T(8,128)(2,1)} %get-tuple-element.38), channel_id=1, source_target_pairs={{0,128},{64,192},{128,256},{192,320},{256,384},{320,448},{384,512}... | collective-permute-start | bytes 1769480 | tf_op jit(solution)/shard_map/ppermute | solution.py:296
  73.2 4.9 %collective-permute-start.7 = (bf16[256,1152]{1,0:T(8,128)(2,1)}, bf16[256,1152]{1,0:T(8,128)(2,1)S(1)}, u32[]{:S(2)}, u32[]{:S(2)}) collective-permute-start(bf16[256,1152]{1,0:T(8,128)(2,1)} %get-tuple-element.39), channel_id=1, source_target_pairs={{0,896},{64,960},{128,0},{192,64},{256,128},{320,192},{384,256},{4... | collective-permute-start | bytes 1769480 | tf_op jit(solution)/shard_map/ppermute | solution.py:296
  78.1 16.5 %all_to_all.10 = f32[16,1,128]{2,1,0:T(1,128)S(1)} all-to-all(f32[16,1,128]{2,1,0:T(1,128)S(1)} %middle.1), channel_id=1, replica_groups=mesh['blk'=16,'group'=64] {'blk'}, dimensions={0} | all-to-all | bytes 16384 | tf_op jit(solution)/shard_map/all_to_all | solution.py:283
  94.7 2.6 %final.1 = (bf16[128,1152]{1,0:T(8,128)(2,1)}, bf16[128,1152]{1,0:T(8,128)(2,1)}, f32[3]{0:T(128)}) custom-call(f32[2]{0:T(128)S(1)} %pad_maximum_fusion.scal_ref, bf16[128,1152]{1,0:T(8,128)(2,1)S(1)} %copy-done.1, bf16[128,1152]{1,0:T(8,128)(2,1)S(1)} %copy-done.3, f32[128,1152]{1,0:T(8,128)S(1)} %get-tuple-element.26.image_total_ref, ...), custom_call_target="tpu_custom_call" | custom-call | flops 377487360 | tf_op jit(solution)/shard_map/final/pallas_call | solution.py:356
  (20 shorter events, 0.1 us)
Async XLA Ops:
  0.6 9.9 %copy-start = (bf16[128,1152]{1,0:T(8,128)(2,1)S(1)}, bf16[128,1152]{1,0:T(8,128)(2,1)}, u32[]{:S(2)}) copy-start(bf16[128,1152]{1,0:T(8,128)(2,1)} %image_ref.3) | copy-start | bytes 884740
  0.6 1.0 %copy-start.2 = (bf16[128,1152]{1,0:T(8,128)(2,1)S(1)}, bf16[128,1152]{1,0:T(8,128)(2,1)}, u32[]{:S(2)}) copy-start(bf16[128,1152]{1,0:T(8,128)(2,1)} %text_ref.3) | copy-start | bytes 884740
  1.8 8.8 %copy-start.7 = (f32[128]{0:T(128)S(1)}, f32[128]{0:T(128)}, u32[]{:S(2)}) copy-start(f32[128]{0:T(128)} %param.9) | copy-start | bytes 1540
  1.8 32.1 %collective-permute-start.2 = (bf16[128,1152]{1,0:T(8,128)(2,1)S(1)}, bf16[128,1152]{1,0:T(8,128)(2,1)}, u32[]{:S(2)}, u32[]{:S(2)}) collective-permute-start(bf16[128,1152]{1,0:T(8,128)(2,1)S(1)} %text.1.text_unit_ref), channel_id=1, source_target_pairs={{0,64},{64,0},{128,192},{192,128},{256,320},{320,256},{384,448},{4... | collective-permute-start | bytes 884744 | tf_op jit(solution)/shard_map/ppermute | solution.py:296
  11.5 29.5 %collective-permute-start.1 = (bf16[128,2432]{1,0:T(8,128)(2,1)S(1)}, bf16[128,2432]{1,0:T(8,128)(2,1)S(1)}, u32[]{:S(2)}, u32[]{:S(2)}) collective-permute-start(bf16[128,2432]{1,0:T(8,128)(2,1)S(1)} %get-tuple-element.22.own_ref.own_any), channel_id=1, source_target_pairs={{0,896},{64,960},{128,0},{192,64},{256,128},{320,192},{384,256},{4... | collective-permute-start | bytes 1867784 | tf_op jit(solution)/shard_map/ppermute | solution.py:296
  28.7 17.5 %collective-permute-start = (bf16[128,2432]{1,0:T(8,128)(2,1)S(1)}, bf16[128,2432]{1,0:T(8,128)(2,1)S(1)}, u32[]{:S(2)}, u32[]{:S(2)}) collective-permute-start(bf16[128,2432]{1,0:T(8,128)(2,1)S(1)} %get-tuple-element.22.own_ref.own_any), channel_id=1, source_target_pairs={{0,128},{64,192},{128,256},{192,320},{256,384},{320,448},{384,512}... | collective-permute-start | bytes 1867784 | tf_op jit(solution)/shard_map/ppermute | solution.py:296
  30.6 5.2 %copy-start.4 = (s32[16,128]{1,0:T(8,128)S(1)}, s32[16,128]{1,0:T(8,128)}, u32[]{:S(2)}) copy-start(s32[16,128]{1,0:T(8,128)} %label_any.1) | copy-start | bytes 24580
  30.6 24.2 %collective-permute-start.4 = (bf16[128,1280]{1,0:T(8,128)(2,1)}, bf16[128,1280]{1,0:T(8,128)(2,1)}, u32[]{:S(2)}, u32[]{:S(2)}) collective-permute-start(bf16[128,1280]{1,0:T(8,128)(2,1)} %get-tuple-element.30), channel_id=1, source_target_pairs={{0,64},{64,0},{128,192},{192,128},{256,320},{320,256},{384,448},{4... | collective-permute-start | bytes 983048 | tf_op jit(solution)/shard_map/ppermute | solution.py:296
  33.9 18.6 %collective-permute-start.3 = (bf16[128,1152]{1,0:T(8,128)(2,1)}, bf16[128,1152]{1,0:T(8,128)(2,1)S(1)}, u32[]{:S(2)}, u32[]{:S(2)}) collective-permute-start(bf16[128,1152]{1,0:T(8,128)(2,1)} %collective-permute-done.2.cross_ref.cross_v_any), channel_id=1, source_target_pairs={{0,128},{64,960},{128,256},{192,64},{256,384},{320,192},{384,512},... | collective-permute-start | bytes 884744 | tf_op jit(solution)/shard_map/ppermute | solution.py:296
  54.1 0.6 copy-start.5
  54.8 11.9 %collective-permute-start.5 = (bf16[128,1280]{1,0:T(8,128)(2,1)}, bf16[128,1280]{1,0:T(8,128)(2,1)}, u32[]{:S(2)}, u32[]{:S(2)}) collective-permute-start(bf16[128,1280]{1,0:T(8,128)(2,1)} %collective-permute-done.4.cross_any.cross_ref), channel_id=1, source_target_pairs={{0,128},{64,960},{128,256},{192,64},{256,384},{320,192},{384,512},... | collective-permute-start | bytes 983048 | tf_op jit(solution)/shard_map/ppermute | solution.py:296
  56.7 21.4 %all-to-all-start = ((f32[64,1,128]{2,1,0:T(1,128)}), f32[64,1,128]{2,1,0:T(1,128)S(1)}, u32[]{:S(2)}, u32[]{:S(2)}) async-start(f32[64,1,128]{2,1,0:T(1,128)} %get-tuple-element.40), calls=%async_computation | async-start | bytes 65536 | tf_op jit(solution)/shard_map/all_to_all | solution.py:283
  66.7 0.8 copy-start.6
  71.3 23.4 %collective-permute-start.6 = (bf16[256,1152]{1,0:T(8,128)(2,1)}, bf16[256,1152]{1,0:T(8,128)(2,1)S(1)}, u32[]{:S(2)}, u32[]{:S(2)}) collective-permute-start(bf16[256,1152]{1,0:T(8,128)(2,1)} %get-tuple-element.38), channel_id=1, source_target_pairs={{0,128},{64,192},{128,256},{192,320},{256,384},{320,448},{384,512}... | collective-permute-start | bytes 1769480 | tf_op jit(solution)/shard_map/ppermute | solution.py:296
  73.2 21.5 %collective-permute-start.7 = (bf16[256,1152]{1,0:T(8,128)(2,1)}, bf16[256,1152]{1,0:T(8,128)(2,1)S(1)}, u32[]{:S(2)}, u32[]{:S(2)}) collective-permute-start(bf16[256,1152]{1,0:T(8,128)(2,1)} %get-tuple-element.39), channel_id=1, source_target_pairs={{0,896},{64,960},{128,0},{192,64},{256,128},{320,192},{384,256},{4... | collective-permute-start | bytes 1769480 | tf_op jit(solution)/shard_map/ppermute | solution.py:296
  78.1 16.6 %copy-start.1 = (bf16[128,1152]{1,0:T(8,128)(2,1)S(1)}, bf16[128,1152]{1,0:T(8,128)(2,1)}, u32[]{:S(2)}) copy-start(bf16[128,1152]{1,0:T(8,128)(2,1)} %image_ref.3) | copy-start | bytes 884740
  78.1 16.6 %copy-start.3 = (bf16[128,1152]{1,0:T(8,128)(2,1)S(1)}, bf16[128,1152]{1,0:T(8,128)(2,1)}, u32[]{:S(2)}) copy-start(bf16[128,1152]{1,0:T(8,128)(2,1)} %text_ref.3) | copy-start | bytes 884740

commit v10 on v9

--- a/solution.py
+++ b/solution.py
@@ -198,9 +198,9 @@
         for at, (source, target) in enumerate((
             (label_any, label_ref),
             (cross_any, cross_ref),
+            (own_any.at[text_part], v_ref),
             (before_any, before_ref),
             (after_any.at[text_part], va_ref),
-            (own_any.at[text_part], v_ref),
             (relay_any, relay_ref),
             (far_g_any, far_g_ref),
             (relay_v_any, relay_v_ref),
@@ -211,24 +211,27 @@
     ]
     for copy in copies:
         copy.start()
-    for copy in copies[:5]:
+    for copy in copies[:3]:
         copy.wait()
     scorer = Scorer(scal_ref, label_ref, place_ref)
     side = scorer.side()
     even = side == 1
-    v, va, vb = v_ref[...], va_ref[...], before_ref[:, width + 128 :]
+    v = v_ref[...]
     uc = cross_ref[:, :width]
     wc = weight_of(cross_ref, width)
     col_c = as_column(scorer.label_row(side).astype(F32))
     col_r = as_column(scorer.label_row(-side).astype(F32))
     row, row_a, row_b = scorer.label_row(0), scorer.label_row(2), scorer.label_row(-2)
+    cross_g_ref[...] = scorer.grads(uc, v, wc, col_c, row, False)
+    for copy in copies[3:5]:
+        copy.wait()
+    va, vb = va_ref[...], before_ref[:, width + 128 :]
     gcx = scorer.grads(uc, jnp.where(even, vb, va), wc, col_c, jnp.where(even, row_b, row_a), False)
-    gc = scorer.grads(uc, v, wc, col_c, row, False)
     for copy in copies[5:]:
         copy.wait()
     ur, wr = relay_ref[:, :width], weight_of(relay_ref, width)
     grx = scorer.grads(ur, jnp.where(even, va, vb), wr, col_r, jnp.where(even, row_a, row_b), False)
-    gr = scorer.grads(ur, v, wr, col_r, row, False)
+    relay_g_ref[...] = scorer.grads(ur, v, wr, col_r, row, False)
     far_text_c, far_text_r = t_matmul(gcx, uc), t_matmul(grx, ur)
     far_image_r = matmul(far_g_ref[...], relay_v_ref[...])
     far_image_c = matmul(far_cross_ref[...], cross_v_ref[...])
@@ -237,7 +240,6 @@
     to_up_ref[rows:, :] = (t_matmul(g, before_ref[:, :width]) + jnp.where(even, far_text_r, far_text_c)).astype(BF16)
     to_down_ref[:rows, :] = (matmul(g, va) + jnp.where(even, far_image_c, far_image_r)).astype(BF16)
     to_down_ref[rows:, :] = jnp.where(even, far_text_c, far_text_r).astype(BF16)
-    cross_g_ref[...], relay_g_ref[...] = gc, gr
 
 
 def middle_kernel(got_ref, sums_ref):

time: 99 us -> 99.2 us (level)
  no operation moved by 1% of the time
where the time goes in v10:
time: 99.2 us; the launch traced here: 97.6 us
  starting transfers between devices  50.3 us (51%)
  blocking collectives  16.5 us (17%)
  Pallas kernels  13.4 us (14%)
  waiting for transfers between devices  12.7 us (13%)
  local copies, waits for them, and re-layouts  2.4 us (2%)
  between operations  2.14 us (2%)
    ppermute x8, starting transfers between devices, passed(): lax.ppermute(value, 'blk', [(p, (p + step_of(p)) % cycle) for p in range(...  40.3 us
    all_to_all x1, blocking collectives, exchanged(): return lax.all_to_all(sent, axis, 0, 0).reshape(sent.shape[0], 128)  16.5 us
    ppermute x8, waiting for transfers between devices, passed(): lax.ppermute(value, 'blk', [(p, (p + step_of(p)) % cycle) for p in range(...  12.7 us
    all_to_all x1, starting transfers between devices, exchanged(): return lax.all_to_all(sent, axis, 0, 0).reshape(sent.shape[0], 128)  9.97 us
    pallas_call x1, Pallas kernels, per_device(): call(late_kernel, [SMEM, SMEM] + [HBM] * 11, (shape(2 * rows, width, BF16...  4.09 us
    pallas_call x1, Pallas kernels, per_device(): call(functools.partial(final_kernel, count), [SMEM] + [VMEM] * 13, (shape...  2.63 us
    unnamed x16, local copies, waits for them, and re-layouts  2.4 us
    pallas_call x1, Pallas kernels, per_device(): call(early_kernel, head + [VMEM] * 7, (block, block, square, square, shap...  2.16 us
  transfers between devices with their start and end apart: 9, of which 3 were waited for; matrix products, arithmetic and copies ran while one was open for 0% of the time, Pallas kernels for 11%

profile of v10, /device:TPU:1, one launch (start us, length us, event | category | flops | bytes accessed | tf_op | source)
XLA Modules:
  0.0 97.6 jit_solution(2470486898914563077)
XLA Ops:
  0.7 1.0 %copy-done.2 = bf16[128,1152]{1,0:T(8,128)(2,1)S(1)} copy-done((bf16[128,1152]{1,0:T(8,128)(2,1)S(1)}, bf16[128,1152]{1,0:T(8,128)(2,1)}, u32[]{:S(2)}) %copy-start.2) | copy-done | bytes 294936
  1.6 0.1 text.1.text_unit_ref
  1.8 8.7 %collective-permute-start.2 = (bf16[128,1152]{1,0:T(8,128)(2,1)S(1)}, bf16[128,1152]{1,0:T(8,128)(2,1)}, u32[]{:S(2)}, u32[]{:S(2)}) collective-permute-start(bf16[128,1152]{1,0:T(8,128)(2,1)S(1)} %text.1.text_unit_ref), channel_id=1, source_target_pairs={{0,64},{64,0},{128,192},{192,128},{256,320},{320,256},{384,448},{4... | collective-permute-start | bytes 884744 | tf_op jit(solution)/shard_map/ppermute | solution.py:298
  10.6 0.9 image.1
  11.5 17.2 %collective-permute-start.1 = (bf16[128,2432]{1,0:T(8,128)(2,1)S(1)}, bf16[128,2432]{1,0:T(8,128)(2,1)S(1)}, u32[]{:S(2)}, u32[]{:S(2)}) collective-permute-start(bf16[128,2432]{1,0:T(8,128)(2,1)S(1)} %get-tuple-element.22.own_ref.own_any), channel_id=1, source_target_pairs={{0,896},{64,960},{128,0},{192,64},{256,128},{320,192},{384,256},{4... | collective-permute-start | bytes 1867784 | tf_op jit(solution)/shard_map/ppermute | solution.py:298
  28.7 1.9 %collective-permute-start = (bf16[128,2432]{1,0:T(8,128)(2,1)S(1)}, bf16[128,2432]{1,0:T(8,128)(2,1)S(1)}, u32[]{:S(2)}, u32[]{:S(2)}) collective-permute-start(bf16[128,2432]{1,0:T(8,128)(2,1)S(1)} %get-tuple-element.22.own_ref.own_any), channel_id=1, source_target_pairs={{0,128},{64,192},{128,256},{192,320},{256,384},{320,448},{384,512}... | collective-permute-start | bytes 1867784 | tf_op jit(solution)/shard_map/ppermute | solution.py:298
  30.6 1.9 %collective-permute-start.4 = (bf16[128,1280]{1,0:T(8,128)(2,1)}, bf16[128,1280]{1,0:T(8,128)(2,1)}, u32[]{:S(2)}, u32[]{:S(2)}) collective-permute-start(bf16[128,1280]{1,0:T(8,128)(2,1)} %get-tuple-element.30), channel_id=1, source_target_pairs={{0,64},{64,0},{128,192},{192,128},{256,320},{320,256},{384,448},{4... | collective-permute-start | bytes 983048 | tf_op jit(solution)/shard_map/ppermute | solution.py:298
  33.8 0.1 pad_maximum_fusion.scal_ref
  33.9 1.9 %collective-permute-start.3 = (bf16[128,1152]{1,0:T(8,128)(2,1)}, bf16[128,1152]{1,0:T(8,128)(2,1)S(1)}, u32[]{:S(2)}, u32[]{:S(2)}) collective-permute-start(bf16[128,1152]{1,0:T(8,128)(2,1)} %collective-permute-done.2.cross_ref.cross_v_any), channel_id=1, source_target_pairs={{0,128},{64,960},{128,256},{192,64},{256,384},{320,192},{384,512},... | collective-permute-start | bytes 884744 | tf_op jit(solution)/shard_map/ppermute | solution.py:298
  35.8 1.8 %own.1 = (f32[128,1152]{1,0:T(8,128)S(1)}, f32[128,1152]{1,0:T(8,128)S(1)}, f32[8,128]{1,0:T(8,128)S(1)}) custom-call(f32[2]{0:T(128)S(1)} %pad_maximum_fusion.scal_ref, s32[1]{0:T(128)} %bitcast.place_ref, s32[16,128]{1,0:T(8,128)S(1)} %copy-done.4, bf16[128,2432]{1,0:T(8,128)(2,1)S(1)} %get-tuple-element.22.own_ref.own_any, ...), custom_call_target="tpu_custom_call" | custom-call | flops 5662310400 | tf_op jit(solution)/shard_map/own/pallas_call | solution.py:326
  37.6 3.4 %collective-permute-done.1.after_ref.after_any = bf16[128,2432]{1,0:T(8,128)(2,1)S(1)} collective-permute-done((bf16[128,2432]{1,0:T(8,128)(2,1)S(1)}, bf16[128,2432]{1,0:T(8,128)(2,1)S(1)}, u32[]{:S(2)}, u32[]{:S(2)}) %collective-permute-start.1) | collective-permute-done | bytes 622624 | tf_op jit(solution)/shard_map/ppermute | solution.py:298
  41.0 5.1 %collective-permute-done.before_ref.before_any = bf16[128,2432]{1,0:T(8,128)(2,1)S(1)} collective-permute-done((bf16[128,2432]{1,0:T(8,128)(2,1)S(1)}, bf16[128,2432]{1,0:T(8,128)(2,1)S(1)}, u32[]{:S(2)}, u32[]{:S(2)}) %collective-permute-start) | collective-permute-done | bytes 622624 | tf_op jit(solution)/shard_map/ppermute | solution.py:298
  46.1 2.2 %early.1 = (f32[128,1152]{1,0:T(8,128)S(1)}, f32[128,1152]{1,0:T(8,128)S(1)}, bf16[128,128]{1,0:T(8,128)(2,1)S(1)}, bf16[128,128]{1,0:T(8,128)(2,1)S(1)}, f32[8,128]{1,0:T(8,128)S(1)}) custom-call(f32[2]{0:T(128)S(1)} %pad_maximum_fusion.scal_ref, s32[1]{0:T(128)} %bitcast.place_ref, s32[16,128]{1,0:T(8,128)S(1)} %copy-done.4, ...), custom_call_target="tpu_custom_call" | custom-call | flops 754974720 | tf_op jit(solution)/shard_map/early/pallas_call | solution.py:329
  48.3 4.2 %collective-permute-done.3.relay_ref.relay_v_any.relay_v_ref = bf16[128,1152]{1,0:T(8,128)(2,1)S(1)} collective-permute-done((bf16[128,1152]{1,0:T(8,128)(2,1)}, bf16[128,1152]{1,0:T(8,128)(2,1)S(1)}, u32[]{:S(2)}, u32[]{:S(2)}) %collective-permute-start.3) | collective-permute-done | bytes 294944 | tf_op jit(solution)/shard_map/ppermute | solution.py:298
  52.5 1.7 %relay.1 = (bf16[128,128]{1,0:T(8,128)(2,1)S(1)}, bf16[128,128]{1,0:T(8,128)(2,1)S(1)}, f32[64,1,128]{2,1,0:T(1,128)}) custom-call(f32[2]{0:T(128)S(1)} %pad_maximum_fusion.scal_ref, s32[1]{0:T(128)} %bitcast.place_ref, s32[16,128]{1,0:T(8,128)S(1)} %copy-done.4, bf16[128,2432]{1,0:T(8,128)(2,1)S(1)} %get-tuple-element.22.own_ref.own_any, ...), custom_call_target="tpu_custom_call" | custom-call | flops 377487360 | tf_op jit(solution)/shard_map/relay/pallas_call | solution.py:332
  54.1 0.6 copy-done.5
  54.8 1.9 %collective-permute-start.5 = (bf16[128,1280]{1,0:T(8,128)(2,1)}, bf16[128,1280]{1,0:T(8,128)(2,1)}, u32[]{:S(2)}, u32[]{:S(2)}) collective-permute-start(bf16[128,1280]{1,0:T(8,128)(2,1)} %collective-permute-done.4.cross_any.cross_ref), channel_id=1, source_target_pairs={{0,128},{64,960},{128,256},{192,64},{256,384},{320,192},{384,512},... | collective-permute-start | bytes 983048 | tf_op jit(solution)/shard_map/ppermute | solution.py:298
  56.7 10.0 %all-to-all-start = ((f32[64,1,128]{2,1,0:T(1,128)}), f32[64,1,128]{2,1,0:T(1,128)S(1)}, u32[]{:S(2)}, u32[]{:S(2)}) async-start(f32[64,1,128]{2,1,0:T(1,128)} %get-tuple-element.40), calls=%async_computation | async-start | bytes 65536 | tf_op jit(solution)/shard_map/all_to_all | solution.py:285
  66.7 0.7 copy-done.6
  67.4 4.1 %late.1 = (bf16[256,1152]{1,0:T(8,128)(2,1)}, bf16[256,1152]{1,0:T(8,128)(2,1)}, bf16[128,128]{1,0:T(8,128)(2,1)S(1)}, bf16[128,128]{1,0:T(8,128)(2,1)S(1)}) custom-call(f32[2]{0:T(128)S(1)} %pad_maximum_fusion.scal_ref, s32[1]{0:T(128)} %bitcast.place_ref, s32[16,128]{1,0:T(8,128)S(1)} %copy-done.4, ...), custom_call_target="tpu_custom_call" | custom-call | flops 15099494400 | tf_op jit(solution)/shard_map/late/pallas_call | solution.py:345
  71.5 1.9 %collective-permute-start.6 = (bf16[256,1152]{1,0:T(8,128)(2,1)}, bf16[256,1152]{1,0:T(8,128)(2,1)S(1)}, u32[]{:S(2)}, u32[]{:S(2)}) collective-permute-start(bf16[256,1152]{1,0:T(8,128)(2,1)} %get-tuple-element.38), channel_id=1, source_target_pairs={{0,128},{64,192},{128,256},{192,320},{256,384},{320,448},{384,512}... | collective-permute-start | bytes 1769480 | tf_op jit(solution)/shard_map/ppermute | solution.py:298
  73.5 4.9 %collective-permute-start.7 = (bf16[256,1152]{1,0:T(8,128)(2,1)}, bf16[256,1152]{1,0:T(8,128)(2,1)S(1)}, u32[]{:S(2)}, u32[]{:S(2)}) collective-permute-start(bf16[256,1152]{1,0:T(8,128)(2,1)} %get-tuple-element.39), channel_id=1, source_target_pairs={{0,896},{64,960},{128,0},{192,64},{256,128},{320,192},{384,256},{4... | collective-permute-start | bytes 1769480 | tf_op jit(solution)/shard_map/ppermute | solution.py:298
  78.4 16.5 %all_to_all.10 = f32[16,1,128]{2,1,0:T(1,128)S(1)} all-to-all(f32[16,1,128]{2,1,0:T(1,128)S(1)} %middle.1), channel_id=1, replica_groups=mesh['blk'=16,'group'=64] {'blk'}, dimensions={0} | all-to-all | bytes 16384 | tf_op jit(solution)/shard_map/all_to_all | solution.py:285
  94.9 2.6 %final.1 = (bf16[128,1152]{1,0:T(8,128)(2,1)}, bf16[128,1152]{1,0:T(8,128)(2,1)}, f32[3]{0:T(128)}) custom-call(f32[2]{0:T(128)S(1)} %pad_maximum_fusion.scal_ref, bf16[128,1152]{1,0:T(8,128)(2,1)S(1)} %copy-done.1, bf16[128,1152]{1,0:T(8,128)(2,1)S(1)} %copy-done.3, f32[128,1152]{1,0:T(8,128)S(1)} %get-tuple-element.26.image_total_ref, ...), custom_call_target="tpu_custom_call" | custom-call | flops 377487360 | tf_op jit(solution)/shard_map/final/pallas_call | solution.py:358
  (20 shorter events, 0.1 us)
Async XLA Ops:
  0.6 9.9 %copy-start = (bf16[128,1152]{1,0:T(8,128)(2,1)S(1)}, bf16[128,1152]{1,0:T(8,128)(2,1)}, u32[]{:S(2)}) copy-start(bf16[128,1152]{1,0:T(8,128)(2,1)} %image_ref.3) | copy-start | bytes 884740
  0.6 1.0 %copy-start.2 = (bf16[128,1152]{1,0:T(8,128)(2,1)S(1)}, bf16[128,1152]{1,0:T(8,128)(2,1)}, u32[]{:S(2)}) copy-start(bf16[128,1152]{1,0:T(8,128)(2,1)} %text_ref.3) | copy-start | bytes 884740
  1.8 8.8 %copy-start.7 = (f32[128]{0:T(128)S(1)}, f32[128]{0:T(128)}, u32[]{:S(2)}) copy-start(f32[128]{0:T(128)} %param.9) | copy-start | bytes 1540
  1.8 32.1 %collective-permute-start.2 = (bf16[128,1152]{1,0:T(8,128)(2,1)S(1)}, bf16[128,1152]{1,0:T(8,128)(2,1)}, u32[]{:S(2)}, u32[]{:S(2)}) collective-permute-start(bf16[128,1152]{1,0:T(8,128)(2,1)S(1)} %text.1.text_unit_ref), channel_id=1, source_target_pairs={{0,64},{64,0},{128,192},{192,128},{256,320},{320,256},{384,448},{4... | collective-permute-start | bytes 884744 | tf_op jit(solution)/shard_map/ppermute | solution.py:298
  11.5 29.5 %collective-permute-start.1 = (bf16[128,2432]{1,0:T(8,128)(2,1)S(1)}, bf16[128,2432]{1,0:T(8,128)(2,1)S(1)}, u32[]{:S(2)}, u32[]{:S(2)}) collective-permute-start(bf16[128,2432]{1,0:T(8,128)(2,1)S(1)} %get-tuple-element.22.own_ref.own_any), channel_id=1, source_target_pairs={{0,896},{64,960},{128,0},{192,64},{256,128},{320,192},{384,256},{4... | collective-permute-start | bytes 1867784 | tf_op jit(solution)/shard_map/ppermute | solution.py:298
  28.7 17.5 %collective-permute-start = (bf16[128,2432]{1,0:T(8,128)(2,1)S(1)}, bf16[128,2432]{1,0:T(8,128)(2,1)S(1)}, u32[]{:S(2)}, u32[]{:S(2)}) collective-permute-start(bf16[128,2432]{1,0:T(8,128)(2,1)S(1)} %get-tuple-element.22.own_ref.own_any), channel_id=1, source_target_pairs={{0,128},{64,192},{128,256},{192,320},{256,384},{320,448},{384,512}... | collective-permute-start | bytes 1867784 | tf_op jit(solution)/shard_map/ppermute | solution.py:298
  30.6 5.2 %copy-start.4 = (s32[16,128]{1,0:T(8,128)S(1)}, s32[16,128]{1,0:T(8,128)}, u32[]{:S(2)}) copy-start(s32[16,128]{1,0:T(8,128)} %label_any.1) | copy-start | bytes 24580
  30.6 24.2 %collective-permute-start.4 = (bf16[128,1280]{1,0:T(8,128)(2,1)}, bf16[128,1280]{1,0:T(8,128)(2,1)}, u32[]{:S(2)}, u32[]{:S(2)}) collective-permute-start(bf16[128,1280]{1,0:T(8,128)(2,1)} %get-tuple-element.30), channel_id=1, source_target_pairs={{0,64},{64,0},{128,192},{192,128},{256,320},{320,256},{384,448},{4... | collective-permute-start | bytes 983048 | tf_op jit(solution)/shard_map/ppermute | solution.py:298
  33.9 18.6 %collective-permute-start.3 = (bf16[128,1152]{1,0:T(8,128)(2,1)}, bf16[128,1152]{1,0:T(8,128)(2,1)S(1)}, u32[]{:S(2)}, u32[]{:S(2)}) collective-permute-start(bf16[128,1152]{1,0:T(8,128)(2,1)} %collective-permute-done.2.cross_ref.cross_v_any), channel_id=1, source_target_pairs={{0,128},{64,960},{128,256},{192,64},{256,384},{320,192},{384,512},... | collective-permute-start | bytes 884744 | tf_op jit(solution)/shard_map/ppermute | solution.py:298
  54.1 0.6 copy-start.5
  54.8 11.9 %collective-permute-start.5 = (bf16[128,1280]{1,0:T(8,128)(2,1)}, bf16[128,1280]{1,0:T(8,128)(2,1)}, u32[]{:S(2)}, u32[]{:S(2)}) collective-permute-start(bf16[128,1280]{1,0:T(8,128)(2,1)} %collective-permute-done.4.cross_any.cross_ref), channel_id=1, source_target_pairs={{0,128},{64,960},{128,256},{192,64},{256,384},{320,192},{384,512},... | collective-permute-start | bytes 983048 | tf_op jit(solution)/shard_map/ppermute | solution.py:298
  56.7 21.6 %all-to-all-start = ((f32[64,1,128]{2,1,0:T(1,128)}), f32[64,1,128]{2,1,0:T(1,128)S(1)}, u32[]{:S(2)}, u32[]{:S(2)}) async-start(f32[64,1,128]{2,1,0:T(1,128)} %get-tuple-element.40), calls=%async_computation | async-start | bytes 65536 | tf_op jit(solution)/shard_map/all_to_all | solution.py:285
  66.7 0.8 copy-start.6
  71.5 23.4 %collective-permute-start.6 = (bf16[256,1152]{1,0:T(8,128)(2,1)}, bf16[256,1152]{1,0:T(8,128)(2,1)S(1)}, u32[]{:S(2)}, u32[]{:S(2)}) collective-permute-start(bf16[256,1152]{1,0:T(8,128)(2,1)} %get-tuple-element.38), channel_id=1, source_target_pairs={{0,128},{64,192},{128,256},{192,320},{256,384},{320,448},{384,512}... | collective-permute-start | bytes 1769480 | tf_op jit(solution)/shard_map/ppermute | solution.py:298
  73.5 21.5 %collective-permute-start.7 = (bf16[256,1152]{1,0:T(8,128)(2,1)}, bf16[256,1152]{1,0:T(8,128)(2,1)S(1)}, u32[]{:S(2)}, u32[]{:S(2)}) collective-permute-start(bf16[256,1152]{1,0:T(8,128)(2,1)} %get-tuple-element.39), channel_id=1, source_target_pairs={{0,896},{64,960},{128,0},{192,64},{256,128},{320,192},{384,256},{4... | collective-permute-start | bytes 1769480 | tf_op jit(solution)/shard_map/ppermute | solution.py:298
  78.3 16.6 %copy-start.1 = (bf16[128,1152]{1,0:T(8,128)(2,1)S(1)}, bf16[128,1152]{1,0:T(8,128)(2,1)}, u32[]{:S(2)}) copy-start(bf16[128,1152]{1,0:T(8,128)(2,1)} %image_ref.3) | copy-start | bytes 884740
  78.3 16.6 %copy-start.3 = (bf16[128,1152]{1,0:T(8,128)(2,1)S(1)}, bf16[128,1152]{1,0:T(8,128)(2,1)}, u32[]{:S(2)}) copy-start(bf16[128,1152]{1,0:T(8,128)(2,1)} %text_ref.3) | copy-start | bytes 884740
